TPU v7x, 256 devices: a whole 4x4x8 slice. The times are simulated.
256 devices in a mesh: blk: 32 (over x, z), rep: 8 (over y, core).
Axes of the slice: x: 4, y: 4, z: 8, core: 2. Of those that a mesh axis runs over, the one named last changes fastest.
Arguments:
- features: bfloat16 [65536, 256], P(('blk', 'rep')), may hold values from -6 to 6
- degree: int32 [65536], P(('blk', 'rep')), may hold values from 1 to 8
- weight: bfloat16 [256, 256], replicated, may hold values from -0.375 to 0.375
- bias: float32 [256], replicated, may hold values from -3 to 3
- tile_rows: int32 [256, 192], P(('blk', 'rep')), may hold values from 0 to 15
- tile_cols: int32 [256, 192], P(('blk', 'rep')), may hold values from 0 to 63
- tile_count: int32 [256], P(('blk', 'rep')), may hold values from 48 to 192, as said below
- tile_values: bfloat16 [256, 192, 128, 128], P(('blk', 'rep')), may hold values from -0.15625 to 0.15625
- cotangent: bfloat16 [65536, 256], P(('blk', 'rep')), may hold values from -6 to 6
Outputs:
- layer_out: bfloat16 [65536, 256], P(('blk', 'rep'))
- grad_weight: float32 [256, 256], replicated
- grad_bias: float32 [256], replicated
- grad_features: bfloat16 [65536, 256], P(('blk', 'rep'))
Inputs may be any that keep to these rules, and one draw needn't show every extreme that they name: `tile_count`: at least one device has all 192 slots live; every device has at least 48.
All inputs are finite; a program needn't handle non-finite values.
Results may differ from a plain program's by a relative error of at most 0.0051.
Values may be sent and summed in bfloat16 or wider, within the bound.
No kernel may reach another device: no remote copies, remote signals or barrier semaphores. Data moves between devices by JAX's collectives and lax.ppermute only.
A program may use at most 128 MiB of HBM per device.

v0:
```python
import math

import jax
import jax.numpy as jnp
from jax import lax
from jax.sharding import PartitionSpec as P


def shards(
    features, degree, weight, bias, tile_rows, tile_cols, tile_count, tile_values, cotangent
):
    local_rows, hidden = features.shape
    tile_size = tile_values.shape[-1]
    capacity = tile_rows.shape[1]
    blk_count = lax.axis_size("blk")
    rep_count = lax.axis_size("rep")
    band_blocks = local_rows * rep_count // tile_size
    group_blocks = local_rows * blk_count // tile_size
    step_tiles = math.gcd(capacity, 32)
    tile_total = tile_count[0]
    row_list = tile_rows[0]
    col_list = tile_cols[0]
    tile_block = tile_values[0]

    def slot_slices(turn):
        first_tile = turn * step_tiles
        row_ids = lax.dynamic_slice_in_dim(row_list, first_tile, step_tiles)
        col_ids = lax.dynamic_slice_in_dim(col_list, first_tile, step_tiles)
        tile_vals = lax.dynamic_slice_in_dim(tile_block, first_tile, step_tiles, 0)
        active = first_tile + jnp.arange(step_tiles, dtype=jnp.int32) < tile_total
        return (row_ids, col_ids, tile_vals, active)

    inv_root = lax.rsqrt(degree.astype(jnp.float32))
    scaled = (features.astype(jnp.float32) * inv_root[:, None]).astype(jnp.bfloat16)
    gathered = lax.all_gather(scaled, "blk", axis=0, tiled=True).reshape(
        group_blocks, tile_size, hidden
    )

    def forward_step(turn, running):
        row_ids, col_ids, tile_vals, active = slot_slices(turn)
        picked = jnp.take(gathered, col_ids, axis=0)
        products = jnp.einsum("tij,tjh->tih", tile_vals, picked, preferred_element_type=jnp.float32)
        selector = (
            (row_ids[:, None] == jnp.arange(band_blocks, dtype=jnp.int32)[None, :])
            & active[:, None]
        ).astype(jnp.float32)
        return running + jnp.einsum(
            "tr,tih->rih", selector, products, precision=lax.Precision.HIGHEST
        )

    partial_value = lax.fori_loop(
        0,
        capacity // step_tiles,
        forward_step,
        jnp.zeros((band_blocks, tile_size, hidden), jnp.float32),
    )
    own_rows = lax.psum_scatter(
        partial_value.reshape(band_blocks * tile_size, hidden),
        "rep",
        scatter_dimension=0,
        tiled=True,
    )
    aggregated = (own_rows * inv_root[:, None]).astype(jnp.bfloat16)
    layer_out = (jnp.dot(aggregated, weight, preferred_element_type=jnp.float32) + bias).astype(
        jnp.bfloat16
    )
    grad_w = lax.dot_general(
        aggregated, cotangent, (((0,), (0,)), ((), ())), preferred_element_type=jnp.float32
    )
    grad_b = jnp.sum(cotangent.astype(jnp.float32), axis=0)
    grad_weight, grad_bias = lax.psum((grad_w, grad_b), ("blk", "rep"))
    back_proj = lax.dot_general(
        cotangent, weight, (((1,), (1,)), ((), ())), preferred_element_type=jnp.float32
    )
    grad_scaled = (back_proj * inv_root[:, None]).astype(jnp.bfloat16)
    band_rows = lax.all_gather(grad_scaled, "rep", axis=0, tiled=True).reshape(
        band_blocks, tile_size, hidden
    )

    def backward_step(turn, running):
        row_ids, col_ids, tile_vals, active = slot_slices(turn)
        picked = jnp.take(band_rows, row_ids, axis=0)
        products = jnp.einsum("tij,tih->tjh", tile_vals, picked, preferred_element_type=jnp.float32)
        selector = (
            (col_ids[:, None] == jnp.arange(group_blocks, dtype=jnp.int32)[None, :])
            & active[:, None]
        ).astype(jnp.float32)
        return running + jnp.einsum(
            "tc,tjh->cjh", selector, products, precision=lax.Precision.HIGHEST
        )

    col_terms = lax.fori_loop(
        0,
        capacity // step_tiles,
        backward_step,
        jnp.zeros((group_blocks, tile_size, hidden), jnp.float32),
    )
    mine = lax.psum_scatter(
        col_terms.reshape(group_blocks * tile_size, hidden), "blk", scatter_dimension=0, tiled=True
    )
    grad_features = (mine * inv_root[:, None]).astype(jnp.bfloat16)
    return (layer_out, grad_weight, grad_bias, grad_features)


def solution(mesh):
    return jax.shard_map(
        shards,
        mesh=mesh,
        in_specs=(
            P(("blk", "rep"), None),
            P(("blk", "rep")),
            P(),
            P(),
            P(("blk", "rep"), None),
            P(("blk", "rep"), None),
            P(("blk", "rep")),
            P(("blk", "rep"), None, None, None),
            P(("blk", "rep"), None),
        ),
        out_specs=(P(("blk", "rep"), None), P(), P(), P(("blk", "rep"), None)),
        check_vma=False,
    )
```

profile of v0, /device:TPU:1, one launch (start us, length us, event | category | flops | bytes accessed | tf_op | source)
XLA Modules:
  0.0 921.0 jit_solution(9210167972075605604)
XLA Ops:
  9.9 30.7 %all-gather.5.cloned.1.call-done = bf16[2048,256]{1,0:T(8,128)(2,1)} async-done(((bf16[256,256]{1,0:T(8,128)(2,1)}), bf16[2048,256]{1,0:T(8,128)(2,1)}) %all-gather.5.cloned.1.call-update) | async-done | bytes 1048592 | tf_op jit(solution)/shard_map/all_gather | solution.py:76
  40.6 128.5 %while.29 = (s32[]{:T(128)}, f32[64,128,256]{2,0,1:T(8,128)}, s32[192]{0:T(256)}, s32[]{:T(128)}, bf16[192,128,128]{2,1,0:T(8,128)(2,1)}, /*index=5*/s32[192]{0:...) while((s32[]{:T(128)}, f32[64,128,256]{2,0,1:T(8,128)}, ...), condition=%wide.region_7.8_spmd.clone, body=%wide.region_6.7_spmd.clone.sunk | while | flops 1078990080 | bytes 32514260 | solution.py:92
  44.0 4.0 fusion.58
  48.0 12.0 %select_add_fusion.5 = f32[64,128,256]{2,0,1:T(8,128)} fusion(f32[64,128,256]{2,0,1:T(8,128)} %get-tuple-element.448, pred[]{:T(512)S(6)} %compare.7, f32[32,128,256]{2,1,0:T(8,128)} %fusion.58, s32[32]{0:T(128)S(1)} %dynamic_slice.63, pred[32]{0:T(512)(128)(4,1)S(1)} %get-tuple-element.435), kind=kOutput, calls=%fused_computation.21.clone.1 | convolution fusion | flops 809504768 | bytes 20971680 | tf_op jit(solution)/shard_map/while/body/eval_jaxpr/tc,tjh->cjh/dot_general | solution.py:88
  63.3 4.0 fusion.58
  67.4 14.4 %select_add_fusion.5 = f32[64,128,256]{2,0,1:T(8,128)} fusion(f32[64,128,256]{2,0,1:T(8,128)} %get-tuple-element.448, pred[]{:T(512)S(6)} %compare.7, f32[32,128,256]{2,1,0:T(8,128)} %fusion.58, s32[32]{0:T(128)S(1)} %dynamic_slice.63, pred[32]{0:T(512)(128)(4,1)S(1)} %get-tuple-element.435), kind=kOutput, calls=%fused_computation.21.clone.1 | convolution fusion | flops 809504768 | bytes 20971680 | tf_op jit(solution)/shard_map/while/body/eval_jaxpr/tc,tjh->cjh/dot_general | solution.py:88
  89.2 14.4 %select_add_fusion.5 = f32[64,128,256]{2,0,1:T(8,128)} fusion(f32[64,128,256]{2,0,1:T(8,128)} %get-tuple-element.448, pred[]{:T(512)S(6)} %compare.7, f32[32,128,256]{2,1,0:T(8,128)} %fusion.58, s32[32]{0:T(128)S(1)} %dynamic_slice.63, pred[32]{0:T(512)(128)(4,1)S(1)} %get-tuple-element.435), kind=kOutput, calls=%fused_computation.21.clone.1 | convolution fusion | flops 809504768 | bytes 20971680 | tf_op jit(solution)/shard_map/while/body/eval_jaxpr/tc,tjh->cjh/dot_general | solution.py:88
  111.0 14.4 %select_add_fusion.5 = f32[64,128,256]{2,0,1:T(8,128)} fusion(f32[64,128,256]{2,0,1:T(8,128)} %get-tuple-element.448, pred[]{:T(512)S(6)} %compare.7, f32[32,128,256]{2,1,0:T(8,128)} %fusion.58, s32[32]{0:T(128)S(1)} %dynamic_slice.63, pred[32]{0:T(512)(128)(4,1)S(1)} %get-tuple-element.435), kind=kOutput, calls=%fused_computation.21.clone.1 | convolution fusion | flops 809504768 | bytes 20971680 | tf_op jit(solution)/shard_map/while/body/eval_jaxpr/tc,tjh->cjh/dot_general | solution.py:88
  128.8 4.0 fusion.58
  132.9 14.4 %select_add_fusion.5 = f32[64,128,256]{2,0,1:T(8,128)} fusion(f32[64,128,256]{2,0,1:T(8,128)} %get-tuple-element.448, pred[]{:T(512)S(6)} %compare.7, f32[32,128,256]{2,1,0:T(8,128)} %fusion.58, s32[32]{0:T(128)S(1)} %dynamic_slice.63, pred[32]{0:T(512)(128)(4,1)S(1)} %get-tuple-element.435), kind=kOutput, calls=%fused_computation.21.clone.1 | convolution fusion | flops 809504768 | bytes 20971680 | tf_op jit(solution)/shard_map/while/body/eval_jaxpr/tc,tjh->cjh/dot_general | solution.py:88
  154.7 14.4 %select_add_fusion.5 = f32[64,128,256]{2,0,1:T(8,128)} fusion(f32[64,128,256]{2,0,1:T(8,128)} %get-tuple-element.448, pred[]{:T(512)S(6)} %compare.7, f32[32,128,256]{2,1,0:T(8,128)} %fusion.58, s32[32]{0:T(128)S(1)} %dynamic_slice.63, pred[32]{0:T(512)(128)(4,1)S(1)} %get-tuple-element.435), kind=kOutput, calls=%fused_computation.21.clone.1 | convolution fusion | flops 809504768 | bytes 20971680 | tf_op jit(solution)/shard_map/while/body/eval_jaxpr/tc,tjh->cjh/dot_general | solution.py:88
  169.1 11.4 %copy.14 = f32[64,128,256]{2,1,0:T(8,128)} copy(f32[64,128,256]{2,0,1:T(8,128)} %get-tuple-element.253) | data formatting | bytes 16777216 | tf_op jit(solution)/shard_map/while | solution.py:92
  180.7 224.8 %reduce-scatter.5.cloned.1.call-done = f32[256,256]{1,0:T(8,128)} async-done(((f32[8192,256]{1,0:T(8,128)}), f32[256,256]{1,0:T(8,128)}) %reduce-scatter.5.cloned.1.call-update) | async-done | bytes 262160 | tf_op jit(solution)/shard_map/reduce_scatter | solution.py:98
  407.3 83.1 %all-gather.3.cloned.1.call-done = bf16[8192,256]{1,0:T(8,128)(2,1)} async-done(((bf16[256,256]{1,0:T(8,128)(2,1)}), bf16[8192,256]{1,0:T(8,128)(2,1)}) %all-gather.3.cloned.1.call-update) | async-done | bytes 4194320 | tf_op jit(solution)/shard_map/all_gather | solution.py:35
  490.4 93.3 %while.28 = (s32[]{:T(128)}, f32[16,128,256]{2,0,1:T(8,128)}, s32[192]{0:T(256)S(1)}, s32[]{:T(128)}, bf16[192,128,128]{2,1,0:T(8,128)(2,1)}, /*index=5*/s32[192...) while((s32[]{:T(128)}, f32[16,128,256]{2,0,1:T(8,128)}, ...), condition=%wide.region_1.0_spmd.clone, body=%wide.region_0.1_spmd.clone.sunk | while | flops 471861504 | bytes 19928248 | solution.py:51
  498.0 7.3 select_add_fusion.4
  513.0 8.0 select_add_fusion.4
  528.7 8.0 select_add_fusion.4
  544.3 8.0 select_add_fusion.4
  560.0 8.0 select_add_fusion.4
  575.7 8.0 select_add_fusion.4
  583.7 4.2 copy.13
  588.0 78.1 %psum.15 = f32[256]{0:T(256)} all-reduce(f32[256]{0:T(256)S(1)} %convert_reduce_fusion), channel_id=1, replica_groups=mesh['blk'=32,'rep'=8] {'blk','rep'}, use_global_device_ids=true, to_apply=%region_5.6 | all-reduce | flops 256 | bytes 2048 | tf_op jit(solution)/shard_map/psum | solution.py:71
  669.9 242.9 %all-reduce.2.cloned.1.call-done = f32[256,256]{1,0:T(8,128)} async-done(((f32[256,256]{1,0:T(8,128)}), f32[256,256]{1,0:T(8,128)}) %all-reduce.2.cloned.1.call-update) | async-done | bytes 262160 | tf_op jit(solution)/shard_map/psum | solution.py:71
  (101 shorter events, 88.4 us)
Async XLA Ops:
  7.2 0.9 copy-start
  7.2 33.5 %all-gather.5.cloned.1.call-start = ((), (), s32[]{:S(2)}) async-start(), calls=%async_computation.5 | async-start | bytes 1179648 | tf_op jit(solution)/shard_map/all_gather | solution.py:76
  9.9 395.5 %reduce-scatter.5.cloned.1.call-start = ((), (), s32[]{:S(2)}) async-start(), calls=%async_computation.6 | async-start | bytes 8650752 | tf_op jit(solution)/shard_map/reduce_scatter | solution.py:98
  44.0 4.0 copy-start.3
  63.3 4.0 copy-start.3
  85.2 4.0 copy-start.3
  107.0 4.0 copy-start.3
  128.8 4.0 copy-start.3
  150.6 4.0 copy-start.3
  180.6 224.8 %copy-start.2 = (bf16[256,256]{1,0:T(8,128)(2,1)S(1)}, bf16[256,256]{1,0:T(8,128)(2,1)}, u32[]{:S(2)}) copy-start(bf16[256,256]{1,0:T(8,128)(2,1)} %param.13) | copy-start | bytes 393220
  180.6 309.8 %copy-start.4 = (s32[192]{0:T(256)S(1)}, s32[192]{0:T(256)}, u32[]{:S(2)}) copy-start(s32[192]{0:T(256)} %get-tuple-element.527) | copy-start | bytes 2308
  180.6 309.8 %copy-start.5 = (s32[192]{0:T(256)S(1)}, s32[192]{0:T(256)}, u32[]{:S(2)}) copy-start(s32[192]{0:T(256)} %get-tuple-element.528) | copy-start | bytes 2308
  180.6 309.8 %all-gather.3.cloned.1.call-start = ((), (), s32[]{:S(2)}) async-start(), calls=%async_computation.2 | async-start | bytes 4325376 | tf_op jit(solution)/shard_map/all_gather | solution.py:35
  407.2 258.9 %reduce-scatter.3.cloned.1.call-start = ((), (), s32[]{:S(2)}) async-start(), calls=%async_computation.3 | async-start | bytes 2359296 | tf_op jit(solution)/shard_map/reduce_scatter | solution.py:57
  583.7 4.3 copy-start.1
  583.7 84.4 %copy-start.6 = (f32[256]{0:T(256)S(1)}, f32[256]{0:T(256)}, u32[]{:S(2)}) copy-start(f32[256]{0:T(256)} %param.16) | copy-start | bytes 3076
  587.9 324.9 %all-reduce.2.cloned.1.call-start = ((), (), s32[]{:S(2)}) async-start(), calls=%async_computation.4 | async-start | bytes 524288 | tf_op jit(solution)/shard_map/psum | solution.py:71
Sparse Core Ops, SparseCore 0:
  10.4 30.1 all-gather.4
  180.7 224.6 reduce-scatter.4
  408.9 81.4 all-gather.2
  588.0 33.7 reduce-scatter.2
  668.2 244.5 all-reduce.1
where the time goes:
time: 923 us; the launch traced here: 921 us
  waiting for transfers between devices  582 us (63%)
  matrix products  185 us (20%)
  blocking collectives  78.1 us (8%)
  local copies, waits for them, and re-layouts  47 us (5%)
  other arithmetic  15.4 us (2%)
  between operations  13.8 us (1%)
    psum x1, waiting for transfers between devices, shards(): grad_weight, grad_bias = lax.psum((grad_w, grad_b), ('blk', 'rep'))  243 us
    reduce_scatter x1, waiting for transfers between devices, shards(): lax.psum_scatter(col_terms.reshape(group_blocks * tile_size, hidden), 'bl...  225 us
    dot_general x6, matrix products, backward_step(): jnp.einsum('tc,tjh->cjh', selector, products, precision=lax.Precision.HIG...  84.1 us
    all_gather x1, waiting for transfers between devices, shards(): lax.all_gather(scaled, 'blk', axis=0, tiled=True)  83.1 us
    psum x1, blocking collectives, shards(): grad_weight, grad_bias = lax.psum((grad_w, grad_b), ('blk', 'rep'))  78.1 us
    dot_general x6, matrix products, forward_step(): jnp.einsum('tr,tih->rih', selector, products, precision=lax.Precision.HIG...  47.3 us
    all_gather x1, waiting for transfers between devices, shards(): lax.all_gather(grad_scaled, 'rep', axis=0, tiled=True)  30.7 us
    dot_general x6, matrix products, backward_step(): jnp.einsum('tij,tih->tjh', tile_vals, picked, preferred_element_type=jnp....  23.9 us
  transfers between devices with their start and end apart: 5, of which 4 were waited for; matrix products, arithmetic and copies ran while one was open for 0% of the time, Pallas kernels for 0%

commit v1 on v0

v1 whole, which is shorter than its diff:
```python
import jax
import jax.numpy as jnp
from jax import lax
from jax.experimental import pallas as pl
from jax.experimental.pallas import tpu as pltpu
from jax.sharding import Mesh, PartitionSpec as P

F32 = jnp.float32
BF16 = jnp.bfloat16
NX, NZ, NY, NC = 4, 8, 4, 2
H = 256
TILE = 128
TCAP = 192
BAND = 16
GROUP = 64
CHUNK = 48
UNROLL = 8
VMEM_LIMIT = 48 * 1024 * 1024
ALL = ("x", "z", "y", "c")


def tile_steps(count_ref, place_of, product_of, acc_ref, spare):
    first = pl.program_id(0) * CHUNK
    live = jnp.clip(count_ref[0] - first, 0, CHUNK)

    def step(g, carry):
        products, places = [], []
        for u in range(UNROLL):
            t = g * UNROLL + u
            slot = first + t
            places.append(jnp.where(slot < count_ref[0], place_of(slot), spare))
            products.append(product_of(t, slot))
        for u in range(UNROLL):
            acc_ref[places[u]] += products[u]
        return carry

    lax.fori_loop(0, (live + UNROLL - 1) // UNROLL, step, 0)


def clear(acc_ref):
    def zero(i, carry):
        acc_ref[i] = jnp.zeros(acc_ref.shape[1:], F32)
        return carry

    lax.fori_loop(0, acc_ref.shape[0], zero, 0)


def forward_kernel(rows, cols, count, tiles, feats, cot_t, out, grad, acc):
    @pl.when(pl.program_id(0) == 0)
    def _():
        clear(acc)

    tile_steps(
        count,
        lambda slot: rows[slot],
        lambda t, slot: jnp.dot(tiles[t], feats[cols[slot]], preferred_element_type=F32),
        acc,
        BAND,
    )

    @pl.when(pl.program_id(0) == pl.num_programs(0) - 1)
    def _():
        grad[...] = jnp.zeros(grad.shape, F32)

        def finish(i, carry):
            block = acc[i].astype(BF16)
            out[i] = block
            grad[...] += jnp.dot(cot_t[i], block, preferred_element_type=F32)
            return carry

        lax.fori_loop(0, BAND, finish, 0)


def backward_kernel(rows, cols, count, tiles, cot_t, out, acc):
    @pl.when(pl.program_id(0) == 0)
    def _():
        clear(acc)

    tile_steps(
        count,
        lambda slot: cols[slot],
        lambda t, slot: jnp.dot(cot_t[rows[slot]], tiles[t], preferred_element_type=F32),
        acc,
        GROUP,
    )

    @pl.when(pl.program_id(0) == pl.num_programs(0) - 1)
    def _():
        def finish(i, carry):
            out[i] = acc[i].astype(BF16)
            return carry

        lax.fori_loop(0, GROUP, finish, 0)


def whole(shape):
    return pl.BlockSpec(shape, lambda s, *_: (0,) * len(shape))


def tile_block():
    return pl.BlockSpec((CHUNK, TILE, TILE), lambda s, *_: (s, 0, 0))


def forward_tiles(rows, cols, count, tiles, feats, cot_t):
    return pl.pallas_call(
        forward_kernel,
        grid_spec=pltpu.PrefetchScalarGridSpec(
            num_scalar_prefetch=3,
            grid=(TCAP // CHUNK,),
            in_specs=[tile_block(), whole((GROUP, TILE, H)), whole((BAND, H, TILE))],
            out_specs=[whole((BAND, TILE, H)), whole((H, H))],
            scratch_shapes=[pltpu.VMEM((BAND + 1, TILE, H), F32)],
        ),
        out_shape=[
            jax.ShapeDtypeStruct((BAND, TILE, H), BF16),
            jax.ShapeDtypeStruct((H, H), F32),
        ],
        compiler_params=pltpu.CompilerParams(vmem_limit_bytes=VMEM_LIMIT),
        cost_estimate=pl.CostEstimate(
            flops=TCAP * 2 * TILE * TILE * H, bytes_accessed=12 << 20, transcendentals=0
        ),
        name="forward_tiles",
    )(rows, cols, count, tiles, feats, cot_t)


def backward_tiles(rows, cols, count, tiles, cot_t):
    return pl.pallas_call(
        backward_kernel,
        grid_spec=pltpu.PrefetchScalarGridSpec(
            num_scalar_prefetch=3,
            grid=(TCAP // CHUNK,),
            in_specs=[tile_block(), whole((BAND, H, TILE))],
            out_specs=whole((GROUP, H, TILE)),
            scratch_shapes=[pltpu.VMEM((GROUP + 1, H, TILE), F32)],
        ),
        out_shape=jax.ShapeDtypeStruct((GROUP, H, TILE), BF16),
        compiler_params=pltpu.CompilerParams(vmem_limit_bytes=VMEM_LIMIT),
        cost_estimate=pl.CostEstimate(
            flops=TCAP * 2 * TILE * TILE * H, bytes_accessed=12 << 20, transcendentals=0
        ),
        name="backward_tiles",
    )(rows, cols, count, tiles, cot_t)


def shift(value, axis, size, by):
    return lax.ppermute(value, axis, [(i, (i + by) % size) for i in range(size)])


def gather4(value, axis):
    return [value, shift(value, axis, 4, -1), shift(value, axis, 4, 2), shift(value, axis, 4, 1)]


def scatter4(blocks, axis):
    return [
        shift(blocks[1], axis, 4, 1),
        shift(blocks[3], axis, 4, -1),
        shift(blocks[2], axis, 4, 2),
    ]


def swap(value):
    return lax.ppermute(value, "c", [(0, 1), (1, 0)])


def shards(
    features, degree, weight, bias, tile_rows, tile_cols, tile_count, tile_values, cotangent
):
    x, y, c = lax.axis_index("x"), lax.axis_index("y"), lax.axis_index("c")
    rows, cols, tiles = tile_rows[0], tile_cols[0], tile_values[0]
    inv_root = lax.rsqrt(degree.astype(F32))
    scaled = (features.astype(F32) * inv_root[:, None]).astype(BF16)
    cot = cotangent.astype(F32)
    cot_t = (cot * inv_root[:, None]).astype(BF16).reshape(2, TILE, H).transpose(0, 2, 1)

    row_dev = rows >> 1
    row_at = ((((row_dev & 1) ^ c) * 4 + (((row_dev >> 1) - y) & 3)) << 1) | (rows & 1)
    col_dev = cols >> 1
    col_x, col_z = (((col_dev >> 3) - x) & 3), col_dev & 7
    fwd_col = ((col_z * 4 + col_x) << 1) | (cols & 1)
    bwd_col = ((col_x * 8 + col_z) << 1) | (cols & 1)

    near = jnp.concatenate(gather4(scaled, "x"))
    feats = lax.all_gather(near, "z", axis=0, tiled=True).reshape(GROUP, TILE, H)

    cot_y = jnp.concatenate(gather4(cot_t, "y"))
    cot_band = jnp.concatenate([cot_y, swap(cot_y)])

    col_terms = backward_tiles(row_at, bwd_col, tile_count, tiles, cot_band)
    col_terms = col_terms.reshape(NX, NZ, 2, H, TILE)

    def add(a, b):
        return (a.astype(F32) + b.astype(F32)).astype(BF16)

    right1 = shift(col_terms[2, :4], "x", NX, 1)
    left1 = shift(col_terms[2, 4:], "x", NX, -1)
    right2 = shift(col_terms[1, 4:], "x", NX, 1)
    left2 = shift(col_terms[3, :4], "x", NX, -1)
    right3 = shift(add(col_terms[1, :4], right1), "x", NX, 1)
    left3 = shift(add(col_terms[3, 4:], left1), "x", NX, -1)

    band_terms, grad_t = forward_tiles(row_at, fwd_col, tile_count, tiles, feats, cot_band)
    band_terms = band_terms.reshape(NC, NY, 2 * TILE, H)
    half = band_terms[0].astype(F32) + swap(band_terms[1]).astype(F32)
    half16 = half.astype(BF16)
    total = half[0]
    for part in scatter4(half16, "y"):
        total = total + part.astype(F32)
    aggregated = (total * inv_root[:, None]).astype(BF16)
    layer_out = (jnp.dot(aggregated, weight, preferred_element_type=F32) + bias).astype(BF16)

    cot_sum = jnp.sum(cot, axis=0)
    extra = jnp.zeros((8, 8, H), F32).at[:, 0].set(
        jnp.where(jnp.arange(8)[:, None] == 0, cot_sum[None, :], 0.0)
    )
    chunks = jnp.concatenate([grad_t.reshape(8, 32, H), extra], axis=1).reshape(NY, NC, 40, H)
    keep = lax.dynamic_index_in_dim(chunks, c, 1, keepdims=False)
    give = lax.dynamic_index_in_dim(chunks, 1 - c, 1, keepdims=False)
    keep = keep + swap(give)
    keep = [lax.dynamic_index_in_dim(keep, (y + o) & 3, 0, keepdims=False) for o in range(4)]
    part = keep[0]
    for other in scatter4(keep, "y"):
        part = part + other
    near_parts = gather4(part, "x")
    part = (near_parts[0] + near_parts[2]) + (near_parts[1] + near_parts[3])
    part = jnp.sum(
        lax.all_to_all(jnp.broadcast_to(part, (NZ, 40, H)), "z", 0, 0, tiled=True), axis=0
    )
    by_y = jnp.stack(gather4(part, "y"))
    by_y = jnp.take(by_y, (jnp.arange(4) - y) & 3, axis=0)
    by_c = lax.all_gather(by_y, "c", axis=1)
    grad_weight = by_c[:, :, :32].reshape(H, H).T
    grad_bias = by_c[0, 0, 32]

    own_x = jnp.concatenate(
        [
            col_terms[0, :4].astype(F32) + right3.astype(F32) + left2.astype(F32),
            col_terms[0, 4:].astype(F32) + right2.astype(F32) + left3.astype(F32),
        ]
    ).astype(BF16)
    parts = lax.all_to_all(own_x, "z", 0, 0, tiled=True)
    own = jnp.sum(parts.astype(F32), axis=0)
    grad_features = jnp.einsum(
        "ahn,gh->ang", own, weight.astype(F32), precision=lax.Precision.HIGHEST
    ).reshape(2 * TILE, H)
    grad_features = (grad_features * inv_root[:, None]).astype(BF16)
    return (layer_out, grad_weight, grad_bias, grad_features)


def solution(mesh):
    split = Mesh(mesh.devices.reshape(NX, NZ, NY, NC), ALL)
    return jax.shard_map(
        shards,
        mesh=split,
        in_specs=(
            P(ALL, None),
            P(ALL),
            P(),
            P(),
            P(ALL, None),
            P(ALL, None),
            P(ALL),
            P(ALL, None, None, None),
            P(ALL, None),
        ),
        out_specs=(P(ALL, None), P(), P(), P(ALL, None)),
        check_vma=False,
    )
```

time: 923 us -> 168 us (0.18)
  waiting for transfers between devices: 582 us -> 57 us
  matrix products: 185 us -> 1.89 us
  blocking collectives: 78.1 us -> 7.69 us
  starting transfers between devices: 0.21 us -> 53.1 us
  local copies, waits for them, and re-layouts: 47 us -> 4.92 us
  Pallas kernels: 0 us -> 19.6 us
    psum x1 -> x0, waiting for transfers between devices: 243 us -> none  [shards(): grad_weight, grad_bias = lax.psum((grad_w, grad_b), ('blk', 'rep'))]
    reduce_scatter x2 -> x0, waiting for transfers between devices: 225 us -> none  [the longest x1 225 us: shards(): lax.psum_scatter(col_terms.reshape(group_blocks * tile_size, hidden), 'bl...]
    dot_general x27 -> x2, matrix products: 185 us -> 1.89 us  [the longest x1 1 us: shards(): jnp.einsum('ahn,gh->ang', own, weight.astype(F32), precision=lax.Precisio...]
    all_gather x2 -> x1, waiting for transfers between devices: 114 us -> 0.01 us  [shards(): lax.all_gather(near, 'z', axis=0, tiled=True).reshape(GROUP, TILE, H)]
    psum x1 -> x0, blocking collectives: 78.1 us -> none  [shards(): grad_weight, grad_bias = lax.psum((grad_w, grad_b), ('blk', 'rep'))]
    ppermute x0 -> x27, waiting for transfers between devices: none -> 51.8 us  [the longest x24 51 us: shift(): lax.ppermute(value, axis, [(i, (i + by) % size) for i in range(size)])]
    ppermute x0 -> x27, starting transfers between devices: none -> 42.4 us  [the longest x24 37.1 us: shift(): lax.ppermute(value, axis, [(i, (i + by) % size) for i in range(size)])]
    gather x12 -> x1, local copies, waits for them, and re-layouts: 28.6 us -> 0.56 us  [shards(): by_y = jnp.take(by_y, jnp.arange(4) - y & 3, axis=0)]
  transfers between devices with their start and end apart: 5 -> 30, of which waited for: 4 -> 14; matrix products, arithmetic and copies ran while one was open for 0% -> 7% of each run, Pallas kernels for 0% -> 12%
where the time goes in v1:
time: 168 us
  waiting for transfers between devices  57 us (34%)
  starting transfers between devices  53.1 us (32%)
  Pallas kernels  19.6 us (12%)
  between operations  14.9 us (9%)
  other arithmetic  8.88 us (5%)
  blocking collectives  7.69 us (5%)
  local copies, waits for them, and re-layouts  4.92 us (3%)
  matrix products  1.89 us (1%)
    ppermute x24, waiting for transfers between devices, shift(): lax.ppermute(value, axis, [(i, (i + by) % size) for i in range(size)])  51 us
    ppermute x24, starting transfers between devices, shift(): lax.ppermute(value, axis, [(i, (i + by) % size) for i in range(size)])  37.1 us
    pallas_call x1, Pallas kernels, forward_tiles(): pl.pallas_call(forward_kernel, grid_spec=pltpu.PrefetchScalarGridSpec(num...  11.3 us
    pallas_call x1, Pallas kernels, backward_tiles(): pl.pallas_call(backward_kernel, grid_spec=pltpu.PrefetchScalarGridSpec(nu...  8.23 us
    all_gather x1, blocking collectives, shards(): by_c = lax.all_gather(by_y, 'c', axis=1)  7.69 us
    all_to_all x1, starting transfers between devices, shards(): parts = lax.all_to_all(own_x, 'z', 0, 0, tiled=True)  5.73 us
    ppermute x3, starting transfers between devices, swap(): return lax.ppermute(value, 'c', [(0, 1), (1, 0)])  5.33 us
    all_to_all x1, waiting for transfers between devices, shards(): lax.all_to_all(jnp.broadcast_to(part, (NZ, 40, H)), 'z', 0, 0, tiled=True)  5.12 us
  transfers between devices with their start and end apart: 30, of which 14 were waited for; matrix products, arithmetic and copies ran while one was open for 7% of the time, Pallas kernels for 12%

profile of v1, /device:TPU:1, one launch (start us, length us, event | category | flops | bytes accessed | tf_op | source)
XLA Modules:
  0.0 167.9 jit_solution(5691374070117917845)
XLA Ops:
  9.0 2.1 %collective-permute-start.2 = (bf16[256,256]{1,0:T(8,128)(2,1)S(1)}, bf16[256,256]{1,0:T(8,128)(2,1)S(1)}, u32[]{:S(2)}, u32[]{:S(2)}) collective-permute-start(bf16[256,256]{1,0:T(8,128)(2,1)S(1)} %get-tuple-element.52), channel_id=1, source_target_pairs={{0,64},{64,128},{128,192},{192,0},{1,65},{65,129},{129,193},{193,1... | collective-permute-start | bytes 393224 | tf_op jit(solution)/shard_map/ppermute | solution.py:146
  11.1 2.5 %collective-permute-start.1 = (bf16[256,256]{1,0:T(8,128)(2,1)S(1)}, bf16[256,256]{1,0:T(8,128)(2,1)S(1)}, u32[]{:S(2)}, u32[]{:S(2)}) collective-permute-start(bf16[256,256]{1,0:T(8,128)(2,1)S(1)} %get-tuple-element.52), channel_id=1, source_target_pairs={{0,128},{64,192},{128,0},{192,64},{1,129},{65,193},{129,1},{193,65... | collective-permute-start | bytes 393224 | tf_op jit(solution)/shard_map/ppermute | solution.py:146
  14.8 4.5 %collective-permute-done.1 = bf16[256,256]{1,0:T(8,128)(2,1)S(1)} collective-permute-done((bf16[256,256]{1,0:T(8,128)(2,1)S(1)}, bf16[256,256]{1,0:T(8,128)(2,1)S(1)}, u32[]{:S(2)}, u32[]{:S(2)}) %collective-permute-start.1) | collective-permute-done | bytes 131104 | tf_op jit(solution)/shard_map/ppermute | solution.py:146
  21.7 2.6 %collective-permute-start.4 = (bf16[2,256,128]{2,1,0:T(8,128)(2,1)S(1)}, bf16[2,256,128]{2,1,0:T(8,128)(2,1)S(1)}, u32[]{:S(2)}, u32[]{:S(2)}) collective-permute-start(bf16[2,256,128]{2,1,0:T(8,128)(2,1)S(1)} %bitcast.114), channel_id=1, source_target_pairs={{0,4},{2,6},{4,0},{6,2},{1,5},{3,7},{5,1},{7,3},{8,12},{10,14},{12... | collective-permute-start | bytes 393224 | tf_op jit(solution)/shard_map/ppermute | solution.py:146
  26.7 2.0 %collective-permute-done.4 = bf16[2,256,128]{2,1,0:T(8,128)(2,1)S(1)} collective-permute-done((bf16[2,256,128]{2,1,0:T(8,128)(2,1)S(1)}, bf16[2,256,128]{2,1,0:T(8,128)(2,1)S(1)}, u32[]{:S(2)}, u32[]{:S(2)}) %collective-permute-start.4) | collective-permute-done | bytes 131104 | tf_op jit(solution)/shard_map/ppermute | solution.py:146
  29.4 2.4 %collective-permute-start.6 = (bf16[8,256,128]{2,1,0:T(8,128)(2,1)S(1)}, bf16[8,256,128]{2,1,0:T(8,128)(2,1)S(1)}, u32[]{:S(2)}, u32[]{:S(2)}) collective-permute-start(bf16[8,256,128]{2,1,0:T(8,128)(2,1)S(1)} %pad_maximum_fusion.2), channel_id=1, source_target_pairs={{0,1},{1,0},{2,3},{3,2},{4,5},{5,4},{6,7},{7,6},{8,9},{9,8},{10,11... | collective-permute-start | bytes 1572872 | tf_op jit(solution)/shard_map/ppermute | solution.py:162
  33.4 8.2 %backward_tiles.1 = bf16[64,256,128]{2,1,0:T(8,128)(2,1)S(1)} custom-call(s32[192]{0:T(256)S(1)} %bitcast.107, s32[192]{0:T(256)S(1)} %get-tuple-element.50.cols, s32[1]{0:T(128)S(6)} %copy.29.count, bf16[192,128,128]{2,1,0:T(8,128)(2,1)} %bitcast.109, bf16[16,256,128]{2,1,0:T(8,128)(2,1)S(1)} %constant_dynamic-update-slice_fusion.cot_t), custom_call_target="tpu_custom_call" | custom-call | flops 1610612736 | bytes 12582912 | tf_op jit(solution)/shard_map/backward_tiles/pallas_call | solution.py:127
  43.1 3.0 %collective-permute-start.25 = (bf16[4,2,256,128]{3,2,1,0:T(8,128)(2,1)S(1)}, bf16[4,2,256,128]{3,2,1,0:T(8,128)(2,1)S(1)}, u32[]{:S(2)}, u32[]{:S(2)}) collective-permute-start(bf16[4,2,256,128]{3,2,1,0:T(8,128)(2,1)S(1)} %get-tuple-element.35), channel_id=1, source_target_pairs={{0,192},{64,0},{128,64},{192,128},{1,193},{65,1},{129,65},{193,129... | collective-permute-start | bytes 1572872 | tf_op jit(solution)/shard_map/ppermute | solution.py:146
  47.5 9.9 %collective-permute-done.21 = bf16[4,2,256,128]{3,2,1,0:T(8,128)(2,1)S(1)} collective-permute-done((bf16[4,2,256,128]{3,2,1,0:T(8,128)(2,1)S(1)}, bf16[4,2,256,128]{3,2,1,0:T(8,128)(2,1)S(1)}, u32[]{:S(2)}, u32[]{:S(2)}) %collective-permute-start.21) | collective-permute-done | bytes 524320 | tf_op jit(solution)/shard_map/ppermute | solution.py:146
  57.9 10.3 %collective-permute-done.23 = bf16[4,2,256,128]{3,2,1,0:T(8,128)(2,1)S(1)} collective-permute-done((bf16[4,2,256,128]{3,2,1,0:T(8,128)(2,1)S(1)}, bf16[4,2,256,128]{3,2,1,0:T(8,128)(2,1)S(1)}, u32[]{:S(2)}, u32[]{:S(2)}) %collective-permute-start.23) | collective-permute-done | bytes 524320 | tf_op jit(solution)/shard_map/ppermute | solution.py:146
  68.2 4.6 %collective-permute-done.22 = bf16[4,2,256,128]{3,2,1,0:T(8,128)(2,1)S(1)} collective-permute-done((bf16[4,2,256,128]{3,2,1,0:T(8,128)(2,1)S(1)}, bf16[4,2,256,128]{3,2,1,0:T(8,128)(2,1)S(1)}, u32[]{:S(2)}, u32[]{:S(2)}) %collective-permute-start.22) | collective-permute-done | bytes 524320 | tf_op jit(solution)/shard_map/ppermute | solution.py:146
  73.8 9.4 %collective-permute-done.24 = bf16[4,2,256,128]{3,2,1,0:T(8,128)(2,1)S(1)} collective-permute-done((bf16[4,2,256,128]{3,2,1,0:T(8,128)(2,1)S(1)}, bf16[4,2,256,128]{3,2,1,0:T(8,128)(2,1)S(1)}, u32[]{:S(2)}, u32[]{:S(2)}) %collective-permute-start.24) | collective-permute-done | bytes 524320 | tf_op jit(solution)/shard_map/ppermute | solution.py:146
  83.2 3.7 %collective-permute-done.26 = bf16[4,2,256,128]{3,2,1,0:T(8,128)(2,1)S(1)} collective-permute-done((bf16[4,2,256,128]{3,2,1,0:T(8,128)(2,1)S(1)}, bf16[4,2,256,128]{3,2,1,0:T(8,128)(2,1)S(1)}, u32[]{:S(2)}, u32[]{:S(2)}) %collective-permute-start.26) | collective-permute-done | bytes 524320 | tf_op jit(solution)/shard_map/ppermute | solution.py:146
  88.2 5.7 %all-to-all-start.1 = ((bf16[8,2,256,128]{3,2,1,0:T(8,128)(2,1)}), bf16[8,2,256,128]{3,2,1,0:T(8,128)(2,1)S(1)}, u32[]{:S(2)}, u32[]{:S(2)}) async-start(bf16[8,2,256,128]{3,2,1,0:T(8,128)(2,1)} %pad_maximum_fusion), calls=%async_computation.1 | async-start | bytes 2097152 | tf_op jit(solution)/shard_map/all_to_all | solution.py:240
  95.2 11.3 %forward_tiles.1 = (bf16[16,128,256]{2,1,0:T(8,128)(2,1)S(1)}, f32[256,256]{1,0:T(8,128)S(1)}) custom-call(s32[192]{0:T(256)S(1)} %bitcast.108, s32[192]{0:T(256)S(1)} %get-tuple-element.51.cols, s32[1]{0:T(128)S(6)} %copy.29.count, bf16[192,128,128]{2,1,0:T(8,128)(2,1)} %bitcast.110, bf16[64,128,256]{2,1,0:T(8,128)(2,1)} %bitcast.111, ...), custom_call_target="tpu_custom_call" | custom-call | flops 1610612736 | bytes 12582912 | tf_op jit(solution)/shard_map/forward_tiles/pallas_call | solution.py:105
  112.0 5.7 %collective-permute-start.14 = (f32[40,256]{1,0:T(8,128)S(1)}, f32[40,256]{1,0:T(8,128)S(1)}, u32[]{:S(2)}, u32[]{:S(2)}) collective-permute-start(f32[40,256]{1,0:T(8,128)S(1)} %get-tuple-element.46), channel_id=1, source_target_pairs={{0,4},{2,6},{4,0},{6,2},{1,5},{3,7},{5,1},{7,3},{8,12},{10,14},{12... | collective-permute-start | bytes 122888 | tf_op jit(solution)/shard_map/ppermute | solution.py:146
  117.7 2.0 %collective-permute-start.13 = (f32[40,256]{1,0:T(8,128)S(1)}, f32[40,256]{1,0:T(8,128)S(1)}, u32[]{:S(2)}, u32[]{:S(2)}) collective-permute-start(f32[40,256]{1,0:T(8,128)S(1)} %get-tuple-element.47), channel_id=1, source_target_pairs={{0,6},{2,0},{4,2},{6,4},{1,7},{3,1},{5,3},{7,5},{8,14},{10,8},{12,... | collective-permute-start | bytes 122888 | tf_op jit(solution)/shard_map/ppermute | solution.py:146
  121.7 2.7 %collective-permute-start.16 = (f32[40,256]{1,0:T(8,128)S(1)}, f32[40,256]{1,0:T(8,128)S(1)}, u32[]{:S(2)}, u32[]{:S(2)}) collective-permute-start(f32[40,256]{1,0:T(8,128)S(1)} %fusion.22), channel_id=1, source_target_pairs={{0,192},{64,0},{128,64},{192,128},{1,193},{65,1},{129,65},{193,129... | collective-permute-start | bytes 122888 | tf_op jit(solution)/shard_map/ppermute | solution.py:146
  125.8 3.0 %collective-permute-done.15 = f32[40,256]{1,0:T(8,128)S(1)} collective-permute-done((f32[40,256]{1,0:T(8,128)S(1)}, f32[40,256]{1,0:T(8,128)S(1)}, u32[]{:S(2)}, u32[]{:S(2)}) %collective-permute-start.15) | collective-permute-done | bytes 40992 | tf_op jit(solution)/shard_map/ppermute | solution.py:146
  129.5 4.9 %all-to-all-start = ((f32[8,40,256]{2,1,0:T(8,128)}), f32[8,40,256]{2,1,0:T(8,128)S(1)}, u32[]{:S(2)}, u32[]{:S(2)}) async-start(f32[8,40,256]{2,1,0:T(8,128)} %broadcast_in_dim.45), calls=%async_computation | async-start | bytes 655360 | tf_op jit(solution)/shard_map/all_to_all | solution.py:226
  135.3 3.1 %collective-permute-start.10 = (bf16[256,256]{1,0:T(8,128)(2,1)S(1)}, bf16[256,256]{1,0:T(8,128)(2,1)S(1)}, u32[]{:S(2)}, u32[]{:S(2)}) collective-permute-start(bf16[256,256]{1,0:T(8,128)(2,1)S(1)} %get-tuple-element.43), channel_id=1, source_target_pairs={{0,4},{2,6},{4,0},{6,2},{1,5},{3,7},{5,1},{7,3},{8,12},{10,14},{12... | collective-permute-start | bytes 393224 | tf_op jit(solution)/shard_map/ppermute | solution.py:146
  139.4 5.1 %all-to-all-done = f32[8,40,256]{2,1,0:T(8,128)S(1)} async-done(((f32[8,40,256]{2,1,0:T(8,128)}), f32[8,40,256]{2,1,0:T(8,128)S(1)}, u32[]{:S(2)}, u32[]{:S(2)}) %all-to-all-start) | async-done | bytes 327712 | tf_op jit(solution)/shard_map/all_to_all | solution.py:226
  145.3 3.1 %collective-permute-start.19 = (f32[40,256]{1,0:T(8,128)S(1)}, f32[40,256]{1,0:T(8,128)S(1)}, u32[]{:S(2)}, u32[]{:S(2)}) collective-permute-start(f32[40,256]{1,0:T(8,128)S(1)} %reduce_sum.28), channel_id=1, source_target_pairs={{0,4},{2,6},{4,0},{6,2},{1,5},{3,7},{5,1},{7,3},{8,12},{10,14},{12... | collective-permute-start | bytes 122888 | tf_op jit(solution)/shard_map/ppermute | solution.py:146
  151.9 7.7 %all_gather.8 = f32[4,2,40,256]{3,2,0,1:T(8,128)S(1)} all-gather(f32[4,1,40,256]{3,2,0,1:T(8,128)S(1)} %bitcast_select_fusion), channel_id=1, replica_groups=mesh['x'=4,'z'=8,'y'=4,'c'=2] {'c'}, dimensions={1}, use_global_device_ids=true | all-gather | bytes 491520 | tf_op jit(solution)/shard_map/all_gather | solution.py:230
  (93 shorter events, 33.5 us)
Async XLA Ops:
  7.2 88.0 %all-gather.2.cloned.1.call-start = ((), (), s32[]{:S(2)}) async-start(), calls=%async_computation.2 | async-start | bytes 4718592 | tf_op jit(solution)/shard_map/all_gather | solution.py:183
  9.0 5.7 %collective-permute-start.2 = (bf16[256,256]{1,0:T(8,128)(2,1)S(1)}, bf16[256,256]{1,0:T(8,128)(2,1)S(1)}, u32[]{:S(2)}, u32[]{:S(2)}) collective-permute-start(bf16[256,256]{1,0:T(8,128)(2,1)S(1)} %get-tuple-element.52), channel_id=1, source_target_pairs={{0,64},{64,128},{128,192},{192,0},{1,65},{65,129},{129,193},{193,1... | collective-permute-start | bytes 393224 | tf_op jit(solution)/shard_map/ppermute | solution.py:146
  11.1 8.2 %collective-permute-start.1 = (bf16[256,256]{1,0:T(8,128)(2,1)S(1)}, bf16[256,256]{1,0:T(8,128)(2,1)S(1)}, u32[]{:S(2)}, u32[]{:S(2)}) collective-permute-start(bf16[256,256]{1,0:T(8,128)(2,1)S(1)} %get-tuple-element.52), channel_id=1, source_target_pairs={{0,128},{64,192},{128,0},{192,64},{1,129},{65,193},{129,1},{193,65... | collective-permute-start | bytes 393224 | tf_op jit(solution)/shard_map/ppermute | solution.py:146
  13.6 5.7 %collective-permute-start = (bf16[256,256]{1,0:T(8,128)(2,1)S(1)}, bf16[256,256]{1,0:T(8,128)(2,1)S(1)}, u32[]{:S(2)}, u32[]{:S(2)}) collective-permute-start(bf16[256,256]{1,0:T(8,128)(2,1)S(1)} %get-tuple-element.52), channel_id=1, source_target_pairs={{0,192},{64,0},{128,64},{192,128},{1,193},{65,1},{129,65},{193,129... | collective-permute-start | bytes 393224 | tf_op jit(solution)/shard_map/ppermute | solution.py:146
  20.3 6.4 %collective-permute-start.5 = (bf16[2,256,128]{2,1,0:T(8,128)(2,1)S(1)}, bf16[2,256,128]{2,1,0:T(8,128)(2,1)S(1)}, u32[]{:S(2)}, u32[]{:S(2)}) collective-permute-start(bf16[2,256,128]{2,1,0:T(8,128)(2,1)S(1)} %bitcast.113), channel_id=1, source_target_pairs={{0,2},{2,4},{4,6},{6,0},{1,3},{3,5},{5,7},{7,1},{8,10},{10,12},{12... | collective-permute-start | bytes 393224 | tf_op jit(solution)/shard_map/ppermute | solution.py:146
  21.7 7.1 %collective-permute-start.4 = (bf16[2,256,128]{2,1,0:T(8,128)(2,1)S(1)}, bf16[2,256,128]{2,1,0:T(8,128)(2,1)S(1)}, u32[]{:S(2)}, u32[]{:S(2)}) collective-permute-start(bf16[2,256,128]{2,1,0:T(8,128)(2,1)S(1)} %bitcast.114), channel_id=1, source_target_pairs={{0,4},{2,6},{4,0},{6,2},{1,5},{3,7},{5,1},{7,3},{8,12},{10,14},{12... | collective-permute-start | bytes 393224 | tf_op jit(solution)/shard_map/ppermute | solution.py:146
  24.3 5.1 %collective-permute-start.3 = (bf16[2,256,128]{2,1,0:T(8,128)(2,1)S(1)}, bf16[2,256,128]{2,1,0:T(8,128)(2,1)S(1)}, u32[]{:S(2)}, u32[]{:S(2)}) collective-permute-start(bf16[2,256,128]{2,1,0:T(8,128)(2,1)S(1)} %bitcast.115), channel_id=1, source_target_pairs={{0,6},{2,0},{4,2},{6,4},{1,7},{3,1},{5,3},{7,5},{8,14},{10,8},{12,... | collective-permute-start | bytes 393224 | tf_op jit(solution)/shard_map/ppermute | solution.py:146
  41.8 15.6 %collective-permute-start.21 = (bf16[4,2,256,128]{3,2,1,0:T(8,128)(2,1)S(1)}, bf16[4,2,256,128]{3,2,1,0:T(8,128)(2,1)S(1)}, u32[]{:S(2)}, u32[]{:S(2)}) collective-permute-start(bf16[4,2,256,128]{3,2,1,0:T(8,128)(2,1)S(1)} %get-tuple-element.34), channel_id=1, source_target_pairs={{0,64},{64,128},{128,192},{192,0},{1,65},{65,129},{129,193},{193,1... | collective-permute-start | bytes 1572872 | tf_op jit(solution)/shard_map/ppermute | solution.py:146
  43.1 14.8 %collective-permute-start.25 = (bf16[4,2,256,128]{3,2,1,0:T(8,128)(2,1)S(1)}, bf16[4,2,256,128]{3,2,1,0:T(8,128)(2,1)S(1)}, u32[]{:S(2)}, u32[]{:S(2)}) collective-permute-start(bf16[4,2,256,128]{3,2,1,0:T(8,128)(2,1)S(1)} %get-tuple-element.35), channel_id=1, source_target_pairs={{0,192},{64,0},{128,64},{192,128},{1,193},{65,1},{129,65},{193,129... | collective-permute-start | bytes 1572872 | tf_op jit(solution)/shard_map/ppermute | solution.py:146
  46.1 22.1 %collective-permute-start.23 = (bf16[4,2,256,128]{3,2,1,0:T(8,128)(2,1)S(1)}, bf16[4,2,256,128]{3,2,1,0:T(8,128)(2,1)S(1)}, u32[]{:S(2)}, u32[]{:S(2)}) collective-permute-start(bf16[4,2,256,128]{3,2,1,0:T(8,128)(2,1)S(1)} %get-tuple-element.37), channel_id=1, source_target_pairs={{0,192},{64,0},{128,64},{192,128},{1,193},{65,1},{129,65},{193,129... | collective-permute-start | bytes 1572872 | tf_op jit(solution)/shard_map/ppermute | solution.py:146
  57.5 15.3 %collective-permute-start.22 = (bf16[4,2,256,128]{3,2,1,0:T(8,128)(2,1)S(1)}, bf16[4,2,256,128]{3,2,1,0:T(8,128)(2,1)S(1)}, u32[]{:S(2)}, u32[]{:S(2)}) collective-permute-start(bf16[4,2,256,128]{3,2,1,0:T(8,128)(2,1)S(1)} %fusion.5), channel_id=1, source_target_pairs={{0,64},{64,128},{128,192},{192,0},{1,65},{65,129},{129,193},{193,1... | collective-permute-start | bytes 1572872 | tf_op jit(solution)/shard_map/ppermute | solution.py:146
  57.6 25.6 %collective-permute-start.24 = (bf16[4,2,256,128]{3,2,1,0:T(8,128)(2,1)S(1)}, bf16[4,2,256,128]{3,2,1,0:T(8,128)(2,1)S(1)}, u32[]{:S(2)}, u32[]{:S(2)}) collective-permute-start(bf16[4,2,256,128]{3,2,1,0:T(8,128)(2,1)S(1)} %get-tuple-element.36), channel_id=1, source_target_pairs={{0,64},{64,128},{128,192},{192,0},{1,65},{65,129},{129,193},{193,1... | collective-permute-start | bytes 1572872 | tf_op jit(solution)/shard_map/ppermute | solution.py:146
  73.1 13.8 %collective-permute-start.26 = (bf16[4,2,256,128]{3,2,1,0:T(8,128)(2,1)S(1)}, bf16[4,2,256,128]{3,2,1,0:T(8,128)(2,1)S(1)}, u32[]{:S(2)}, u32[]{:S(2)}) collective-permute-start(bf16[4,2,256,128]{3,2,1,0:T(8,128)(2,1)S(1)} %get-tuple-element.33), channel_id=1, source_target_pairs={{0,192},{64,0},{128,64},{192,128},{1,193},{65,1},{129,65},{193,129... | collective-permute-start | bytes 1572872 | tf_op jit(solution)/shard_map/ppermute | solution.py:146
  88.2 36.2 %all-to-all-start.1 = ((bf16[8,2,256,128]{3,2,1,0:T(8,128)(2,1)}), bf16[8,2,256,128]{3,2,1,0:T(8,128)(2,1)S(1)}, u32[]{:S(2)}, u32[]{:S(2)}) async-start(bf16[8,2,256,128]{3,2,1,0:T(8,128)(2,1)} %pad_maximum_fusion), calls=%async_computation.1 | async-start | bytes 2097152 | tf_op jit(solution)/shard_map/all_to_all | solution.py:240
  110.5 11.1 %collective-permute-start.12 = (f32[40,256]{1,0:T(8,128)S(1)}, f32[40,256]{1,0:T(8,128)S(1)}, u32[]{:S(2)}, u32[]{:S(2)}) collective-permute-start(f32[40,256]{1,0:T(8,128)S(1)} %get-tuple-element.45), channel_id=1, source_target_pairs={{0,2},{2,4},{4,6},{6,0},{1,3},{3,5},{5,7},{7,1},{8,10},{10,12},{12... | collective-permute-start | bytes 122888 | tf_op jit(solution)/shard_map/ppermute | solution.py:146
  112.0 9.6 %collective-permute-start.14 = (f32[40,256]{1,0:T(8,128)S(1)}, f32[40,256]{1,0:T(8,128)S(1)}, u32[]{:S(2)}, u32[]{:S(2)}) collective-permute-start(f32[40,256]{1,0:T(8,128)S(1)} %get-tuple-element.46), channel_id=1, source_target_pairs={{0,4},{2,6},{4,0},{6,2},{1,5},{3,7},{5,1},{7,3},{8,12},{10,14},{12... | collective-permute-start | bytes 122888 | tf_op jit(solution)/shard_map/ppermute | solution.py:146
  120.5 13.9 %collective-permute-start.7 = (bf16[4,256,256]{2,1,0:T(8,128)(2,1)}, bf16[4,256,256]{2,1,0:T(8,128)(2,1)S(1)}, u32[]{:S(2)}, u32[]{:S(2)}) collective-permute-start(bf16[4,256,256]{2,1,0:T(8,128)(2,1)} %bitcast.9), channel_id=1, source_target_pairs={{0,1},{1,0},{2,3},{3,2},{4,5},{5,4},{6,7},{7,6},{8,9},{9,8},{10,11... | collective-permute-start | bytes 1572872 | tf_op jit(solution)/shard_map/ppermute | solution.py:162
  124.4 4.4 %collective-permute-start.15 = (f32[40,256]{1,0:T(8,128)S(1)}, f32[40,256]{1,0:T(8,128)S(1)}, u32[]{:S(2)}, u32[]{:S(2)}) collective-permute-start(f32[40,256]{1,0:T(8,128)S(1)} %fusion.22), channel_id=1, source_target_pairs={{0,128},{64,192},{128,0},{192,64},{1,129},{65,193},{129,1},{193,65... | collective-permute-start | bytes 122888 | tf_op jit(solution)/shard_map/ppermute | solution.py:146
  129.5 15.0 %all-to-all-start = ((f32[8,40,256]{2,1,0:T(8,128)}), f32[8,40,256]{2,1,0:T(8,128)S(1)}, u32[]{:S(2)}, u32[]{:S(2)}) async-start(f32[8,40,256]{2,1,0:T(8,128)} %broadcast_in_dim.45), calls=%async_computation | async-start | bytes 655360 | tf_op jit(solution)/shard_map/all_to_all | solution.py:226
  134.6 13.8 %collective-permute-start.8 = (bf16[256,256]{1,0:T(8,128)(2,1)S(1)}, bf16[256,256]{1,0:T(8,128)(2,1)S(1)}, u32[]{:S(2)}, u32[]{:S(2)}) collective-permute-start(bf16[256,256]{1,0:T(8,128)(2,1)S(1)} %get-tuple-element.42), channel_id=1, source_target_pairs={{0,2},{2,4},{4,6},{6,0},{1,3},{3,5},{5,7},{7,1},{8,10},{10,12},{12... | collective-permute-start | bytes 393224 | tf_op jit(solution)/shard_map/ppermute | solution.py:146
  135.3 13.1 %collective-permute-start.10 = (bf16[256,256]{1,0:T(8,128)(2,1)S(1)}, bf16[256,256]{1,0:T(8,128)(2,1)S(1)}, u32[]{:S(2)}, u32[]{:S(2)}) collective-permute-start(bf16[256,256]{1,0:T(8,128)(2,1)S(1)} %get-tuple-element.43), channel_id=1, source_target_pairs={{0,4},{2,6},{4,0},{6,2},{1,5},{3,7},{5,1},{7,3},{8,12},{10,14},{12... | collective-permute-start | bytes 393224 | tf_op jit(solution)/shard_map/ppermute | solution.py:146
  138.4 10.0 %collective-permute-start.9 = (bf16[256,256]{1,0:T(8,128)(2,1)S(1)}, bf16[256,256]{1,0:T(8,128)(2,1)S(1)}, u32[]{:S(2)}, u32[]{:S(2)}) collective-permute-start(bf16[256,256]{1,0:T(8,128)(2,1)S(1)} %get-tuple-element.44), channel_id=1, source_target_pairs={{0,6},{2,0},{4,2},{6,4},{1,7},{3,1},{5,3},{7,5},{8,14},{10,8},{12,... | collective-permute-start | bytes 393224 | tf_op jit(solution)/shard_map/ppermute | solution.py:146
  144.6 4.7 %collective-permute-start.20 = (f32[40,256]{1,0:T(8,128)S(1)}, f32[40,256]{1,0:T(8,128)S(1)}, u32[]{:S(2)}, u32[]{:S(2)}) collective-permute-start(f32[40,256]{1,0:T(8,128)S(1)} %reduce_sum.28), channel_id=1, source_target_pairs={{0,2},{2,4},{4,6},{6,0},{1,3},{3,5},{5,7},{7,1},{8,10},{10,12},{12... | collective-permute-start | bytes 122888 | tf_op jit(solution)/shard_map/ppermute | solution.py:146
  145.3 4.9 %collective-permute-start.19 = (f32[40,256]{1,0:T(8,128)S(1)}, f32[40,256]{1,0:T(8,128)S(1)}, u32[]{:S(2)}, u32[]{:S(2)}) collective-permute-start(f32[40,256]{1,0:T(8,128)S(1)} %reduce_sum.28), channel_id=1, source_target_pairs={{0,4},{2,6},{4,0},{6,2},{1,5},{3,7},{5,1},{7,3},{8,12},{10,14},{12... | collective-permute-start | bytes 122888 | tf_op jit(solution)/shard_map/ppermute | solution.py:146
  (10 other events, 222.7 us)
Sparse Core Ops, SparseCore 0:
  20.3 58.2 all-gather.1

commit v2 on v1

--- a/solution.py
+++ b/solution.py
@@ -15,6 +15,8 @@
 GROUP = 64
 CHUNK = 48
 UNROLL = 8
+PART = 32
+PAD = 8
 VMEM_LIMIT = 48 * 1024 * 1024
 ALL = ("x", "z", "y", "c")
 
@@ -45,13 +47,15 @@
     lax.fori_loop(0, acc_ref.shape[0], zero, 0)
 
 
-def forward_kernel(rows, cols, count, tiles, feats, cot_t, out, grad, acc):
+def forward_kernel(
+    rows, cols, info, tiles, feats, cot_t, cot_sum, out, grad, acc, total
+):
     @pl.when(pl.program_id(0) == 0)
     def _():
         clear(acc)
 
     tile_steps(
-        count,
+        info,
         lambda slot: rows[slot],
         lambda t, slot: jnp.dot(tiles[t], feats[cols[slot]], preferred_element_type=F32),
         acc,
@@ -60,15 +64,20 @@
 
     @pl.when(pl.program_id(0) == pl.num_programs(0) - 1)
     def _():
-        grad[...] = jnp.zeros(grad.shape, F32)
+        total[...] = jnp.zeros(total.shape, F32)
 
         def finish(i, carry):
             block = acc[i].astype(BF16)
             out[i] = block
-            grad[...] += jnp.dot(cot_t[i], block, preferred_element_type=F32)
+            total[...] += jnp.dot(cot_t[i], block, preferred_element_type=F32)
             return carry
 
         lax.fori_loop(0, BAND, finish, 0)
+        total[...] = total[...].T
+        for q in range(NC * NY):
+            to_c, to_y = (q // NY) ^ info[1], (q - info[2]) & 3
+            grad[to_c, to_y, :PART] = total[q * PART : (q + 1) * PART]
+            grad[to_c, to_y, PART:] = jnp.broadcast_to(cot_sum[...], (PAD, H))
 
 
 def backward_kernel(rows, cols, count, tiles, cot_t, out, acc):
@@ -101,26 +110,30 @@
     return pl.BlockSpec((CHUNK, TILE, TILE), lambda s, *_: (s, 0, 0))
 
 
-def forward_tiles(rows, cols, count, tiles, feats, cot_t):
+def forward_tiles(rows, cols, info, tiles, feats, cot_t, cot_sum):
+    operands = (feats, cot_t, cot_sum)
     return pl.pallas_call(
         forward_kernel,
         grid_spec=pltpu.PrefetchScalarGridSpec(
             num_scalar_prefetch=3,
             grid=(TCAP // CHUNK,),
-            in_specs=[tile_block(), whole((GROUP, TILE, H)), whole((BAND, H, TILE))],
-            out_specs=[whole((BAND, TILE, H)), whole((H, H))],
-            scratch_shapes=[pltpu.VMEM((BAND + 1, TILE, H), F32)],
+            in_specs=[tile_block()] + [whole(operand.shape) for operand in operands],
+            out_specs=[whole((BAND, TILE, H)), whole((NC, NY, PART + PAD, H))],
+            scratch_shapes=[
+                pltpu.VMEM((BAND + 1, TILE, H), F32),
+                pltpu.VMEM((H, H), F32),
+            ],
         ),
         out_shape=[
             jax.ShapeDtypeStruct((BAND, TILE, H), BF16),
-            jax.ShapeDtypeStruct((H, H), F32),
+            jax.ShapeDtypeStruct((NC, NY, PART + PAD, H), F32),
         ],
         compiler_params=pltpu.CompilerParams(vmem_limit_bytes=VMEM_LIMIT),
         cost_estimate=pl.CostEstimate(
             flops=TCAP * 2 * TILE * TILE * H, bytes_accessed=12 << 20, transcendentals=0
         ),
         name="forward_tiles",
-    )(rows, cols, count, tiles, feats, cot_t)
+    )(rows, cols, info, tiles, *operands)
 
 
 def backward_tiles(rows, cols, count, tiles, cot_t):
@@ -167,25 +180,27 @@
 ):
     x, y, c = lax.axis_index("x"), lax.axis_index("y"), lax.axis_index("c")
     rows, cols, tiles = tile_rows[0], tile_cols[0], tile_values[0]
+    info = jnp.stack([tile_count[0], c, y])
     inv_root = lax.rsqrt(degree.astype(F32))
-    scaled = (features.astype(F32) * inv_root[:, None]).astype(BF16)
+    scaled = (features.astype(F32) * inv_root[:, None]).astype(BF16).reshape(2, TILE, H)
     cot = cotangent.astype(F32)
     cot_t = (cot * inv_root[:, None]).astype(BF16).reshape(2, TILE, H).transpose(0, 2, 1)
+    cot_sum = jnp.sum(cot, axis=0, keepdims=True)
 
     row_dev = rows >> 1
     row_at = ((((row_dev & 1) ^ c) * 4 + (((row_dev >> 1) - y) & 3)) << 1) | (rows & 1)
     col_dev = cols >> 1
-    col_x, col_z = (((col_dev >> 3) - x) & 3), col_dev & 7
-    fwd_col = ((col_z * 4 + col_x) << 1) | (cols & 1)
-    bwd_col = ((col_x * 8 + col_z) << 1) | (cols & 1)
+    col_x, col_z = ((col_dev >> 3) - x) & 3, col_dev & 7
+    fwd_col = (((col_z << 2) | col_x) << 1) | (cols & 1)
+    bwd_col = (((col_x << 3) | col_z) << 1) | (cols & 1)
 
     near = jnp.concatenate(gather4(scaled, "x"))
-    feats = lax.all_gather(near, "z", axis=0, tiled=True).reshape(GROUP, TILE, H)
+    feats = lax.all_gather(near, "z", axis=0, tiled=True)
 
     cot_y = jnp.concatenate(gather4(cot_t, "y"))
     cot_band = jnp.concatenate([cot_y, swap(cot_y)])
 
-    col_terms = backward_tiles(row_at, bwd_col, tile_count, tiles, cot_band)
+    col_terms = backward_tiles(row_at, bwd_col, info, tiles, cot_band)
     col_terms = col_terms.reshape(NX, NZ, 2, H, TILE)
 
     def add(a, b):
@@ -198,49 +213,50 @@
     right3 = shift(add(col_terms[1, :4], right1), "x", NX, 1)
     left3 = shift(add(col_terms[3, 4:], left1), "x", NX, -1)
 
-    band_terms, grad_t = forward_tiles(row_at, fwd_col, tile_count, tiles, feats, cot_band)
+    band_terms, part = forward_tiles(
+        row_at, fwd_col, info, tiles, feats, cot_band, cot_sum
+    )
     band_terms = band_terms.reshape(NC, NY, 2 * TILE, H)
-    half = band_terms[0].astype(F32) + swap(band_terms[1]).astype(F32)
-    half16 = half.astype(BF16)
-    total = half[0]
-    for part in scatter4(half16, "y"):
-        total = total + part.astype(F32)
-    aggregated = (total * inv_root[:, None]).astype(BF16)
-    layer_out = (jnp.dot(aggregated, weight, preferred_element_type=F32) + bias).astype(BF16)
-
-    cot_sum = jnp.sum(cot, axis=0)
-    extra = jnp.zeros((8, 8, H), F32).at[:, 0].set(
-        jnp.where(jnp.arange(8)[:, None] == 0, cot_sum[None, :], 0.0)
-    )
-    chunks = jnp.concatenate([grad_t.reshape(8, 32, H), extra], axis=1).reshape(NY, NC, 40, H)
-    keep = lax.dynamic_index_in_dim(chunks, c, 1, keepdims=False)
-    give = lax.dynamic_index_in_dim(chunks, 1 - c, 1, keepdims=False)
-    keep = keep + swap(give)
-    keep = [lax.dynamic_index_in_dim(keep, (y + o) & 3, 0, keepdims=False) for o in range(4)]
-    part = keep[0]
-    for other in scatter4(keep, "y"):
-        part = part + other
-    near_parts = gather4(part, "x")
-    part = (near_parts[0] + near_parts[2]) + (near_parts[1] + near_parts[3])
-    part = jnp.sum(
-        lax.all_to_all(jnp.broadcast_to(part, (NZ, 40, H)), "z", 0, 0, tiled=True), axis=0
-    )
-    by_y = jnp.stack(gather4(part, "y"))
-    by_y = jnp.take(by_y, (jnp.arange(4) - y) & 3, axis=0)
-    by_c = lax.all_gather(by_y, "c", axis=1)
-    grad_weight = by_c[:, :, :32].reshape(H, H).T
-    grad_bias = by_c[0, 0, 32]
+    give = swap(part[1])
+    band_terms, give, right2, left2, right3, left3 = lax.optimization_barrier(
+        (band_terms, give, right2, left2, right3, left3)
+    )
 
     own_x = jnp.concatenate(
         [
             col_terms[0, :4].astype(F32) + right3.astype(F32) + left2.astype(F32),
             col_terms[0, 4:].astype(F32) + right2.astype(F32) + left3.astype(F32),
         ]
-    ).astype(BF16)
-    parts = lax.all_to_all(own_x, "z", 0, 0, tiled=True)
-    own = jnp.sum(parts.astype(F32), axis=0)
+    )
+    own_z = lax.psum_scatter(
+        own_x.reshape(NZ * 2 * H, TILE), "z", scatter_dimension=0, tiled=True
+    ).reshape(2, H, TILE)
+
+    part = part[0] + give
+    own, up, across, down = [part[0]] + scatter4(part, "y")
+    part = (own + across) + (up + down)
+    own, up, across, down = gather4(part, "x")
+    part = (own + across) + (up + down)
+    half = band_terms[0].astype(F32) + swap(band_terms[1]).astype(F32)
+    part, half = lax.optimization_barrier((part, half))
+    part = lax.all_to_all(
+        jnp.broadcast_to(part, (NZ, PART + PAD, H)), "z", 0, 0, tiled=True
+    )
+    part = jnp.sum(part, axis=0)
+    grad_bias = part[PART]
+    by_y = jnp.concatenate(gather4(part[:PART], "y"))
+    by_y = lax.dynamic_slice_in_dim(jnp.concatenate([by_y, by_y]), (-y & 3) * PART, NY * PART)
+    grad_weight = lax.all_gather(by_y, "c", axis=0, tiled=True)
+
+    half16 = half.astype(BF16)
+    total = half[0]
+    for other in scatter4(half16, "y"):
+        total = total + other.astype(F32)
+    aggregated = (total * inv_root[:, None]).astype(BF16)
+    layer_out = (jnp.dot(aggregated, weight, preferred_element_type=F32) + bias).astype(BF16)
+
     grad_features = jnp.einsum(
-        "ahn,gh->ang", own, weight.astype(F32), precision=lax.Precision.HIGHEST
+        "ahn,gh->ang", own_z, weight.astype(F32), precision=lax.Precision.HIGHEST
     ).reshape(2 * TILE, H)
     grad_features = (grad_features * inv_root[:, None]).astype(BF16)
     return (layer_out, grad_weight, grad_bias, grad_features)

time: 168 us -> 158 us (0.940)
  starting transfers between devices: 53.1 us -> 41.5 us
  Pallas kernels: 19.6 us -> 21.8 us
    ppermute x24, waiting for transfers between devices: 51 us -> 27.6 us  [shift(): lax.ppermute(value, axis, [(i, (i + by) % size) for i in range(size)])]
    all_gather x1, waiting for transfers between devices: 0.01 us -> 13.9 us  [shards(): feats = lax.all_gather(near, 'z', axis=0, tiled=True)]
    all_to_all x2 -> x1, waiting for transfers between devices: 5.13 us -> 12.2 us  [shards(): lax.all_to_all(jnp.broadcast_to(part, (NZ, PART + PAD, H)), 'z', 0, 0, ti...]
    all_to_all x2 -> x1, starting transfers between devices: 10.6 us -> 4.99 us  [shards(): lax.all_to_all(jnp.broadcast_to(part, (NZ, PART + PAD, H)), 'z', 0, 0, ti...]
    ppermute x24, starting transfers between devices: 37.1 us -> 33.3 us  [shift(): lax.ppermute(value, axis, [(i, (i + by) % size) for i in range(size)])]
    ppermute x3, starting transfers between devices: 5.33 us -> 3.21 us  [swap(): return lax.ppermute(value, 'c', [(0, 1), (1, 0)])]
  transfers between devices with their start and end apart: 30 -> 30, of which waited for: 14 -> 11; matrix products, arithmetic and copies ran while one was open for 7% -> 4% of each run, Pallas kernels for 12% -> 14%
where the time goes in v2:
time: 158 us; the launch traced here: 157 us
  waiting for transfers between devices  55.8 us (35%)
  starting transfers between devices  41.5 us (26%)
  Pallas kernels  21.8 us (14%)
  between operations  15 us (9%)
  other arithmetic  9.3 us (6%)
  blocking collectives  6.88 us (4%)
  local copies, waits for them, and re-layouts  4.89 us (3%)
  matrix products  1.89 us (1%)
    ppermute x24, starting transfers between devices, shift(): lax.ppermute(value, axis, [(i, (i + by) % size) for i in range(size)])  33.3 us
    ppermute x24, waiting for transfers between devices, shift(): lax.ppermute(value, axis, [(i, (i + by) % size) for i in range(size)])  27.6 us
    all_gather x1, waiting for transfers between devices, shards(): feats = lax.all_gather(near, 'z', axis=0, tiled=True)  13.9 us
    pallas_call x1, Pallas kernels, forward_tiles(): pl.pallas_call(forward_kernel, grid_spec=pltpu.PrefetchScalarGridSpec(num...  12.5 us
    all_to_all x1, waiting for transfers between devices, shards(): lax.all_to_all(jnp.broadcast_to(part, (NZ, PART + PAD, H)), 'z', 0, 0, ti...  12.2 us
    pallas_call x1, Pallas kernels, backward_tiles(): pl.pallas_call(backward_kernel, grid_spec=pltpu.PrefetchScalarGridSpec(nu...  9.22 us
    all_gather x1, blocking collectives, shards(): grad_weight = lax.all_gather(by_y, 'c', axis=0, tiled=True)  6.88 us
    all_to_all x1, starting transfers between devices, shards(): lax.all_to_all(jnp.broadcast_to(part, (NZ, PART + PAD, H)), 'z', 0, 0, ti...  4.99 us
  transfers between devices with their start and end apart: 30, of which 11 were waited for; matrix products, arithmetic and copies ran while one was open for 4% of the time, Pallas kernels for 14%

profile of v2, /device:TPU:1, one launch (start us, length us, event | category | flops | bytes accessed | tf_op | source)
XLA Modules:
  0.0 157.1 jit_solution(10572424368787087647)
XLA Ops:
  9.0 2.1 %collective-permute-start.2 = (bf16[2,128,256]{2,1,0:T(8,128)(2,1)S(1)}, bf16[2,128,256]{2,1,0:T(8,128)(2,1)S(1)}, u32[]{:S(2)}, u32[]{:S(2)}) collective-permute-start(bf16[2,128,256]{2,1,0:T(8,128)(2,1)S(1)} %bitcast.106), channel_id=1, source_target_pairs={{0,64},{64,128},{128,192},{192,0},{1,65},{65,129},{129,193},{193,1... | collective-permute-start | bytes 393224 | tf_op jit(solution)/shard_map/ppermute | solution.py:159
  11.1 2.5 %collective-permute-start.1 = (bf16[2,128,256]{2,1,0:T(8,128)(2,1)S(1)}, bf16[2,128,256]{2,1,0:T(8,128)(2,1)S(1)}, u32[]{:S(2)}, u32[]{:S(2)}) collective-permute-start(bf16[2,128,256]{2,1,0:T(8,128)(2,1)S(1)} %bitcast.107), channel_id=1, source_target_pairs={{0,128},{64,192},{128,0},{192,64},{1,129},{65,193},{129,1},{193,65... | collective-permute-start | bytes 393224 | tf_op jit(solution)/shard_map/ppermute | solution.py:159
  14.8 4.5 %collective-permute-done.1 = bf16[2,128,256]{2,1,0:T(8,128)(2,1)S(1)} collective-permute-done((bf16[2,128,256]{2,1,0:T(8,128)(2,1)S(1)}, bf16[2,128,256]{2,1,0:T(8,128)(2,1)S(1)}, u32[]{:S(2)}, u32[]{:S(2)}) %collective-permute-start.1) | collective-permute-done | bytes 131104 | tf_op jit(solution)/shard_map/ppermute | solution.py:159
  20.4 2.8 %collective-permute-start.3 = (bf16[2,256,128]{2,1,0:T(8,128)(2,1)S(1)}, bf16[2,256,128]{2,1,0:T(8,128)(2,1)S(1)}, u32[]{:S(2)}, u32[]{:S(2)}) collective-permute-start(bf16[2,256,128]{2,1,0:T(8,128)(2,1)S(1)} %bitcast.100), channel_id=1, source_target_pairs={{0,6},{2,0},{4,2},{6,4},{1,7},{3,1},{5,3},{7,5},{8,14},{10,8},{12,... | collective-permute-start | bytes 393224 | tf_op jit(solution)/shard_map/ppermute | solution.py:159
  25.7 2.9 %collective-permute-done.4 = bf16[2,256,128]{2,1,0:T(8,128)(2,1)S(1)} collective-permute-done((bf16[2,256,128]{2,1,0:T(8,128)(2,1)S(1)}, bf16[2,256,128]{2,1,0:T(8,128)(2,1)S(1)}, u32[]{:S(2)}, u32[]{:S(2)}) %collective-permute-start.4) | collective-permute-done | bytes 131104 | tf_op jit(solution)/shard_map/ppermute | solution.py:159
  28.6 3.2 %collective-permute-done.5 = bf16[2,256,128]{2,1,0:T(8,128)(2,1)S(1)} collective-permute-done((bf16[2,256,128]{2,1,0:T(8,128)(2,1)S(1)}, bf16[2,256,128]{2,1,0:T(8,128)(2,1)S(1)}, u32[]{:S(2)}, u32[]{:S(2)}) %collective-permute-start.5) | collective-permute-done | bytes 131104 | tf_op jit(solution)/shard_map/ppermute | solution.py:159
  31.9 1.6 %collective-permute-start.6 = (bf16[8,256,128]{2,1,0:T(8,128)(2,1)S(1)}, bf16[8,256,128]{2,1,0:T(8,128)(2,1)S(1)}, u32[]{:S(2)}, u32[]{:S(2)}) collective-permute-start(bf16[8,256,128]{2,1,0:T(8,128)(2,1)S(1)} %pad_maximum_fusion.2), channel_id=1, source_target_pairs={{0,1},{1,0},{2,3},{3,2},{4,5},{5,4},{6,7},{7,6},{8,9},{9,8},{10,11... | collective-permute-start | bytes 1572872 | tf_op jit(solution)/shard_map/ppermute | solution.py:175
  35.2 9.2 %backward_tiles.1 = bf16[64,256,128]{2,1,0:T(8,128)(2,1)S(1)} custom-call(s32[192]{0:T(256)S(1)} %bitcast.94, s32[192]{0:T(256)S(1)} %get-tuple-element.42.cols, s32[3]{0:T(128)S(1)} %pad_add_fusion.info.count, bf16[192,128,128]{2,1,0:T(8,128)(2,1)} %bitcast.97, bf16[16,256,128]{2,1,0:T(8,128)(2,1)S(1)} %constant_dynamic-update-slice_fusion.cot_t), custom_call_target="tpu_custom_call" | custom-call | flops 1610612736 | bytes 12582912 | tf_op jit(solution)/shard_map/backward_tiles/pallas_call | solution.py:140
  50.8 9.9 %collective-permute-done.12 = bf16[4,2,256,128]{3,2,1,0:T(8,128)(2,1)S(1)} collective-permute-done((bf16[4,2,256,128]{3,2,1,0:T(8,128)(2,1)S(1)}, bf16[4,2,256,128]{3,2,1,0:T(8,128)(2,1)S(1)}, u32[]{:S(2)}, u32[]{:S(2)}) %collective-permute-start.12) | collective-permute-done | bytes 524320 | tf_op jit(solution)/shard_map/ppermute | solution.py:159
  62.1 1.5 collective-permute-start.11
  64.7 13.9 %all-gather.2.cloned.1.call-done.feats = bf16[64,128,256]{2,1,0:T(8,128)(2,1)} async-done(((bf16[8,128,256]{2,1,0:T(8,128)(2,1)}), bf16[64,128,256]{2,1,0:T(8,128)(2,1)}) %all-gather.2.cloned.1.call-update) | async-done | bytes 4194320 | tf_op jit(solution)/shard_map/all_gather | solution.py:198
  78.6 12.5 %forward_tiles.1 = (bf16[16,128,256]{2,1,0:T(8,128)(2,1)S(1)}, f32[2,4,40,256]{3,2,1,0:T(8,128)S(1)}) custom-call(s32[192]{0:T(256)S(1)} %bitcast.95, s32[192]{0:T(256)S(1)} %get-tuple-element.43.cols, s32[3]{0:T(128)S(1)} %pad_add_fusion.info.count, bf16[192,128,128]{2,1,0:T(8,128)(2,1)} %bitcast.98, ...), custom_call_target="tpu_custom_call" | custom-call | flops 1610612736 | bytes 12582912 | tf_op jit(solution)/shard_map/forward_tiles/pallas_call | solution.py:115
  92.9 2.1 %fusion.3 = (f32[4,2,256,128]{3,2,1,0:T(8,128)S(1)}, f32[4,2,256,128]{3,2,1,0:T(8,128)S(1)}) fusion(bf16[4,2,256,128]{3,2,1,0:T(8,128)(2,1)} %collective-permute-done.9, bf16[4,2,256,128]{3,2,1,0:T(8,128)(2,1)} %collective-permute-done.11, bf16[4,8,2,256,128]{4,3,2,1,0:T(8,128)(2,1)} %bitcast.91, bf16[4,2,256,128]{3,2,1,0:T(8,128)(2,1)} %collective-permute-done.13, ...), kind=kLoop, calls=%fused_computation.8 | loop fusion | flops 2621440 | bytes 5242880 | tf_op jit(solution)/shard_map/add | solution.py:227
  94.9 1.5 pad_maximum_fusion
  96.5 1.8 %collective-permute-start.14 = (f32[40,256]{1,0:T(8,128)S(1)}, f32[40,256]{1,0:T(8,128)S(1)}, u32[]{:S(2)}, u32[]{:S(2)}) collective-permute-start(f32[40,256]{1,0:T(8,128)S(1)} %get-tuple-element.37), channel_id=1, source_target_pairs={{0,6},{2,0},{4,2},{6,4},{1,7},{3,1},{5,3},{7,5},{8,14},{10,8},{12,... | collective-permute-start | bytes 122888 | tf_op jit(solution)/shard_map/ppermute | solution.py:159
  98.3 3.7 %collective-permute-start.16 = (f32[40,256]{1,0:T(8,128)S(1)}, f32[40,256]{1,0:T(8,128)S(1)}, u32[]{:S(2)}, u32[]{:S(2)}) collective-permute-start(f32[40,256]{1,0:T(8,128)S(1)} %get-tuple-element.35), channel_id=1, source_target_pairs={{0,4},{2,6},{4,0},{6,2},{1,5},{3,7},{5,1},{7,3},{8,12},{10,14},{12... | collective-permute-start | bytes 122888 | tf_op jit(solution)/shard_map/ppermute | solution.py:159
  103.9 2.7 %collective-permute-start.18 = (f32[40,256]{1,0:T(8,128)S(1)}, f32[40,256]{1,0:T(8,128)S(1)}, u32[]{:S(2)}, u32[]{:S(2)}) collective-permute-start(f32[40,256]{1,0:T(8,128)S(1)} %fusion.14), channel_id=1, source_target_pairs={{0,192},{64,0},{128,64},{192,128},{1,193},{65,1},{129,65},{193,129... | collective-permute-start | bytes 122888 | tf_op jit(solution)/shard_map/ppermute | solution.py:159
  107.9 3.2 %collective-permute-done.19 = f32[40,256]{1,0:T(8,128)S(1)} collective-permute-done((f32[40,256]{1,0:T(8,128)S(1)}, f32[40,256]{1,0:T(8,128)S(1)}, u32[]{:S(2)}, u32[]{:S(2)}) %collective-permute-start.19) | collective-permute-done | bytes 40992 | tf_op jit(solution)/shard_map/ppermute | solution.py:159
  112.0 5.0 %all-to-all-start = ((f32[8,40,256]{2,1,0:T(8,128)}), f32[8,40,256]{2,1,0:T(8,128)S(1)}, u32[]{:S(2)}, u32[]{:S(2)}) async-start(f32[8,40,256]{2,1,0:T(8,128)} %broadcast_in_dim.5), calls=%async_computation | async-start | bytes 655360 | tf_op jit(solution)/shard_map/all_to_all | solution.py:242
  118.2 1.7 %collective-permute-start.22 = (bf16[256,256]{1,0:T(8,128)(2,1)S(1)}, bf16[256,256]{1,0:T(8,128)(2,1)S(1)}, u32[]{:S(2)}, u32[]{:S(2)}) collective-permute-start(bf16[256,256]{1,0:T(8,128)(2,1)S(1)} %get-tuple-element.34), channel_id=1, source_target_pairs={{0,6},{2,0},{4,2},{6,4},{1,7},{3,1},{5,3},{7,5},{8,14},{10,8},{12,... | collective-permute-start | bytes 393224 | tf_op jit(solution)/shard_map/ppermute | solution.py:159
  120.3 12.2 %all-to-all-done = f32[8,40,256]{2,1,0:T(8,128)S(1)} async-done(((f32[8,40,256]{2,1,0:T(8,128)}), f32[8,40,256]{2,1,0:T(8,128)S(1)}, u32[]{:S(2)}, u32[]{:S(2)}) %all-to-all-start) | async-done | bytes 327712 | tf_op jit(solution)/shard_map/all_to_all | solution.py:242
  132.6 2.6 %collective-permute-start.24 = (f32[32,256]{1,0:T(8,128)S(1)}, f32[32,256]{1,0:T(8,128)S(1)}, u32[]{:S(2)}, u32[]{:S(2)}) collective-permute-start(f32[32,256]{1,0:T(8,128)S(1)} %get-tuple-element.40), channel_id=1, source_target_pairs={{0,6},{2,0},{4,2},{6,4},{1,7},{3,1},{5,3},{7,5},{8,14},{10,8},{12,... | collective-permute-start | bytes 98312 | tf_op jit(solution)/shard_map/ppermute | solution.py:159
  137.3 3.1 %collective-permute-done.25 = f32[32,256]{1,0:T(8,128)S(1)} collective-permute-done((f32[32,256]{1,0:T(8,128)S(1)}, f32[32,256]{1,0:T(8,128)S(1)}, u32[]{:S(2)}, u32[]{:S(2)}) %collective-permute-start.25) | collective-permute-done | bytes 32800 | tf_op jit(solution)/shard_map/ppermute | solution.py:159
  140.6 6.9 %all_gather.7 = f32[256,256]{1,0:T(8,128)S(1)} all-gather(f32[128,256]{1,0:T(8,128)S(1)} %constant_dynamic-slice_fusion), channel_id=1, replica_groups=mesh['x'=4,'z'=8,'y'=4,'c'=2] {'c'}, dimensions={0}, use_global_device_ids=true | all-gather | bytes 393216 | tf_op jit(solution)/shard_map/all_gather | solution.py:249
  (90 shorter events, 28.8 us)
Async XLA Ops:
  7.2 71.5 %all-gather.2.cloned.1.call-start = ((), (), s32[]{:S(2)}) async-start(), calls=%async_computation.2 | async-start | bytes 4718592 | tf_op jit(solution)/shard_map/all_gather | solution.py:198
  9.0 5.7 %collective-permute-start.2 = (bf16[2,128,256]{2,1,0:T(8,128)(2,1)S(1)}, bf16[2,128,256]{2,1,0:T(8,128)(2,1)S(1)}, u32[]{:S(2)}, u32[]{:S(2)}) collective-permute-start(bf16[2,128,256]{2,1,0:T(8,128)(2,1)S(1)} %bitcast.106), channel_id=1, source_target_pairs={{0,64},{64,128},{128,192},{192,0},{1,65},{65,129},{129,193},{193,1... | collective-permute-start | bytes 393224 | tf_op jit(solution)/shard_map/ppermute | solution.py:159
  11.1 8.2 %collective-permute-start.1 = (bf16[2,128,256]{2,1,0:T(8,128)(2,1)S(1)}, bf16[2,128,256]{2,1,0:T(8,128)(2,1)S(1)}, u32[]{:S(2)}, u32[]{:S(2)}) collective-permute-start(bf16[2,128,256]{2,1,0:T(8,128)(2,1)S(1)} %bitcast.107), channel_id=1, source_target_pairs={{0,128},{64,192},{128,0},{192,64},{1,129},{65,193},{129,1},{193,65... | collective-permute-start | bytes 393224 | tf_op jit(solution)/shard_map/ppermute | solution.py:159
  13.6 5.7 %collective-permute-start = (bf16[2,128,256]{2,1,0:T(8,128)(2,1)S(1)}, bf16[2,128,256]{2,1,0:T(8,128)(2,1)S(1)}, u32[]{:S(2)}, u32[]{:S(2)}) collective-permute-start(bf16[2,128,256]{2,1,0:T(8,128)(2,1)S(1)} %bitcast.108), channel_id=1, source_target_pairs={{0,192},{64,0},{128,64},{192,128},{1,193},{65,1},{129,65},{193,129... | collective-permute-start | bytes 393224 | tf_op jit(solution)/shard_map/ppermute | solution.py:159
  20.2 127.3 %reduce-scatter.2.cloned.1.call-start = ((), (), s32[]{:S(2)}) async-start(), calls=%async_computation.3 | async-start | bytes 2359296 | tf_op jit(solution)/shard_map/reduce_scatter | solution.py:231
  20.4 5.3 %collective-permute-start.3 = (bf16[2,256,128]{2,1,0:T(8,128)(2,1)S(1)}, bf16[2,256,128]{2,1,0:T(8,128)(2,1)S(1)}, u32[]{:S(2)}, u32[]{:S(2)}) collective-permute-start(bf16[2,256,128]{2,1,0:T(8,128)(2,1)S(1)} %bitcast.100), channel_id=1, source_target_pairs={{0,6},{2,0},{4,2},{6,4},{1,7},{3,1},{5,3},{7,5},{8,14},{10,8},{12,... | collective-permute-start | bytes 393224 | tf_op jit(solution)/shard_map/ppermute | solution.py:159
  23.2 5.4 %collective-permute-start.4 = (bf16[2,256,128]{2,1,0:T(8,128)(2,1)S(1)}, bf16[2,256,128]{2,1,0:T(8,128)(2,1)S(1)}, u32[]{:S(2)}, u32[]{:S(2)}) collective-permute-start(bf16[2,256,128]{2,1,0:T(8,128)(2,1)S(1)} %bitcast.101), channel_id=1, source_target_pairs={{0,4},{2,6},{4,0},{6,2},{1,5},{3,7},{5,1},{7,3},{8,12},{10,14},{12... | collective-permute-start | bytes 393224 | tf_op jit(solution)/shard_map/ppermute | solution.py:159
  23.5 8.3 %collective-permute-start.5 = (bf16[2,256,128]{2,1,0:T(8,128)(2,1)S(1)}, bf16[2,256,128]{2,1,0:T(8,128)(2,1)S(1)}, u32[]{:S(2)}, u32[]{:S(2)}) collective-permute-start(bf16[2,256,128]{2,1,0:T(8,128)(2,1)S(1)} %bitcast.102), channel_id=1, source_target_pairs={{0,2},{2,4},{4,6},{6,0},{1,3},{3,5},{5,7},{7,1},{8,10},{10,12},{12... | collective-permute-start | bytes 393224 | tf_op jit(solution)/shard_map/ppermute | solution.py:159
  45.8 14.9 %collective-permute-start.12 = (bf16[4,2,256,128]{3,2,1,0:T(8,128)(2,1)S(1)}, bf16[4,2,256,128]{3,2,1,0:T(8,128)(2,1)S(1)}, u32[]{:S(2)}, u32[]{:S(2)}) collective-permute-start(bf16[4,2,256,128]{3,2,1,0:T(8,128)(2,1)S(1)} %get-tuple-element.28), channel_id=1, source_target_pairs={{0,192},{64,0},{128,64},{192,128},{1,193},{65,1},{129,65},{193,129... | collective-permute-start | bytes 1572872 | tf_op jit(solution)/shard_map/ppermute | solution.py:159
  46.7 14.0 %collective-permute-start.10 = (bf16[4,2,256,128]{3,2,1,0:T(8,128)(2,1)S(1)}, bf16[4,2,256,128]{3,2,1,0:T(8,128)(2,1)S(1)}, u32[]{:S(2)}, u32[]{:S(2)}) collective-permute-start(bf16[4,2,256,128]{3,2,1,0:T(8,128)(2,1)S(1)} %get-tuple-element.29), channel_id=1, source_target_pairs={{0,64},{64,128},{128,192},{192,0},{1,65},{65,129},{129,193},{193,1... | collective-permute-start | bytes 1572872 | tf_op jit(solution)/shard_map/ppermute | solution.py:159
  48.1 43.3 %collective-permute-start.8 = (bf16[4,2,256,128]{3,2,1,0:T(8,128)(2,1)}, bf16[4,2,256,128]{3,2,1,0:T(8,128)(2,1)S(1)}, u32[]{:S(2)}, u32[]{:S(2)}) collective-permute-start(bf16[4,2,256,128]{3,2,1,0:T(8,128)(2,1)} %get-tuple-element.31), channel_id=1, source_target_pairs={{0,64},{64,128},{128,192},{192,0},{1,65},{65,129},{129,193},{193,1... | collective-permute-start | bytes 1572872 | tf_op jit(solution)/shard_map/ppermute | solution.py:159
  49.6 41.9 %collective-permute-start.9 = (bf16[4,2,256,128]{3,2,1,0:T(8,128)(2,1)}, bf16[4,2,256,128]{3,2,1,0:T(8,128)(2,1)}, u32[]{:S(2)}, u32[]{:S(2)}) collective-permute-start(bf16[4,2,256,128]{3,2,1,0:T(8,128)(2,1)} %get-tuple-element.30), channel_id=1, source_target_pairs={{0,192},{64,0},{128,64},{192,128},{1,193},{65,1},{129,65},{193,129... | collective-permute-start | bytes 1572872 | tf_op jit(solution)/shard_map/ppermute | solution.py:159
  62.1 29.5 %collective-permute-start.11 = (bf16[4,2,256,128]{3,2,1,0:T(8,128)(2,1)}, bf16[4,2,256,128]{3,2,1,0:T(8,128)(2,1)}, u32[]{:S(2)}, u32[]{:S(2)}) collective-permute-start(bf16[4,2,256,128]{3,2,1,0:T(8,128)(2,1)} %get-tuple-element.27), channel_id=1, source_target_pairs={{0,64},{64,128},{128,192},{192,0},{1,65},{65,129},{129,193},{193,1... | collective-permute-start | bytes 1572872 | tf_op jit(solution)/shard_map/ppermute | solution.py:159
  63.6 28.0 %collective-permute-start.13 = (bf16[4,2,256,128]{3,2,1,0:T(8,128)(2,1)}, bf16[4,2,256,128]{3,2,1,0:T(8,128)(2,1)}, u32[]{:S(2)}, u32[]{:S(2)}) collective-permute-start(bf16[4,2,256,128]{3,2,1,0:T(8,128)(2,1)} %get-tuple-element.26), channel_id=1, source_target_pairs={{0,192},{64,0},{128,64},{192,128},{1,193},{65,1},{129,65},{193,129... | collective-permute-start | bytes 1572872 | tf_op jit(solution)/shard_map/ppermute | solution.py:159
  96.5 6.8 %collective-permute-start.14 = (f32[40,256]{1,0:T(8,128)S(1)}, f32[40,256]{1,0:T(8,128)S(1)}, u32[]{:S(2)}, u32[]{:S(2)}) collective-permute-start(f32[40,256]{1,0:T(8,128)S(1)} %get-tuple-element.37), channel_id=1, source_target_pairs={{0,6},{2,0},{4,2},{6,4},{1,7},{3,1},{5,3},{7,5},{8,14},{10,8},{12,... | collective-permute-start | bytes 122888 | tf_op jit(solution)/shard_map/ppermute | solution.py:159
  98.3 5.1 %collective-permute-start.15 = (f32[40,256]{1,0:T(8,128)S(1)}, f32[40,256]{1,0:T(8,128)S(1)}, u32[]{:S(2)}, u32[]{:S(2)}) collective-permute-start(f32[40,256]{1,0:T(8,128)S(1)} %get-tuple-element.36), channel_id=1, source_target_pairs={{0,2},{2,4},{4,6},{6,0},{1,3},{3,5},{5,7},{7,1},{8,10},{10,12},{12... | collective-permute-start | bytes 122888 | tf_op jit(solution)/shard_map/ppermute | solution.py:159
  98.3 5.6 %collective-permute-start.16 = (f32[40,256]{1,0:T(8,128)S(1)}, f32[40,256]{1,0:T(8,128)S(1)}, u32[]{:S(2)}, u32[]{:S(2)}) collective-permute-start(f32[40,256]{1,0:T(8,128)S(1)} %get-tuple-element.35), channel_id=1, source_target_pairs={{0,4},{2,6},{4,0},{6,2},{1,5},{3,7},{5,1},{7,3},{8,12},{10,14},{12... | collective-permute-start | bytes 122888 | tf_op jit(solution)/shard_map/ppermute | solution.py:159
  102.1 9.1 %collective-permute-start.20 = (bf16[4,256,256]{2,1,0:T(8,128)(2,1)S(1)}, bf16[4,256,256]{2,1,0:T(8,128)(2,1)S(1)}, u32[]{:S(2)}, u32[]{:S(2)}) collective-permute-start(bf16[4,256,256]{2,1,0:T(8,128)(2,1)S(1)} %slice_bitcast_fusion.8), channel_id=1, source_target_pairs={{0,1},{1,0},{2,3},{3,2},{4,5},{5,4},{6,7},{7,6},{8,9},{9,8},{10,11... | collective-permute-start | bytes 1572872 | tf_op jit(solution)/shard_map/ppermute | solution.py:175
  106.6 4.5 %collective-permute-start.19 = (f32[40,256]{1,0:T(8,128)S(1)}, f32[40,256]{1,0:T(8,128)S(1)}, u32[]{:S(2)}, u32[]{:S(2)}) collective-permute-start(f32[40,256]{1,0:T(8,128)S(1)} %fusion.14), channel_id=1, source_target_pairs={{0,64},{64,128},{128,192},{192,0},{1,65},{65,129},{129,193},{193,1... | collective-permute-start | bytes 122888 | tf_op jit(solution)/shard_map/ppermute | solution.py:159
  112.0 20.5 %all-to-all-start = ((f32[8,40,256]{2,1,0:T(8,128)}), f32[8,40,256]{2,1,0:T(8,128)S(1)}, u32[]{:S(2)}, u32[]{:S(2)}) async-start(f32[8,40,256]{2,1,0:T(8,128)} %broadcast_in_dim.5), calls=%async_computation | async-start | bytes 655360 | tf_op jit(solution)/shard_map/all_to_all | solution.py:242
  117.1 18.1 %collective-permute-start.23 = (bf16[256,256]{1,0:T(8,128)(2,1)S(1)}, bf16[256,256]{1,0:T(8,128)(2,1)S(1)}, u32[]{:S(2)}, u32[]{:S(2)}) collective-permute-start(bf16[256,256]{1,0:T(8,128)(2,1)S(1)} %get-tuple-element.33), channel_id=1, source_target_pairs={{0,4},{2,6},{4,0},{6,2},{1,5},{3,7},{5,1},{7,3},{8,12},{10,14},{12... | collective-permute-start | bytes 393224 | tf_op jit(solution)/shard_map/ppermute | solution.py:159
  118.2 17.1 %collective-permute-start.22 = (bf16[256,256]{1,0:T(8,128)(2,1)S(1)}, bf16[256,256]{1,0:T(8,128)(2,1)S(1)}, u32[]{:S(2)}, u32[]{:S(2)}) collective-permute-start(bf16[256,256]{1,0:T(8,128)(2,1)S(1)} %get-tuple-element.34), channel_id=1, source_target_pairs={{0,6},{2,0},{4,2},{6,4},{1,7},{3,1},{5,3},{7,5},{8,14},{10,8},{12,... | collective-permute-start | bytes 393224 | tf_op jit(solution)/shard_map/ppermute | solution.py:159
  119.9 15.4 %collective-permute-start.21 = (bf16[256,256]{1,0:T(8,128)(2,1)S(1)}, bf16[256,256]{1,0:T(8,128)(2,1)S(1)}, u32[]{:S(2)}, u32[]{:S(2)}) collective-permute-start(bf16[256,256]{1,0:T(8,128)(2,1)S(1)} %get-tuple-element.32), channel_id=1, source_target_pairs={{0,2},{2,4},{4,6},{6,0},{1,3},{3,5},{5,7},{7,1},{8,10},{10,12},{12... | collective-permute-start | bytes 393224 | tf_op jit(solution)/shard_map/ppermute | solution.py:159
  132.6 4.7 %collective-permute-start.24 = (f32[32,256]{1,0:T(8,128)S(1)}, f32[32,256]{1,0:T(8,128)S(1)}, u32[]{:S(2)}, u32[]{:S(2)}) collective-permute-start(f32[32,256]{1,0:T(8,128)S(1)} %get-tuple-element.40), channel_id=1, source_target_pairs={{0,6},{2,0},{4,2},{6,4},{1,7},{3,1},{5,3},{7,5},{8,14},{10,8},{12,... | collective-permute-start | bytes 98312 | tf_op jit(solution)/shard_map/ppermute | solution.py:159
  (9 other events, 205.2 us)
Sparse Core Ops, SparseCore 0:
  20.3 58.2 all-gather.1
  96.6 42.8 reduce-scatter.1

commit v3 on v2

--- a/solution.py
+++ b/solution.py
@@ -14,9 +14,8 @@
 BAND = 16
 GROUP = 64
 CHUNK = 48
-UNROLL = 8
-PART = 32
-PAD = 8
+UNROLL = 16
+PAD = 16
 VMEM_LIMIT = 48 * 1024 * 1024
 ALL = ("x", "z", "y", "c")
 
@@ -74,10 +73,10 @@
 
         lax.fori_loop(0, BAND, finish, 0)
         total[...] = total[...].T
-        for q in range(NC * NY):
-            to_c, to_y = (q // NY) ^ info[1], (q - info[2]) & 3
-            grad[to_c, to_y, :PART] = total[q * PART : (q + 1) * PART]
-            grad[to_c, to_y, PART:] = jnp.broadcast_to(cot_sum[...], (PAD, H))
+        for q in range(NC):
+            to = q ^ info[1]
+            grad[to, :TILE] = total[q * TILE : (q + 1) * TILE]
+            grad[to, TILE:] = jnp.broadcast_to(cot_sum[...], (PAD, H))
 
 
 def backward_kernel(rows, cols, count, tiles, cot_t, out, acc):
@@ -118,7 +117,7 @@
             num_scalar_prefetch=3,
             grid=(TCAP // CHUNK,),
             in_specs=[tile_block()] + [whole(operand.shape) for operand in operands],
-            out_specs=[whole((BAND, TILE, H)), whole((NC, NY, PART + PAD, H))],
+            out_specs=[whole((BAND, TILE, H)), whole((NC, TILE + PAD, H))],
             scratch_shapes=[
                 pltpu.VMEM((BAND + 1, TILE, H), F32),
                 pltpu.VMEM((H, H), F32),
@@ -126,7 +125,7 @@
         ),
         out_shape=[
             jax.ShapeDtypeStruct((BAND, TILE, H), BF16),
-            jax.ShapeDtypeStruct((NC, NY, PART + PAD, H), F32),
+            jax.ShapeDtypeStruct((NC, TILE + PAD, H), F32),
         ],
         compiler_params=pltpu.CompilerParams(vmem_limit_bytes=VMEM_LIMIT),
         cost_estimate=pl.CostEstimate(
@@ -180,7 +179,7 @@
 ):
     x, y, c = lax.axis_index("x"), lax.axis_index("y"), lax.axis_index("c")
     rows, cols, tiles = tile_rows[0], tile_cols[0], tile_values[0]
-    info = jnp.stack([tile_count[0], c, y])
+    info = jnp.stack([tile_count[0], c])
     inv_root = lax.rsqrt(degree.astype(F32))
     scaled = (features.astype(F32) * inv_root[:, None]).astype(BF16).reshape(2, TILE, H)
     cot = cotangent.astype(F32)
@@ -195,9 +194,10 @@
     bwd_col = (((col_x << 3) | col_z) << 1) | (cols & 1)
 
     near = jnp.concatenate(gather4(scaled, "x"))
+    cot_y = jnp.concatenate(gather4(cot_t, "y"))
+    near, cot_y = lax.optimization_barrier((near, cot_y))
     feats = lax.all_gather(near, "z", axis=0, tiled=True)
 
-    cot_y = jnp.concatenate(gather4(cot_t, "y"))
     cot_band = jnp.concatenate([cot_y, swap(cot_y)])
 
     col_terms = backward_tiles(row_at, bwd_col, info, tiles, cot_band)
@@ -213,40 +213,36 @@
     right3 = shift(add(col_terms[1, :4], right1), "x", NX, 1)
     left3 = shift(add(col_terms[3, 4:], left1), "x", NX, -1)
 
-    band_terms, part = forward_tiles(
-        row_at, fwd_col, info, tiles, feats, cot_band, cot_sum
-    )
-    band_terms = band_terms.reshape(NC, NY, 2 * TILE, H)
-    give = swap(part[1])
-    band_terms, give, right2, left2, right3, left3 = lax.optimization_barrier(
-        (band_terms, give, right2, left2, right3, left3)
-    )
-
     own_x = jnp.concatenate(
         [
             col_terms[0, :4].astype(F32) + right3.astype(F32) + left2.astype(F32),
             col_terms[0, 4:].astype(F32) + right2.astype(F32) + left3.astype(F32),
         ]
     )
+    feats, own_x = lax.optimization_barrier((feats, own_x))
     own_z = lax.psum_scatter(
         own_x.reshape(NZ * 2 * H, TILE), "z", scatter_dimension=0, tiled=True
     ).reshape(2, H, TILE)
 
-    part = part[0] + give
-    own, up, across, down = [part[0]] + scatter4(part, "y")
-    part = (own + across) + (up + down)
-    own, up, across, down = gather4(part, "x")
-    part = (own + across) + (up + down)
+    band_terms, part = forward_tiles(
+        row_at, fwd_col, info, tiles, feats, cot_band, cot_sum
+    )
+    band_terms = band_terms.reshape(NC, NY, 2 * TILE, H)
+    give = swap(part[1])
+
+    part = (part[0] + give).astype(BF16)
+    for axis in ("y", "x"):
+        own, up, across, down = (value.astype(F32) for value in gather4(part, axis))
+        part = ((own + across) + (up + down)).astype(BF16)
     half = band_terms[0].astype(F32) + swap(band_terms[1]).astype(F32)
     part, half = lax.optimization_barrier((part, half))
-    part = lax.all_to_all(
-        jnp.broadcast_to(part, (NZ, PART + PAD, H)), "z", 0, 0, tiled=True
-    )
-    part = jnp.sum(part, axis=0)
-    grad_bias = part[PART]
-    by_y = jnp.concatenate(gather4(part[:PART], "y"))
-    by_y = lax.dynamic_slice_in_dim(jnp.concatenate([by_y, by_y]), (-y & 3) * PART, NY * PART)
-    grad_weight = lax.all_gather(by_y, "c", axis=0, tiled=True)
+    own, up, down, across = (
+        value.astype(F32) for value in [part] + [shift(part, "z", NZ, by) for by in (2, -2, 4)]
+    )
+    part = (own + across) + (up + down)
+    part = part + lax.ppermute(part, "z", [(i, i ^ 1) for i in range(NZ)])
+    grad_bias = part[TILE]
+    grad_weight = lax.all_gather(part[:TILE], "c", axis=0, tiled=True)
 
     half16 = half.astype(BF16)
     total = half[0]

time: 158 us -> 150 us (0.949)
  Pallas kernels: 21.8 us -> 18.7 us
  other arithmetic: 9.3 us -> 6.67 us
  local copies, waits for them, and re-layouts: 4.89 us -> 2.94 us
  starting transfers between devices: 41.5 us -> 39.8 us
    ppermute x24, waiting for transfers between devices: 27.6 us -> 53.3 us  [shift(): lax.ppermute(value, axis, [(i, (i + by) % size) for i in range(size)])]
    all_to_all x1 -> x0, waiting for transfers between devices: 12.2 us -> none  [shards(): lax.all_to_all(jnp.broadcast_to(part, (NZ, PART + PAD, H)), 'z', 0, 0, ti...]
    all_gather x1, waiting for transfers between devices: 13.9 us -> 1.8 us  [shards(): feats = lax.all_gather(near, 'z', axis=0, tiled=True)]
    all_to_all x1 -> x0, starting transfers between devices: 4.99 us -> none  [shards(): lax.all_to_all(jnp.broadcast_to(part, (NZ, PART + PAD, H)), 'z', 0, 0, ti...]
    ppermute x0 -> x1, starting transfers between devices: none -> 1.97 us  [shards(): part = part + lax.ppermute(part, 'z', [(i, i ^ 1) for i in range(NZ)])]
    add x1, other arithmetic: 2.06 us -> 0.32 us  [shards(): col_terms[0, :4].astype(F32) + right3.astype(F32) + left2.astype(F32)]
    ppermute x3, starting transfers between devices: 3.21 us -> 4.9 us  [swap(): return lax.ppermute(value, 'c', [(0, 1), (1, 0)])]
  transfers between devices with their start and end apart: 30 -> 30, of which waited for: 11 -> 18; matrix products, arithmetic and copies ran while one was open for 4% -> 4% of each run, Pallas kernels for 14% -> 13%
where the time goes in v3:
time: 150 us; the launch traced here: 148 us
  waiting for transfers between devices  57 us (38%)
  starting transfers between devices  39.8 us (27%)
  Pallas kernels  18.7 us (12%)
  between operations  14.9 us (10%)
  other arithmetic  6.67 us (4%)
  blocking collectives  6 us (4%)
  local copies, waits for them, and re-layouts  2.94 us (2%)
  matrix products  1.89 us (1%)
    ppermute x24, waiting for transfers between devices, shift(): lax.ppermute(value, axis, [(i, (i + by) % size) for i in range(size)])  53.3 us
    ppermute x24, starting transfers between devices, shift(): lax.ppermute(value, axis, [(i, (i + by) % size) for i in range(size)])  32.9 us
    pallas_call x1, Pallas kernels, forward_tiles(): pl.pallas_call(forward_kernel, grid_spec=pltpu.PrefetchScalarGridSpec(num...  11 us
    pallas_call x1, Pallas kernels, backward_tiles(): pl.pallas_call(backward_kernel, grid_spec=pltpu.PrefetchScalarGridSpec(nu...  7.75 us
    all_gather x1, blocking collectives, shards(): grad_weight = lax.all_gather(part[:TILE], 'c', axis=0, tiled=True)  6 us
    ppermute x3, starting transfers between devices, swap(): return lax.ppermute(value, 'c', [(0, 1), (1, 0)])  4.9 us
  transfers between devices with their start and end apart: 30, of which 18 were waited for; matrix products, arithmetic and copies ran while one was open for 4% of the time, Pallas kernels for 13%

profile of v3, /device:TPU:1, one launch (start us, length us, event | category | flops | bytes accessed | tf_op | source)
XLA Modules:
  0.0 148.0 jit_solution(3930153929846864167)
XLA Ops:
  9.1 3.6 %collective-permute-start.3 = (bf16[2,256,128]{2,1,0:T(8,128)(2,1)S(1)}, bf16[2,256,128]{2,1,0:T(8,128)(2,1)S(1)}, u32[]{:S(2)}, u32[]{:S(2)}) collective-permute-start(bf16[2,256,128]{2,1,0:T(8,128)(2,1)S(1)} %bitcast.90), channel_id=1, source_target_pairs={{0,6},{2,0},{4,2},{6,4},{1,7},{3,1},{5,3},{7,5},{8,14},{10,8},{12,... | collective-permute-start | bytes 393224 | tf_op jit(solution)/shard_map/ppermute | solution.py:158
  13.8 2.5 %collective-permute-start = (bf16[2,128,256]{2,1,0:T(8,128)(2,1)S(1)}, bf16[2,128,256]{2,1,0:T(8,128)(2,1)S(1)}, u32[]{:S(2)}, u32[]{:S(2)}) collective-permute-start(bf16[2,128,256]{2,1,0:T(8,128)(2,1)S(1)} %bitcast.94), channel_id=1, source_target_pairs={{0,192},{64,0},{128,64},{192,128},{1,193},{65,1},{129,65},{193,129... | collective-permute-start | bytes 393224 | tf_op jit(solution)/shard_map/ppermute | solution.py:158
  16.8 2.2 %collective-permute-start.2 = (bf16[2,128,256]{2,1,0:T(8,128)(2,1)S(1)}, bf16[2,128,256]{2,1,0:T(8,128)(2,1)S(1)}, u32[]{:S(2)}, u32[]{:S(2)}) collective-permute-start(bf16[2,128,256]{2,1,0:T(8,128)(2,1)S(1)} %bitcast.96), channel_id=1, source_target_pairs={{0,64},{64,128},{128,192},{192,0},{1,65},{65,129},{129,193},{193,1... | collective-permute-start | bytes 393224 | tf_op jit(solution)/shard_map/ppermute | solution.py:158
  19.0 3.4 %collective-permute-done.5 = bf16[2,256,128]{2,1,0:T(8,128)(2,1)S(1)} collective-permute-done((bf16[2,256,128]{2,1,0:T(8,128)(2,1)S(1)}, bf16[2,256,128]{2,1,0:T(8,128)(2,1)S(1)}, u32[]{:S(2)}, u32[]{:S(2)}) %collective-permute-start.5) | collective-permute-done | bytes 131104 | tf_op jit(solution)/shard_map/ppermute | solution.py:158
  26.3 2.6 %collective-permute-start.6 = (bf16[8,256,128]{2,1,0:T(8,128)(2,1)S(1)}, bf16[8,256,128]{2,1,0:T(8,128)(2,1)S(1)}, u32[]{:S(2)}, u32[]{:S(2)}) collective-permute-start(bf16[8,256,128]{2,1,0:T(8,128)(2,1)S(1)} %pad_maximum_fusion.2), channel_id=1, source_target_pairs={{0,1},{1,0},{2,3},{3,2},{4,5},{5,4},{6,7},{7,6},{8,9},{9,8},{10,11... | collective-permute-start | bytes 1572872 | tf_op jit(solution)/shard_map/ppermute | solution.py:174
  30.5 7.7 %backward_tiles.1 = bf16[64,256,128]{2,1,0:T(8,128)(2,1)S(1)} custom-call(s32[192]{0:T(256)S(1)} %bitcast.80, s32[192]{0:T(256)S(1)} %get-tuple-element.33.cols, s32[2]{0:T(128)S(1)} %pad_add_fusion.count.info, bf16[192,128,128]{2,1,0:T(8,128)(2,1)} %bitcast.83, bf16[16,256,128]{2,1,0:T(8,128)(2,1)S(1)} %constant_dynamic-update-slice_fusion.cot_t), custom_call_target="tpu_custom_call" | custom-call | flops 1610612736 | bytes 12582912 | tf_op jit(solution)/shard_map/backward_tiles/pallas_call | solution.py:139
  38.6 2.7 %collective-permute-start.11 = (bf16[4,2,256,128]{3,2,1,0:T(8,128)(2,1)S(1)}, bf16[4,2,256,128]{3,2,1,0:T(8,128)(2,1)S(1)}, u32[]{:S(2)}, u32[]{:S(2)}) collective-permute-start(bf16[4,2,256,128]{3,2,1,0:T(8,128)(2,1)S(1)} %get-tuple-element.23), channel_id=1, source_target_pairs={{0,192},{64,0},{128,64},{192,128},{1,193},{65,1},{129,65},{193,129... | collective-permute-start | bytes 1572872 | tf_op jit(solution)/shard_map/ppermute | solution.py:158
  41.3 12.2 %collective-permute-done.7 = bf16[4,2,256,128]{3,2,1,0:T(8,128)(2,1)S(1)} collective-permute-done((bf16[4,2,256,128]{3,2,1,0:T(8,128)(2,1)S(1)}, bf16[4,2,256,128]{3,2,1,0:T(8,128)(2,1)S(1)}, u32[]{:S(2)}, u32[]{:S(2)}) %collective-permute-start.7) | collective-permute-done | bytes 524320 | tf_op jit(solution)/shard_map/ppermute | solution.py:158
  53.9 9.7 %collective-permute-done.9 = bf16[4,2,256,128]{3,2,1,0:T(8,128)(2,1)S(1)} collective-permute-done((bf16[4,2,256,128]{3,2,1,0:T(8,128)(2,1)S(1)}, bf16[4,2,256,128]{3,2,1,0:T(8,128)(2,1)S(1)}, u32[]{:S(2)}, u32[]{:S(2)}) %collective-permute-start.9) | collective-permute-done | bytes 524320 | tf_op jit(solution)/shard_map/ppermute | solution.py:158
  63.6 4.3 %collective-permute-done.8 = bf16[4,2,256,128]{3,2,1,0:T(8,128)(2,1)S(1)} collective-permute-done((bf16[4,2,256,128]{3,2,1,0:T(8,128)(2,1)S(1)}, bf16[4,2,256,128]{3,2,1,0:T(8,128)(2,1)S(1)}, u32[]{:S(2)}, u32[]{:S(2)}) %collective-permute-start.8) | collective-permute-done | bytes 524320 | tf_op jit(solution)/shard_map/ppermute | solution.py:158
  68.4 10.8 %collective-permute-done.10 = bf16[4,2,256,128]{3,2,1,0:T(8,128)(2,1)S(1)} collective-permute-done((bf16[4,2,256,128]{3,2,1,0:T(8,128)(2,1)S(1)}, bf16[4,2,256,128]{3,2,1,0:T(8,128)(2,1)S(1)}, u32[]{:S(2)}, u32[]{:S(2)}) %collective-permute-start.10) | collective-permute-done | bytes 524320 | tf_op jit(solution)/shard_map/ppermute | solution.py:158
  81.2 1.8 %all-gather.2.cloned.1.call-done.feats = bf16[64,128,256]{2,1,0:T(8,128)(2,1)} async-done(((bf16[8,128,256]{2,1,0:T(8,128)(2,1)}), bf16[64,128,256]{2,1,0:T(8,128)(2,1)}) %all-gather.2.cloned.1.call-update) | async-done | bytes 4194320 | tf_op jit(solution)/shard_map/all_gather | solution.py:199
  83.0 11.0 %forward_tiles.1 = (bf16[16,128,256]{2,1,0:T(8,128)(2,1)S(1)}, f32[2,144,256]{2,1,0:T(8,128)S(1)}) custom-call(s32[192]{0:T(256)S(1)} %bitcast.81, s32[192]{0:T(256)S(1)} %get-tuple-element.34.cols, s32[2]{0:T(128)S(1)} %pad_add_fusion.count.info, bf16[192,128,128]{2,1,0:T(8,128)(2,1)} %bitcast.84, bf16[64,128,256]{2,1,0:T(8,128)(2,1)} %all-gather.2.cloned.1.call-done.feats, ...), custom_call_target="tpu_custom_call" | custom-call | flops 1610612736 | bytes 12582912 | tf_op jit(solution)/shard_map/forward_tiles/pallas_call | solution.py:114
  96.3 2.2 %collective-permute-start.14 = (bf16[144,256]{1,0:T(8,128)(2,1)S(1)}, bf16[144,256]{1,0:T(8,128)(2,1)S(1)}, u32[]{:S(2)}, u32[]{:S(2)}) collective-permute-start(bf16[144,256]{1,0:T(8,128)(2,1)S(1)} %fusion.11), channel_id=1, source_target_pairs={{0,4},{2,6},{4,0},{6,2},{1,5},{3,7},{5,1},{7,3},{8,12},{10,14},{12... | collective-permute-start | bytes 221192 | tf_op jit(solution)/shard_map/ppermute | solution.py:158
  98.5 1.9 %collective-permute-start.15 = (bf16[144,256]{1,0:T(8,128)(2,1)S(1)}, bf16[144,256]{1,0:T(8,128)(2,1)S(1)}, u32[]{:S(2)}, u32[]{:S(2)}) collective-permute-start(bf16[144,256]{1,0:T(8,128)(2,1)S(1)} %fusion.11), channel_id=1, source_target_pairs={{0,6},{2,0},{4,2},{6,4},{1,7},{3,1},{5,3},{7,5},{8,14},{10,8},{12,... | collective-permute-start | bytes 221192 | tf_op jit(solution)/shard_map/ppermute | solution.py:158
  102.1 3.1 %collective-permute-done.16 = bf16[144,256]{1,0:T(8,128)(2,1)S(1)} collective-permute-done((bf16[144,256]{1,0:T(8,128)(2,1)S(1)}, bf16[144,256]{1,0:T(8,128)(2,1)S(1)}, u32[]{:S(2)}, u32[]{:S(2)}) %collective-permute-start.16) | collective-permute-done | bytes 73760 | tf_op jit(solution)/shard_map/ppermute | solution.py:158
  105.2 2.5 %collective-permute-start.17 = (bf16[144,256]{1,0:T(8,128)(2,1)S(1)}, bf16[144,256]{1,0:T(8,128)(2,1)S(1)}, u32[]{:S(2)}, u32[]{:S(2)}) collective-permute-start(bf16[144,256]{1,0:T(8,128)(2,1)S(1)} %add_convert_fusion.1), channel_id=1, source_target_pairs={{0,128},{64,192},{128,0},{192,64},{1,129},{65,193},{129,1},{193,65... | collective-permute-start | bytes 221192 | tf_op jit(solution)/shard_map/ppermute | solution.py:158
  111.3 2.0 %collective-permute-done.19 = bf16[144,256]{1,0:T(8,128)(2,1)S(1)} collective-permute-done((bf16[144,256]{1,0:T(8,128)(2,1)S(1)}, bf16[144,256]{1,0:T(8,128)(2,1)S(1)}, u32[]{:S(2)}, u32[]{:S(2)}) %collective-permute-start.19) | collective-permute-done | bytes 73760 | tf_op jit(solution)/shard_map/ppermute | solution.py:158
  113.5 5.4 %collective-permute-start.24 = (bf16[144,256]{1,0:T(8,128)(2,1)S(1)}, bf16[144,256]{1,0:T(8,128)(2,1)S(1)}, u32[]{:S(2)}, u32[]{:S(2)}) collective-permute-start(bf16[144,256]{1,0:T(8,128)(2,1)S(1)} %add_convert_fusion), channel_id=1, source_target_pairs={{0,32},{8,40},{16,48},{24,56},{32,0},{40,8},{48,16},{56,24},{1,33}... | collective-permute-start | bytes 221192 | tf_op jit(solution)/shard_map/ppermute | solution.py:158
  119.0 3.6 %collective-permute-start.26 = (bf16[144,256]{1,0:T(8,128)(2,1)S(1)}, bf16[144,256]{1,0:T(8,128)(2,1)S(1)}, u32[]{:S(2)}, u32[]{:S(2)}) collective-permute-start(bf16[144,256]{1,0:T(8,128)(2,1)S(1)} %add_convert_fusion), channel_id=1, source_target_pairs={{0,48},{8,56},{16,0},{24,8},{32,16},{40,24},{48,32},{56,40},{1,49}... | collective-permute-start | bytes 221192 | tf_op jit(solution)/shard_map/ppermute | solution.py:158
  122.7 2.7 %collective-permute-start.22 = (bf16[256,256]{1,0:T(8,128)(2,1)S(1)}, bf16[256,256]{1,0:T(8,128)(2,1)S(1)}, u32[]{:S(2)}, u32[]{:S(2)}) collective-permute-start(bf16[256,256]{1,0:T(8,128)(2,1)S(1)} %get-tuple-element.30), channel_id=1, source_target_pairs={{0,6},{2,0},{4,2},{6,4},{1,7},{3,1},{5,3},{7,5},{8,14},{10,8},{12,... | collective-permute-start | bytes 393224 | tf_op jit(solution)/shard_map/ppermute | solution.py:158
  126.7 2.0 %collective-permute-start.27 = (f32[144,256]{1,0:T(8,128)S(1)}, f32[144,256]{1,0:T(8,128)S(1)}, u32[]{:S(2)}, u32[]{:S(2)}) collective-permute-start(f32[144,256]{1,0:T(8,128)S(1)} %add_add_fusion), channel_id=1, source_target_pairs={{0,8},{8,0},{16,24},{24,16},{32,40},{40,32},{48,56},{56,48},{1,9},... | collective-permute-start | bytes 442376 | tf_op jit(solution)/shard_map/ppermute | solution.py:243
  128.7 2.1 %collective-permute-done.23 = bf16[256,256]{1,0:T(8,128)(2,1)S(1)} collective-permute-done((bf16[256,256]{1,0:T(8,128)(2,1)S(1)}, bf16[256,256]{1,0:T(8,128)(2,1)S(1)}, u32[]{:S(2)}, u32[]{:S(2)}) %collective-permute-start.23) | collective-permute-done | bytes 131104 | tf_op jit(solution)/shard_map/ppermute | solution.py:158
  132.3 6.0 %all_gather.7 = f32[256,256]{1,0:T(8,128)S(1)} all-gather(f32[128,256]{1,0:T(8,128)S(1)} %slice.85), channel_id=1, replica_groups=mesh['x'=4,'z'=8,'y'=4,'c'=2] {'c'}, dimensions={0}, use_global_device_ids=true | all-gather | bytes 393216 | tf_op jit(solution)/shard_map/all_gather | solution.py:245
  (77 shorter events, 24.9 us)
Async XLA Ops:
  7.2 75.8 %all-gather.2.cloned.1.call-start = ((), (), s32[]{:S(2)}) async-start(), calls=%async_computation.1 | async-start | bytes 4718592 | tf_op jit(solution)/shard_map/all_gather | solution.py:199
  9.1 7.7 %collective-permute-start.3 = (bf16[2,256,128]{2,1,0:T(8,128)(2,1)S(1)}, bf16[2,256,128]{2,1,0:T(8,128)(2,1)S(1)}, u32[]{:S(2)}, u32[]{:S(2)}) collective-permute-start(bf16[2,256,128]{2,1,0:T(8,128)(2,1)S(1)} %bitcast.90), channel_id=1, source_target_pairs={{0,6},{2,0},{4,2},{6,4},{1,7},{3,1},{5,3},{7,5},{8,14},{10,8},{12,... | collective-permute-start | bytes 393224 | tf_op jit(solution)/shard_map/ppermute | solution.py:158
  12.8 6.2 %collective-permute-start.4 = (bf16[2,256,128]{2,1,0:T(8,128)(2,1)S(1)}, bf16[2,256,128]{2,1,0:T(8,128)(2,1)S(1)}, u32[]{:S(2)}, u32[]{:S(2)}) collective-permute-start(bf16[2,256,128]{2,1,0:T(8,128)(2,1)S(1)} %bitcast.91), channel_id=1, source_target_pairs={{0,4},{2,6},{4,0},{6,2},{1,5},{3,7},{5,1},{7,3},{8,12},{10,14},{12... | collective-permute-start | bytes 393224 | tf_op jit(solution)/shard_map/ppermute | solution.py:158
  13.1 9.3 %collective-permute-start.5 = (bf16[2,256,128]{2,1,0:T(8,128)(2,1)S(1)}, bf16[2,256,128]{2,1,0:T(8,128)(2,1)S(1)}, u32[]{:S(2)}, u32[]{:S(2)}) collective-permute-start(bf16[2,256,128]{2,1,0:T(8,128)(2,1)S(1)} %bitcast.92), channel_id=1, source_target_pairs={{0,2},{2,4},{4,6},{6,0},{1,3},{3,5},{5,7},{7,1},{8,10},{10,12},{12... | collective-permute-start | bytes 393224 | tf_op jit(solution)/shard_map/ppermute | solution.py:158
  13.8 8.7 %collective-permute-start = (bf16[2,128,256]{2,1,0:T(8,128)(2,1)S(1)}, bf16[2,128,256]{2,1,0:T(8,128)(2,1)S(1)}, u32[]{:S(2)}, u32[]{:S(2)}) collective-permute-start(bf16[2,128,256]{2,1,0:T(8,128)(2,1)S(1)} %bitcast.94), channel_id=1, source_target_pairs={{0,192},{64,0},{128,64},{192,128},{1,193},{65,1},{129,65},{193,129... | collective-permute-start | bytes 393224 | tf_op jit(solution)/shard_map/ppermute | solution.py:158
  16.3 6.2 %collective-permute-start.1 = (bf16[2,128,256]{2,1,0:T(8,128)(2,1)S(1)}, bf16[2,128,256]{2,1,0:T(8,128)(2,1)S(1)}, u32[]{:S(2)}, u32[]{:S(2)}) collective-permute-start(bf16[2,128,256]{2,1,0:T(8,128)(2,1)S(1)} %bitcast.95), channel_id=1, source_target_pairs={{0,128},{64,192},{128,0},{192,64},{1,129},{65,193},{129,1},{193,65... | collective-permute-start | bytes 393224 | tf_op jit(solution)/shard_map/ppermute | solution.py:158
  16.8 7.1 %collective-permute-start.2 = (bf16[2,128,256]{2,1,0:T(8,128)(2,1)S(1)}, bf16[2,128,256]{2,1,0:T(8,128)(2,1)S(1)}, u32[]{:S(2)}, u32[]{:S(2)}) collective-permute-start(bf16[2,128,256]{2,1,0:T(8,128)(2,1)S(1)} %bitcast.96), channel_id=1, source_target_pairs={{0,64},{64,128},{128,192},{192,0},{1,65},{65,129},{129,193},{193,1... | collective-permute-start | bytes 393224 | tf_op jit(solution)/shard_map/ppermute | solution.py:158
  24.8 113.5 %reduce-scatter.2.cloned.1.call-start = ((), (), s32[]{:S(2)}) async-start(), calls=%async_computation.2 | async-start | bytes 2359296 | tf_op jit(solution)/shard_map/reduce_scatter | solution.py:223
  38.5 15.0 %collective-permute-start.7 = (bf16[4,2,256,128]{3,2,1,0:T(8,128)(2,1)S(1)}, bf16[4,2,256,128]{3,2,1,0:T(8,128)(2,1)S(1)}, u32[]{:S(2)}, u32[]{:S(2)}) collective-permute-start(bf16[4,2,256,128]{3,2,1,0:T(8,128)(2,1)S(1)} %get-tuple-element.22), channel_id=1, source_target_pairs={{0,64},{64,128},{128,192},{192,0},{1,65},{65,129},{129,193},{193,1... | collective-permute-start | bytes 1572872 | tf_op jit(solution)/shard_map/ppermute | solution.py:158
  38.6 15.3 %collective-permute-start.11 = (bf16[4,2,256,128]{3,2,1,0:T(8,128)(2,1)S(1)}, bf16[4,2,256,128]{3,2,1,0:T(8,128)(2,1)S(1)}, u32[]{:S(2)}, u32[]{:S(2)}) collective-permute-start(bf16[4,2,256,128]{3,2,1,0:T(8,128)(2,1)S(1)} %get-tuple-element.23), channel_id=1, source_target_pairs={{0,192},{64,0},{128,64},{192,128},{1,193},{65,1},{129,65},{193,129... | collective-permute-start | bytes 1572872 | tf_op jit(solution)/shard_map/ppermute | solution.py:158
  41.2 22.4 %collective-permute-start.9 = (bf16[4,2,256,128]{3,2,1,0:T(8,128)(2,1)S(1)}, bf16[4,2,256,128]{3,2,1,0:T(8,128)(2,1)S(1)}, u32[]{:S(2)}, u32[]{:S(2)}) collective-permute-start(bf16[4,2,256,128]{3,2,1,0:T(8,128)(2,1)S(1)} %get-tuple-element.25), channel_id=1, source_target_pairs={{0,192},{64,0},{128,64},{192,128},{1,193},{65,1},{129,65},{193,129... | collective-permute-start | bytes 1572872 | tf_op jit(solution)/shard_map/ppermute | solution.py:158
  53.7 14.3 %collective-permute-start.8 = (bf16[4,2,256,128]{3,2,1,0:T(8,128)(2,1)S(1)}, bf16[4,2,256,128]{3,2,1,0:T(8,128)(2,1)S(1)}, u32[]{:S(2)}, u32[]{:S(2)}) collective-permute-start(bf16[4,2,256,128]{3,2,1,0:T(8,128)(2,1)S(1)} %fusion.4), channel_id=1, source_target_pairs={{0,64},{64,128},{128,192},{192,0},{1,65},{65,129},{129,193},{193,1... | collective-permute-start | bytes 1572872 | tf_op jit(solution)/shard_map/ppermute | solution.py:158
  53.8 25.4 %collective-permute-start.10 = (bf16[4,2,256,128]{3,2,1,0:T(8,128)(2,1)S(1)}, bf16[4,2,256,128]{3,2,1,0:T(8,128)(2,1)S(1)}, u32[]{:S(2)}, u32[]{:S(2)}) collective-permute-start(bf16[4,2,256,128]{3,2,1,0:T(8,128)(2,1)S(1)} %get-tuple-element.24), channel_id=1, source_target_pairs={{0,64},{64,128},{128,192},{192,0},{1,65},{65,129},{129,193},{193,1... | collective-permute-start | bytes 1572872 | tf_op jit(solution)/shard_map/ppermute | solution.py:158
  68.3 11.2 %collective-permute-start.12 = (bf16[4,2,256,128]{3,2,1,0:T(8,128)(2,1)S(1)}, bf16[4,2,256,128]{3,2,1,0:T(8,128)(2,1)S(1)}, u32[]{:S(2)}, u32[]{:S(2)}) collective-permute-start(bf16[4,2,256,128]{3,2,1,0:T(8,128)(2,1)S(1)} %get-tuple-element.21), channel_id=1, source_target_pairs={{0,192},{64,0},{128,64},{192,128},{1,193},{65,1},{129,65},{193,129... | collective-permute-start | bytes 1572872 | tf_op jit(solution)/shard_map/ppermute | solution.py:158
  96.3 5.2 %collective-permute-start.14 = (bf16[144,256]{1,0:T(8,128)(2,1)S(1)}, bf16[144,256]{1,0:T(8,128)(2,1)S(1)}, u32[]{:S(2)}, u32[]{:S(2)}) collective-permute-start(bf16[144,256]{1,0:T(8,128)(2,1)S(1)} %fusion.11), channel_id=1, source_target_pairs={{0,4},{2,6},{4,0},{6,2},{1,5},{3,7},{5,1},{7,3},{8,12},{10,14},{12... | collective-permute-start | bytes 221192 | tf_op jit(solution)/shard_map/ppermute | solution.py:158
  100.5 12.9 %collective-permute-start.20 = (bf16[4,256,256]{2,1,0:T(8,128)(2,1)S(1)}, bf16[4,256,256]{2,1,0:T(8,128)(2,1)S(1)}, u32[]{:S(2)}, u32[]{:S(2)}) collective-permute-start(bf16[4,256,256]{2,1,0:T(8,128)(2,1)S(1)} %bitcast.89), channel_id=1, source_target_pairs={{0,1},{1,0},{2,3},{3,2},{4,5},{5,4},{6,7},{7,6},{8,9},{9,8},{10,11... | collective-permute-start | bytes 1572872 | tf_op jit(solution)/shard_map/ppermute | solution.py:174
  107.7 5.6 %collective-permute-start.19 = (bf16[144,256]{1,0:T(8,128)(2,1)S(1)}, bf16[144,256]{1,0:T(8,128)(2,1)S(1)}, u32[]{:S(2)}, u32[]{:S(2)}) collective-permute-start(bf16[144,256]{1,0:T(8,128)(2,1)S(1)} %add_convert_fusion.1), channel_id=1, source_target_pairs={{0,64},{64,128},{128,192},{192,0},{1,65},{65,129},{129,193},{193,1... | collective-permute-start | bytes 221192 | tf_op jit(solution)/shard_map/ppermute | solution.py:158
  113.5 11.9 %collective-permute-start.24 = (bf16[144,256]{1,0:T(8,128)(2,1)S(1)}, bf16[144,256]{1,0:T(8,128)(2,1)S(1)}, u32[]{:S(2)}, u32[]{:S(2)}) collective-permute-start(bf16[144,256]{1,0:T(8,128)(2,1)S(1)} %add_convert_fusion), channel_id=1, source_target_pairs={{0,32},{8,40},{16,48},{24,56},{32,0},{40,8},{48,16},{56,24},{1,33}... | collective-permute-start | bytes 221192 | tf_op jit(solution)/shard_map/ppermute | solution.py:158
  119.0 7.6 %collective-permute-start.25 = (bf16[144,256]{1,0:T(8,128)(2,1)S(1)}, bf16[144,256]{1,0:T(8,128)(2,1)S(1)}, u32[]{:S(2)}, u32[]{:S(2)}) collective-permute-start(bf16[144,256]{1,0:T(8,128)(2,1)S(1)} %add_convert_fusion), channel_id=1, source_target_pairs={{0,16},{8,24},{16,32},{24,40},{32,48},{40,56},{48,0},{56,8},{1,17}... | collective-permute-start | bytes 221192 | tf_op jit(solution)/shard_map/ppermute | solution.py:158
  119.0 7.6 %collective-permute-start.26 = (bf16[144,256]{1,0:T(8,128)(2,1)S(1)}, bf16[144,256]{1,0:T(8,128)(2,1)S(1)}, u32[]{:S(2)}, u32[]{:S(2)}) collective-permute-start(bf16[144,256]{1,0:T(8,128)(2,1)S(1)} %add_convert_fusion), channel_id=1, source_target_pairs={{0,48},{8,56},{16,0},{24,8},{32,16},{40,24},{48,32},{56,40},{1,49}... | collective-permute-start | bytes 221192 | tf_op jit(solution)/shard_map/ppermute | solution.py:158
  122.6 6.0 %collective-permute-start.21 = (bf16[256,256]{1,0:T(8,128)(2,1)S(1)}, bf16[256,256]{1,0:T(8,128)(2,1)S(1)}, u32[]{:S(2)}, u32[]{:S(2)}) collective-permute-start(bf16[256,256]{1,0:T(8,128)(2,1)S(1)} %get-tuple-element.28), channel_id=1, source_target_pairs={{0,2},{2,4},{4,6},{6,0},{1,3},{3,5},{5,7},{7,1},{8,10},{10,12},{12... | collective-permute-start | bytes 393224 | tf_op jit(solution)/shard_map/ppermute | solution.py:158
  122.7 6.0 %collective-permute-start.22 = (bf16[256,256]{1,0:T(8,128)(2,1)S(1)}, bf16[256,256]{1,0:T(8,128)(2,1)S(1)}, u32[]{:S(2)}, u32[]{:S(2)}) collective-permute-start(bf16[256,256]{1,0:T(8,128)(2,1)S(1)} %get-tuple-element.30), channel_id=1, source_target_pairs={{0,6},{2,0},{4,2},{6,4},{1,7},{3,1},{5,3},{7,5},{8,14},{10,8},{12,... | collective-permute-start | bytes 393224 | tf_op jit(solution)/shard_map/ppermute | solution.py:158
  125.4 5.4 %collective-permute-start.23 = (bf16[256,256]{1,0:T(8,128)(2,1)S(1)}, bf16[256,256]{1,0:T(8,128)(2,1)S(1)}, u32[]{:S(2)}, u32[]{:S(2)}) collective-permute-start(bf16[256,256]{1,0:T(8,128)(2,1)S(1)} %get-tuple-element.29), channel_id=1, source_target_pairs={{0,4},{2,6},{4,0},{6,2},{1,5},{3,7},{5,1},{7,3},{8,12},{10,14},{12... | collective-permute-start | bytes 393224 | tf_op jit(solution)/shard_map/ppermute | solution.py:158
  126.7 5.1 %collective-permute-start.27 = (f32[144,256]{1,0:T(8,128)S(1)}, f32[144,256]{1,0:T(8,128)S(1)}, u32[]{:S(2)}, u32[]{:S(2)}) collective-permute-start(f32[144,256]{1,0:T(8,128)S(1)} %add_add_fusion), channel_id=1, source_target_pairs={{0,8},{8,0},{16,24},{24,16},{32,40},{40,32},{48,56},{56,48},{1,9},... | collective-permute-start | bytes 442376 | tf_op jit(solution)/shard_map/ppermute | solution.py:243
  (8 other events, 183.8 us)
Sparse Core Ops, SparseCore 0:
  24.9 57.9 all-gather.1
  85.5 37.9 reduce-scatter.1

commit v4 on v3

--- a/solution.py
+++ b/solution.py
@@ -79,7 +79,7 @@
             grad[to, TILE:] = jnp.broadcast_to(cot_sum[...], (PAD, H))
 
 
-def backward_kernel(rows, cols, count, tiles, cot_t, out, acc):
+def backward_kernel(rows, cols, count, tiles, cot_t, right, left, rest, acc):
     @pl.when(pl.program_id(0) == 0)
     def _():
         clear(acc)
@@ -95,10 +95,13 @@
     @pl.when(pl.program_id(0) == pl.num_programs(0) - 1)
     def _():
         def finish(i, carry):
-            out[i] = acc[i].astype(BF16)
+            right[i] = acc[i].astype(BF16)
+            left[i] = acc[16 + i].astype(BF16)
+            rest[i] = acc[32 + i].astype(BF16)
+            rest[16 + i] = acc[48 + i].astype(BF16)
             return carry
 
-        lax.fori_loop(0, GROUP, finish, 0)
+        lax.fori_loop(0, 16, finish, 0)
 
 
 def whole(shape):
@@ -142,10 +145,10 @@
             num_scalar_prefetch=3,
             grid=(TCAP // CHUNK,),
             in_specs=[tile_block(), whole((BAND, H, TILE))],
-            out_specs=whole((GROUP, H, TILE)),
+            out_specs=[whole((blocks, H, TILE)) for blocks in (16, 16, 32)],
             scratch_shapes=[pltpu.VMEM((GROUP + 1, H, TILE), F32)],
         ),
-        out_shape=jax.ShapeDtypeStruct((GROUP, H, TILE), BF16),
+        out_shape=[jax.ShapeDtypeStruct((blocks, H, TILE), BF16) for blocks in (16, 16, 32)],
         compiler_params=pltpu.CompilerParams(vmem_limit_bytes=VMEM_LIMIT),
         cost_estimate=pl.CostEstimate(
             flops=TCAP * 2 * TILE * TILE * H, bytes_accessed=12 << 20, transcendentals=0
@@ -191,7 +194,10 @@
     col_dev = cols >> 1
     col_x, col_z = ((col_dev >> 3) - x) & 3, col_dev & 7
     fwd_col = (((col_z << 2) | col_x) << 1) | (cols & 1)
-    bwd_col = (((col_x << 3) | col_z) << 1) | (cols & 1)
+    places = {(2, 0): 0, (1, 1): 8, (2, 1): 16, (3, 0): 24, (1, 0): 32, (3, 1): 40, (0, 0): 48, (0, 1): 56}
+    bwd_col = ((col_z & 3) << 1) | (cols & 1)
+    for (of_x, of_z), place in places.items():
+        bwd_col += jnp.where((col_x == of_x) & (col_z >> 2 == of_z), place, 0)
 
     near = jnp.concatenate(gather4(scaled, "x"))
     cot_y = jnp.concatenate(gather4(cot_t, "y"))
@@ -200,23 +206,23 @@
 
     cot_band = jnp.concatenate([cot_y, swap(cot_y)])
 
-    col_terms = backward_tiles(row_at, bwd_col, info, tiles, cot_band)
-    col_terms = col_terms.reshape(NX, NZ, 2, H, TILE)
+    to_right, to_left, kept = backward_tiles(row_at, bwd_col, info, tiles, cot_band)
 
     def add(a, b):
         return (a.astype(F32) + b.astype(F32)).astype(BF16)
 
-    right1 = shift(col_terms[2, :4], "x", NX, 1)
-    left1 = shift(col_terms[2, 4:], "x", NX, -1)
-    right2 = shift(col_terms[1, 4:], "x", NX, 1)
-    left2 = shift(col_terms[3, :4], "x", NX, -1)
-    right3 = shift(add(col_terms[1, :4], right1), "x", NX, 1)
-    left3 = shift(add(col_terms[3, 4:], left1), "x", NX, -1)
+    right1 = shift(to_right, "x", NX, 1)
+    left1 = shift(to_left, "x", NX, -1)
+    to_right, to_left = lax.optimization_barrier(
+        (add(kept[:8], right1[:8]), add(kept[8:16], left1[:8]))
+    )
+    right2 = shift(to_right, "x", NX, 1)
+    left2 = shift(to_left, "x", NX, -1)
 
     own_x = jnp.concatenate(
         [
-            col_terms[0, :4].astype(F32) + right3.astype(F32) + left2.astype(F32),
-            col_terms[0, 4:].astype(F32) + right2.astype(F32) + left3.astype(F32),
+            kept[16:24].astype(F32) + right2.astype(F32) + left1[8:].astype(F32),
+            kept[24:].astype(F32) + right1[8:].astype(F32) + left2.astype(F32),
         ]
     )
     feats, own_x = lax.optimization_barrier((feats, own_x))
@@ -240,9 +246,9 @@
         value.astype(F32) for value in [part] + [shift(part, "z", NZ, by) for by in (2, -2, 4)]
     )
     part = (own + across) + (up + down)
-    part = part + lax.ppermute(part, "z", [(i, i ^ 1) for i in range(NZ)])
-    grad_bias = part[TILE]
-    grad_weight = lax.all_gather(part[:TILE], "c", axis=0, tiled=True)
+    other = lax.ppermute(part, "z", [(i, i ^ 1) for i in range(NZ)])
+    grad_bias = part[TILE] + other[TILE]
+    part = part[:TILE] + other[:TILE]
 
     half16 = half.astype(BF16)
     total = half[0]
@@ -255,6 +261,8 @@
         "ahn,gh->ang", own_z, weight.astype(F32), precision=lax.Precision.HIGHEST
     ).reshape(2 * TILE, H)
     grad_features = (grad_features * inv_root[:, None]).astype(BF16)
+    part, grad_features = lax.optimization_barrier((part, grad_features))
+    grad_weight = lax.all_gather(part, "c", axis=0, tiled=True)
     return (layer_out, grad_weight, grad_bias, grad_features)
 
 

time: 150 us -> 149 us (level)
  waiting for transfers between devices: 57 us -> 61 us
    ppermute x1, starting transfers between devices: 1.97 us -> 0.09 us  [shards(): other = lax.ppermute(part, 'z', [(i, i ^ 1) for i in range(NZ)])]
    ppermute x24 -> x22, waiting for transfers between devices: 53.3 us -> 55.1 us  [shift(): lax.ppermute(value, axis, [(i, (i + by) % size) for i in range(size)])]
    all_gather x1, waiting for transfers between devices: 1.8 us -> 3.44 us  [shards(): feats = lax.all_gather(near, 'z', axis=0, tiled=True)]
    ppermute x24 -> x22, starting transfers between devices: 32.9 us -> 34.3 us  [shift(): lax.ppermute(value, axis, [(i, (i + by) % size) for i in range(size)])]
  transfers between devices with their start and end apart: 30 -> 28, of which waited for: 18 -> 16; matrix products, arithmetic and copies ran while one was open for 4% -> 3% of each run, Pallas kernels for 13% -> 12%
where the time goes in v4:
time: 149 us; the launch traced here: 148 us
  waiting for transfers between devices  61 us (41%)
  starting transfers between devices  39.2 us (26%)
  Pallas kernels  17.7 us (12%)
  between operations  14.9 us (10%)
  other arithmetic  5.94 us (4%)
  blocking collectives  4.99 us (3%)
  local copies, waits for them, and re-layouts  2.16 us (1%)
  matrix products  1.89 us (1%)
    ppermute x22, waiting for transfers between devices, shift(): lax.ppermute(value, axis, [(i, (i + by) % size) for i in range(size)])  55.1 us
    ppermute x22, starting transfers between devices, shift(): lax.ppermute(value, axis, [(i, (i + by) % size) for i in range(size)])  34.3 us
    pallas_call x1, Pallas kernels, forward_tiles(): pl.pallas_call(forward_kernel, grid_spec=pltpu.PrefetchScalarGridSpec(num...  10.5 us
    pallas_call x1, Pallas kernels, backward_tiles(): pl.pallas_call(backward_kernel, grid_spec=pltpu.PrefetchScalarGridSpec(nu...  7.19 us
    all_gather x1, blocking collectives, shards(): grad_weight = lax.all_gather(part, 'c', axis=0, tiled=True)  4.99 us
    ppermute x3, starting transfers between devices, swap(): return lax.ppermute(value, 'c', [(0, 1), (1, 0)])  4.67 us
    all_gather x1, waiting for transfers between devices, shards(): feats = lax.all_gather(near, 'z', axis=0, tiled=True)  3.44 us
  transfers between devices with their start and end apart: 28, of which 16 were waited for; matrix products, arithmetic and copies ran while one was open for 3% of the time, Pallas kernels for 12%

profile of v4, /device:TPU:1, one launch (start us, length us, event | category | flops | bytes accessed | tf_op | source)
XLA Modules:
  0.0 147.8 jit_solution(558527814942820204)
XLA Ops:
  9.2 3.6 %collective-permute-start.3 = (bf16[2,256,128]{2,1,0:T(8,128)(2,1)S(1)}, bf16[2,256,128]{2,1,0:T(8,128)(2,1)S(1)}, u32[]{:S(2)}, u32[]{:S(2)}) collective-permute-start(bf16[2,256,128]{2,1,0:T(8,128)(2,1)S(1)} %bitcast.58), channel_id=1, source_target_pairs={{0,6},{2,0},{4,2},{6,4},{1,7},{3,1},{5,3},{7,5},{8,14},{10,8},{12,... | collective-permute-start | bytes 393224 | tf_op jit(solution)/shard_map/ppermute | solution.py:161
  13.9 2.5 %collective-permute-start = (bf16[2,128,256]{2,1,0:T(8,128)(2,1)S(1)}, bf16[2,128,256]{2,1,0:T(8,128)(2,1)S(1)}, u32[]{:S(2)}, u32[]{:S(2)}) collective-permute-start(bf16[2,128,256]{2,1,0:T(8,128)(2,1)S(1)} %bitcast.62), channel_id=1, source_target_pairs={{0,192},{64,0},{128,64},{192,128},{1,193},{65,1},{129,65},{193,129... | collective-permute-start | bytes 393224 | tf_op jit(solution)/shard_map/ppermute | solution.py:161
  16.9 2.2 %collective-permute-start.2 = (bf16[2,128,256]{2,1,0:T(8,128)(2,1)S(1)}, bf16[2,128,256]{2,1,0:T(8,128)(2,1)S(1)}, u32[]{:S(2)}, u32[]{:S(2)}) collective-permute-start(bf16[2,128,256]{2,1,0:T(8,128)(2,1)S(1)} %bitcast.64), channel_id=1, source_target_pairs={{0,64},{64,128},{128,192},{192,0},{1,65},{65,129},{129,193},{193,1... | collective-permute-start | bytes 393224 | tf_op jit(solution)/shard_map/ppermute | solution.py:161
  19.0 3.4 %collective-permute-done.5 = bf16[2,256,128]{2,1,0:T(8,128)(2,1)S(1)} collective-permute-done((bf16[2,256,128]{2,1,0:T(8,128)(2,1)S(1)}, bf16[2,256,128]{2,1,0:T(8,128)(2,1)S(1)}, u32[]{:S(2)}, u32[]{:S(2)}) %collective-permute-start.5) | collective-permute-done | bytes 131104 | tf_op jit(solution)/shard_map/ppermute | solution.py:161
  25.6 2.7 %collective-permute-start.6 = (bf16[8,256,128]{2,1,0:T(8,128)(2,1)S(1)}, bf16[8,256,128]{2,1,0:T(8,128)(2,1)S(1)}, u32[]{:S(2)}, u32[]{:S(2)}) collective-permute-start(bf16[8,256,128]{2,1,0:T(8,128)(2,1)S(1)} %pad_maximum_fusion.2), channel_id=1, source_target_pairs={{0,1},{1,0},{2,3},{3,2},{4,5},{5,4},{6,7},{7,6},{8,9},{9,8},{10,11... | collective-permute-start | bytes 1572872 | tf_op jit(solution)/shard_map/ppermute | solution.py:177
  29.9 7.2 %backward_tiles.1 = (bf16[16,256,128]{2,1,0:T(8,128)(2,1)S(1)}, bf16[16,256,128]{2,1,0:T(8,128)(2,1)S(1)}, bf16[32,256,128]{2,1,0:T(8,128)(2,1)S(1)}) custom-call(s32[192]{0:T(256)S(1)} %bitcast.46, s32[192]{0:T(256)S(1)} %bitcast.50, s32[2]{0:T(128)S(1)} %pad_add_fusion.count.info, bf16[192,128,128]{2,1,0:T(8,128)(2,1)} %bitcast.51, ...), custom_call_target="tpu_custom_call" | custom-call | flops 1610612736 | bytes 12582912 | tf_op jit(solution)/shard_map/backward_tiles/pallas_call | solution.py:142
  37.2 2.7 %collective-permute-start.8 = (bf16[16,256,128]{2,1,0:T(8,128)(2,1)S(1)}, bf16[16,256,128]{2,1,0:T(8,128)(2,1)S(1)}, u32[]{:S(2)}, u32[]{:S(2)}) collective-permute-start(bf16[16,256,128]{2,1,0:T(8,128)(2,1)S(1)} %get-tuple-element.23), channel_id=1, source_target_pairs={{0,192},{64,0},{128,64},{192,128},{1,193},{65,1},{129,65},{193,129... | collective-permute-start | bytes 3145736 | tf_op jit(solution)/shard_map/ppermute | solution.py:161
  39.8 22.5 %collective-permute-done.7 = bf16[16,256,128]{2,1,0:T(8,128)(2,1)S(1)} collective-permute-done((bf16[16,256,128]{2,1,0:T(8,128)(2,1)S(1)}, bf16[16,256,128]{2,1,0:T(8,128)(2,1)S(1)}, u32[]{:S(2)}, u32[]{:S(2)}) %collective-permute-start.7) | collective-permute-done | bytes 1048608 | tf_op jit(solution)/shard_map/ppermute | solution.py:161
  62.6 2.4 %collective-permute-start.10 = (bf16[8,256,128]{2,1,0:T(8,128)(2,1)S(1)}, bf16[8,256,128]{2,1,0:T(8,128)(2,1)S(1)}, u32[]{:S(2)}, u32[]{:S(2)}) collective-permute-start(bf16[8,256,128]{2,1,0:T(8,128)(2,1)S(1)} %get-tuple-element.25), channel_id=1, source_target_pairs={{0,192},{64,0},{128,64},{192,128},{1,193},{65,1},{129,65},{193,129... | collective-permute-start | bytes 1572872 | tf_op jit(solution)/shard_map/ppermute | solution.py:161
  65.1 9.6 %collective-permute-done.10 = bf16[8,256,128]{2,1,0:T(8,128)(2,1)S(1)} collective-permute-done((bf16[8,256,128]{2,1,0:T(8,128)(2,1)S(1)}, bf16[8,256,128]{2,1,0:T(8,128)(2,1)S(1)}, u32[]{:S(2)}, u32[]{:S(2)}) %collective-permute-start.10) | collective-permute-done | bytes 524320 | tf_op jit(solution)/shard_map/ppermute | solution.py:161
  74.6 3.0 %collective-permute-done.9 = bf16[8,256,128]{2,1,0:T(8,128)(2,1)S(1)} collective-permute-done((bf16[8,256,128]{2,1,0:T(8,128)(2,1)S(1)}, bf16[8,256,128]{2,1,0:T(8,128)(2,1)S(1)}, u32[]{:S(2)}, u32[]{:S(2)}) %collective-permute-start.9) | collective-permute-done | bytes 524320 | tf_op jit(solution)/shard_map/ppermute | solution.py:161
  79.5 3.4 %all-gather.2.cloned.1.call-done.feats = bf16[64,128,256]{2,1,0:T(8,128)(2,1)} async-done(((bf16[8,128,256]{2,1,0:T(8,128)(2,1)}), bf16[64,128,256]{2,1,0:T(8,128)(2,1)}) %all-gather.2.cloned.1.call-update) | async-done | bytes 4194320 | tf_op jit(solution)/shard_map/all_gather | solution.py:205
  83.0 10.5 %forward_tiles.1 = (bf16[16,128,256]{2,1,0:T(8,128)(2,1)S(1)}, f32[2,144,256]{2,1,0:T(8,128)S(1)}) custom-call(s32[192]{0:T(256)S(1)} %bitcast.47, s32[192]{0:T(256)S(1)} %bitcast.49, s32[2]{0:T(128)S(1)} %pad_add_fusion.count.info, bf16[192,128,128]{2,1,0:T(8,128)(2,1)} %bitcast.52, bf16[64,128,256]{2,1,0:T(8,128)(2,1)} %all-gather.2.cloned.1.call-done.feats, ...), custom_call_target="tpu_custom_call" | custom-call | flops 1610612736 | bytes 12582912 | tf_op jit(solution)/shard_map/forward_tiles/pallas_call | solution.py:117
  95.8 3.6 %collective-permute-start.12 = (bf16[144,256]{1,0:T(8,128)(2,1)S(1)}, bf16[144,256]{1,0:T(8,128)(2,1)S(1)}, u32[]{:S(2)}, u32[]{:S(2)}) collective-permute-start(bf16[144,256]{1,0:T(8,128)(2,1)S(1)} %fusion.7), channel_id=1, source_target_pairs={{0,4},{2,6},{4,0},{6,2},{1,5},{3,7},{5,1},{7,3},{8,12},{10,14},{12... | collective-permute-start | bytes 221192 | tf_op jit(solution)/shard_map/ppermute | solution.py:161
  99.4 2.3 %collective-permute-start.13 = (bf16[144,256]{1,0:T(8,128)(2,1)S(1)}, bf16[144,256]{1,0:T(8,128)(2,1)S(1)}, u32[]{:S(2)}, u32[]{:S(2)}) collective-permute-start(bf16[144,256]{1,0:T(8,128)(2,1)S(1)} %fusion.7), channel_id=1, source_target_pairs={{0,6},{2,0},{4,2},{6,4},{1,7},{3,1},{5,3},{7,5},{8,14},{10,8},{12,... | collective-permute-start | bytes 221192 | tf_op jit(solution)/shard_map/ppermute | solution.py:161
  103.1 3.1 %collective-permute-done.14 = bf16[144,256]{1,0:T(8,128)(2,1)S(1)} collective-permute-done((bf16[144,256]{1,0:T(8,128)(2,1)S(1)}, bf16[144,256]{1,0:T(8,128)(2,1)S(1)}, u32[]{:S(2)}, u32[]{:S(2)}) %collective-permute-start.14) | collective-permute-done | bytes 73760 | tf_op jit(solution)/shard_map/ppermute | solution.py:161
  108.5 2.5 %collective-permute-done.15 = bf16[144,256]{1,0:T(8,128)(2,1)S(1)} collective-permute-done((bf16[144,256]{1,0:T(8,128)(2,1)S(1)}, bf16[144,256]{1,0:T(8,128)(2,1)S(1)}, u32[]{:S(2)}, u32[]{:S(2)}) %collective-permute-start.15) | collective-permute-done | bytes 73760 | tf_op jit(solution)/shard_map/ppermute | solution.py:161
  111.0 3.0 %collective-permute-done.17 = bf16[144,256]{1,0:T(8,128)(2,1)S(1)} collective-permute-done((bf16[144,256]{1,0:T(8,128)(2,1)S(1)}, bf16[144,256]{1,0:T(8,128)(2,1)S(1)}, u32[]{:S(2)}, u32[]{:S(2)}) %collective-permute-start.17) | collective-permute-done | bytes 73760 | tf_op jit(solution)/shard_map/ppermute | solution.py:161
  114.2 4.6 %collective-permute-start.22 = (bf16[144,256]{1,0:T(8,128)(2,1)S(1)}, bf16[144,256]{1,0:T(8,128)(2,1)S(1)}, u32[]{:S(2)}, u32[]{:S(2)}) collective-permute-start(bf16[144,256]{1,0:T(8,128)(2,1)S(1)} %add_convert_fusion.2), channel_id=1, source_target_pairs={{0,32},{8,40},{16,48},{24,56},{32,0},{40,8},{48,16},{56,24},{1,33}... | collective-permute-start | bytes 221192 | tf_op jit(solution)/shard_map/ppermute | solution.py:161
  118.9 3.5 %collective-permute-start.24 = (bf16[144,256]{1,0:T(8,128)(2,1)S(1)}, bf16[144,256]{1,0:T(8,128)(2,1)S(1)}, u32[]{:S(2)}, u32[]{:S(2)}) collective-permute-start(bf16[144,256]{1,0:T(8,128)(2,1)S(1)} %add_convert_fusion.2), channel_id=1, source_target_pairs={{0,48},{8,56},{16,0},{24,8},{32,16},{40,24},{48,32},{56,40},{1,49}... | collective-permute-start | bytes 221192 | tf_op jit(solution)/shard_map/ppermute | solution.py:161
  122.5 2.7 %collective-permute-start.20 = (bf16[256,256]{1,0:T(8,128)(2,1)S(1)}, bf16[256,256]{1,0:T(8,128)(2,1)S(1)}, u32[]{:S(2)}, u32[]{:S(2)}) collective-permute-start(bf16[256,256]{1,0:T(8,128)(2,1)S(1)} %get-tuple-element.42), channel_id=1, source_target_pairs={{0,6},{2,0},{4,2},{6,4},{1,7},{3,1},{5,3},{7,5},{8,14},{10,8},{12,... | collective-permute-start | bytes 393224 | tf_op jit(solution)/shard_map/ppermute | solution.py:161
  125.4 1.6 %collective-permute-done.23 = bf16[144,256]{1,0:T(8,128)(2,1)S(1)} collective-permute-done((bf16[144,256]{1,0:T(8,128)(2,1)S(1)}, bf16[144,256]{1,0:T(8,128)(2,1)S(1)}, u32[]{:S(2)}, u32[]{:S(2)}) %collective-permute-start.23) | collective-permute-done | bytes 73760 | tf_op jit(solution)/shard_map/ppermute | solution.py:161
  128.6 3.1 %collective-permute-done.21 = bf16[256,256]{1,0:T(8,128)(2,1)S(1)} collective-permute-done((bf16[256,256]{1,0:T(8,128)(2,1)S(1)}, bf16[256,256]{1,0:T(8,128)(2,1)S(1)}, u32[]{:S(2)}, u32[]{:S(2)}) %collective-permute-start.21) | collective-permute-done | bytes 131104 | tf_op jit(solution)/shard_map/ppermute | solution.py:161
  135.3 5.0 %all_gather.7 = f32[256,256]{1,0:T(8,128)S(1)} all-gather(f32[128,256]{1,0:T(8,128)S(1)} %slice_add_fusion), channel_id=1, replica_groups=mesh['x'=4,'z'=8,'y'=4,'c'=2] {'c'}, dimensions={0}, use_global_device_ids=true | all-gather | bytes 393216 | tf_op jit(solution)/shard_map/all_gather | solution.py:265
  (73 shorter events, 22.3 us)
Async XLA Ops:
  7.2 75.8 %all-gather.2.cloned.1.call-start = ((), (), s32[]{:S(2)}) async-start(), calls=%async_computation.1 | async-start | bytes 4718592 | tf_op jit(solution)/shard_map/all_gather | solution.py:205
  9.2 7.7 %collective-permute-start.3 = (bf16[2,256,128]{2,1,0:T(8,128)(2,1)S(1)}, bf16[2,256,128]{2,1,0:T(8,128)(2,1)S(1)}, u32[]{:S(2)}, u32[]{:S(2)}) collective-permute-start(bf16[2,256,128]{2,1,0:T(8,128)(2,1)S(1)} %bitcast.58), channel_id=1, source_target_pairs={{0,6},{2,0},{4,2},{6,4},{1,7},{3,1},{5,3},{7,5},{8,14},{10,8},{12,... | collective-permute-start | bytes 393224 | tf_op jit(solution)/shard_map/ppermute | solution.py:161
  12.8 6.2 %collective-permute-start.4 = (bf16[2,256,128]{2,1,0:T(8,128)(2,1)S(1)}, bf16[2,256,128]{2,1,0:T(8,128)(2,1)S(1)}, u32[]{:S(2)}, u32[]{:S(2)}) collective-permute-start(bf16[2,256,128]{2,1,0:T(8,128)(2,1)S(1)} %bitcast.59), channel_id=1, source_target_pairs={{0,4},{2,6},{4,0},{6,2},{1,5},{3,7},{5,1},{7,3},{8,12},{10,14},{12... | collective-permute-start | bytes 393224 | tf_op jit(solution)/shard_map/ppermute | solution.py:161
  13.2 9.3 %collective-permute-start.5 = (bf16[2,256,128]{2,1,0:T(8,128)(2,1)S(1)}, bf16[2,256,128]{2,1,0:T(8,128)(2,1)S(1)}, u32[]{:S(2)}, u32[]{:S(2)}) collective-permute-start(bf16[2,256,128]{2,1,0:T(8,128)(2,1)S(1)} %bitcast.60), channel_id=1, source_target_pairs={{0,2},{2,4},{4,6},{6,0},{1,3},{3,5},{5,7},{7,1},{8,10},{10,12},{12... | collective-permute-start | bytes 393224 | tf_op jit(solution)/shard_map/ppermute | solution.py:161
  13.9 8.7 %collective-permute-start = (bf16[2,128,256]{2,1,0:T(8,128)(2,1)S(1)}, bf16[2,128,256]{2,1,0:T(8,128)(2,1)S(1)}, u32[]{:S(2)}, u32[]{:S(2)}) collective-permute-start(bf16[2,128,256]{2,1,0:T(8,128)(2,1)S(1)} %bitcast.62), channel_id=1, source_target_pairs={{0,192},{64,0},{128,64},{192,128},{1,193},{65,1},{129,65},{193,129... | collective-permute-start | bytes 393224 | tf_op jit(solution)/shard_map/ppermute | solution.py:161
  16.3 6.2 %collective-permute-start.1 = (bf16[2,128,256]{2,1,0:T(8,128)(2,1)S(1)}, bf16[2,128,256]{2,1,0:T(8,128)(2,1)S(1)}, u32[]{:S(2)}, u32[]{:S(2)}) collective-permute-start(bf16[2,128,256]{2,1,0:T(8,128)(2,1)S(1)} %bitcast.63), channel_id=1, source_target_pairs={{0,128},{64,192},{128,0},{192,64},{1,129},{65,193},{129,1},{193,65... | collective-permute-start | bytes 393224 | tf_op jit(solution)/shard_map/ppermute | solution.py:161
  16.9 7.1 %collective-permute-start.2 = (bf16[2,128,256]{2,1,0:T(8,128)(2,1)S(1)}, bf16[2,128,256]{2,1,0:T(8,128)(2,1)S(1)}, u32[]{:S(2)}, u32[]{:S(2)}) collective-permute-start(bf16[2,128,256]{2,1,0:T(8,128)(2,1)S(1)} %bitcast.64), channel_id=1, source_target_pairs={{0,64},{64,128},{128,192},{192,0},{1,65},{65,129},{129,193},{193,1... | collective-permute-start | bytes 393224 | tf_op jit(solution)/shard_map/ppermute | solution.py:161
  24.8 108.3 %reduce-scatter.2.cloned.1.call-start = ((), (), s32[]{:S(2)}) async-start(), calls=%async_computation.2 | async-start | bytes 2359296 | tf_op jit(solution)/shard_map/reduce_scatter | solution.py:229
  37.1 25.3 %collective-permute-start.7 = (bf16[16,256,128]{2,1,0:T(8,128)(2,1)S(1)}, bf16[16,256,128]{2,1,0:T(8,128)(2,1)S(1)}, u32[]{:S(2)}, u32[]{:S(2)}) collective-permute-start(bf16[16,256,128]{2,1,0:T(8,128)(2,1)S(1)} %get-tuple-element.22), channel_id=1, source_target_pairs={{0,64},{64,128},{128,192},{192,0},{1,65},{65,129},{129,193},{193,1... | collective-permute-start | bytes 3145736 | tf_op jit(solution)/shard_map/ppermute | solution.py:161
  37.2 25.2 %collective-permute-start.8 = (bf16[16,256,128]{2,1,0:T(8,128)(2,1)S(1)}, bf16[16,256,128]{2,1,0:T(8,128)(2,1)S(1)}, u32[]{:S(2)}, u32[]{:S(2)}) collective-permute-start(bf16[16,256,128]{2,1,0:T(8,128)(2,1)S(1)} %get-tuple-element.23), channel_id=1, source_target_pairs={{0,192},{64,0},{128,64},{192,128},{1,193},{65,1},{129,65},{193,129... | collective-permute-start | bytes 3145736 | tf_op jit(solution)/shard_map/ppermute | solution.py:161
  62.6 12.0 %collective-permute-start.10 = (bf16[8,256,128]{2,1,0:T(8,128)(2,1)S(1)}, bf16[8,256,128]{2,1,0:T(8,128)(2,1)S(1)}, u32[]{:S(2)}, u32[]{:S(2)}) collective-permute-start(bf16[8,256,128]{2,1,0:T(8,128)(2,1)S(1)} %get-tuple-element.25), channel_id=1, source_target_pairs={{0,192},{64,0},{128,64},{192,128},{1,193},{65,1},{129,65},{193,129... | collective-permute-start | bytes 1572872 | tf_op jit(solution)/shard_map/ppermute | solution.py:161
  65.1 12.5 %collective-permute-start.9 = (bf16[8,256,128]{2,1,0:T(8,128)(2,1)S(1)}, bf16[8,256,128]{2,1,0:T(8,128)(2,1)S(1)}, u32[]{:S(2)}, u32[]{:S(2)}) collective-permute-start(bf16[8,256,128]{2,1,0:T(8,128)(2,1)S(1)} %get-tuple-element.24), channel_id=1, source_target_pairs={{0,64},{64,128},{128,192},{192,0},{1,65},{65,129},{129,193},{193,1... | collective-permute-start | bytes 1572872 | tf_op jit(solution)/shard_map/ppermute | solution.py:161
  95.8 6.8 %collective-permute-start.12 = (bf16[144,256]{1,0:T(8,128)(2,1)S(1)}, bf16[144,256]{1,0:T(8,128)(2,1)S(1)}, u32[]{:S(2)}, u32[]{:S(2)}) collective-permute-start(bf16[144,256]{1,0:T(8,128)(2,1)S(1)} %fusion.7), channel_id=1, source_target_pairs={{0,4},{2,6},{4,0},{6,2},{1,5},{3,7},{5,1},{7,3},{8,12},{10,14},{12... | collective-permute-start | bytes 221192 | tf_op jit(solution)/shard_map/ppermute | solution.py:161
  101.7 4.5 %collective-permute-start.14 = (bf16[144,256]{1,0:T(8,128)(2,1)S(1)}, bf16[144,256]{1,0:T(8,128)(2,1)S(1)}, u32[]{:S(2)}, u32[]{:S(2)}) collective-permute-start(bf16[144,256]{1,0:T(8,128)(2,1)S(1)} %fusion.7), channel_id=1, source_target_pairs={{0,2},{2,4},{4,6},{6,0},{1,3},{3,5},{5,7},{7,1},{8,10},{10,12},{12... | collective-permute-start | bytes 221192 | tf_op jit(solution)/shard_map/ppermute | solution.py:161
  101.8 12.3 %collective-permute-start.18 = (bf16[4,256,256]{2,1,0:T(8,128)(2,1)S(1)}, bf16[4,256,256]{2,1,0:T(8,128)(2,1)S(1)}, u32[]{:S(2)}, u32[]{:S(2)}) collective-permute-start(bf16[4,256,256]{2,1,0:T(8,128)(2,1)S(1)} %bitcast.57), channel_id=1, source_target_pairs={{0,1},{1,0},{2,3},{3,2},{4,5},{5,4},{6,7},{7,6},{8,9},{9,8},{10,11... | collective-permute-start | bytes 1572872 | tf_op jit(solution)/shard_map/ppermute | solution.py:177
  106.2 4.8 %collective-permute-start.15 = (bf16[144,256]{1,0:T(8,128)(2,1)S(1)}, bf16[144,256]{1,0:T(8,128)(2,1)S(1)}, u32[]{:S(2)}, u32[]{:S(2)}) collective-permute-start(bf16[144,256]{1,0:T(8,128)(2,1)S(1)} %add_convert_fusion.3), channel_id=1, source_target_pairs={{0,128},{64,192},{128,0},{192,64},{1,129},{65,193},{129,1},{193,65... | collective-permute-start | bytes 221192 | tf_op jit(solution)/shard_map/ppermute | solution.py:161
  108.4 5.6 %collective-permute-start.17 = (bf16[144,256]{1,0:T(8,128)(2,1)S(1)}, bf16[144,256]{1,0:T(8,128)(2,1)S(1)}, u32[]{:S(2)}, u32[]{:S(2)}) collective-permute-start(bf16[144,256]{1,0:T(8,128)(2,1)S(1)} %add_convert_fusion.3), channel_id=1, source_target_pairs={{0,64},{64,128},{128,192},{192,0},{1,65},{65,129},{129,193},{193,1... | collective-permute-start | bytes 221192 | tf_op jit(solution)/shard_map/ppermute | solution.py:161
  114.2 11.0 %collective-permute-start.22 = (bf16[144,256]{1,0:T(8,128)(2,1)S(1)}, bf16[144,256]{1,0:T(8,128)(2,1)S(1)}, u32[]{:S(2)}, u32[]{:S(2)}) collective-permute-start(bf16[144,256]{1,0:T(8,128)(2,1)S(1)} %add_convert_fusion.2), channel_id=1, source_target_pairs={{0,32},{8,40},{16,48},{24,56},{32,0},{40,8},{48,16},{56,24},{1,33}... | collective-permute-start | bytes 221192 | tf_op jit(solution)/shard_map/ppermute | solution.py:161
  118.8 8.3 %collective-permute-start.23 = (bf16[144,256]{1,0:T(8,128)(2,1)S(1)}, bf16[144,256]{1,0:T(8,128)(2,1)S(1)}, u32[]{:S(2)}, u32[]{:S(2)}) collective-permute-start(bf16[144,256]{1,0:T(8,128)(2,1)S(1)} %add_convert_fusion.2), channel_id=1, source_target_pairs={{0,16},{8,24},{16,32},{24,40},{32,48},{40,56},{48,0},{56,8},{1,17}... | collective-permute-start | bytes 221192 | tf_op jit(solution)/shard_map/ppermute | solution.py:161
  118.9 8.2 %collective-permute-start.24 = (bf16[144,256]{1,0:T(8,128)(2,1)S(1)}, bf16[144,256]{1,0:T(8,128)(2,1)S(1)}, u32[]{:S(2)}, u32[]{:S(2)}) collective-permute-start(bf16[144,256]{1,0:T(8,128)(2,1)S(1)} %add_convert_fusion.2), channel_id=1, source_target_pairs={{0,48},{8,56},{16,0},{24,8},{32,16},{40,24},{48,32},{56,40},{1,49}... | collective-permute-start | bytes 221192 | tf_op jit(solution)/shard_map/ppermute | solution.py:161
  122.5 5.5 %collective-permute-start.19 = (bf16[256,256]{1,0:T(8,128)(2,1)S(1)}, bf16[256,256]{1,0:T(8,128)(2,1)S(1)}, u32[]{:S(2)}, u32[]{:S(2)}) collective-permute-start(bf16[256,256]{1,0:T(8,128)(2,1)S(1)} %get-tuple-element.40), channel_id=1, source_target_pairs={{0,2},{2,4},{4,6},{6,0},{1,3},{3,5},{5,7},{7,1},{8,10},{10,12},{12... | collective-permute-start | bytes 393224 | tf_op jit(solution)/shard_map/ppermute | solution.py:161
  122.5 6.0 %collective-permute-start.20 = (bf16[256,256]{1,0:T(8,128)(2,1)S(1)}, bf16[256,256]{1,0:T(8,128)(2,1)S(1)}, u32[]{:S(2)}, u32[]{:S(2)}) collective-permute-start(bf16[256,256]{1,0:T(8,128)(2,1)S(1)} %get-tuple-element.42), channel_id=1, source_target_pairs={{0,6},{2,0},{4,2},{6,4},{1,7},{3,1},{5,3},{7,5},{8,14},{10,8},{12,... | collective-permute-start | bytes 393224 | tf_op jit(solution)/shard_map/ppermute | solution.py:161
  125.2 6.5 %collective-permute-start.21 = (bf16[256,256]{1,0:T(8,128)(2,1)S(1)}, bf16[256,256]{1,0:T(8,128)(2,1)S(1)}, u32[]{:S(2)}, u32[]{:S(2)}) collective-permute-start(bf16[256,256]{1,0:T(8,128)(2,1)S(1)} %get-tuple-element.41), channel_id=1, source_target_pairs={{0,4},{2,6},{4,0},{6,2},{1,5},{3,7},{5,1},{7,3},{8,12},{10,14},{12... | collective-permute-start | bytes 393224 | tf_op jit(solution)/shard_map/ppermute | solution.py:161
  127.1 5.5 %collective-permute-start.25 = (f32[144,256]{1,0:T(8,128)S(1)}, f32[144,256]{1,0:T(8,128)S(1)}, u32[]{:S(2)}, u32[]{:S(2)}) collective-permute-start(f32[144,256]{1,0:T(8,128)S(1)} %add_add_fusion), channel_id=1, source_target_pairs={{0,8},{8,0},{16,24},{24,16},{32,40},{40,32},{48,56},{56,48},{1,9},... | collective-permute-start | bytes 442376 | tf_op jit(solution)/shard_map/ppermute | solution.py:249
  (8 other events, 198.4 us)
Sparse Core Ops, SparseCore 0:
  24.9 57.9 all-gather.1
  85.5 39.3 reduce-scatter.1

commit v5 on v4

--- a/solution.py
+++ b/solution.py
@@ -63,15 +63,16 @@
 
     @pl.when(pl.program_id(0) == pl.num_programs(0) - 1)
     def _():
-        total[...] = jnp.zeros(total.shape, F32)
-
-        def finish(i, carry):
-            block = acc[i].astype(BF16)
-            out[i] = block
-            total[...] += jnp.dot(cot_t[i], block, preferred_element_type=F32)
-            return carry
-
-        lax.fori_loop(0, BAND, finish, 0)
+        for first in (0, BAND // 2):
+            products = []
+            for i in range(first, first + BAND // 2, 2):
+                out[i] = acc[i].astype(BF16)
+                out[i + 1] = acc[i + 1].astype(BF16)
+                left = jnp.concatenate([cot_t[i], cot_t[i + 1]], axis=1)
+                right = jnp.concatenate([out[i], out[i + 1]], axis=0)
+                products.append(jnp.dot(left, right, preferred_element_type=F32))
+            product = (products[0] + products[1]) + (products[2] + products[3])
+            total[...] = product if first == 0 else total[...] + product
         total[...] = total[...].T
         for q in range(NC):
             to = q ^ info[1]
@@ -241,14 +242,11 @@
         own, up, across, down = (value.astype(F32) for value in gather4(part, axis))
         part = ((own + across) + (up + down)).astype(BF16)
     half = band_terms[0].astype(F32) + swap(band_terms[1]).astype(F32)
-    part, half = lax.optimization_barrier((part, half))
     own, up, down, across = (
         value.astype(F32) for value in [part] + [shift(part, "z", NZ, by) for by in (2, -2, 4)]
     )
-    part = (own + across) + (up + down)
-    other = lax.ppermute(part, "z", [(i, i ^ 1) for i in range(NZ)])
-    grad_bias = part[TILE] + other[TILE]
-    part = part[:TILE] + other[:TILE]
+    part, half = lax.optimization_barrier(((own + across) + (up + down), half))
+    paired = lax.ppermute(part, "z", [(i, i ^ 1) for i in range(NZ)])
 
     half16 = half.astype(BF16)
     total = half[0]
@@ -261,7 +259,9 @@
         "ahn,gh->ang", own_z, weight.astype(F32), precision=lax.Precision.HIGHEST
     ).reshape(2 * TILE, H)
     grad_features = (grad_features * inv_root[:, None]).astype(BF16)
-    part, grad_features = lax.optimization_barrier((part, grad_features))
+    paired, grad_features = lax.optimization_barrier((paired, grad_features))
+    grad_bias = part[TILE] + paired[TILE]
+    part = part[:TILE] + paired[:TILE]
     grad_weight = lax.all_gather(part, "c", axis=0, tiled=True)
     return (layer_out, grad_weight, grad_bias, grad_features)
 

time: 149 us -> 151 us (1.013)
  starting transfers between devices: 39.2 us -> 42.9 us
    ppermute x3, starting transfers between devices: 4.67 us -> 6.69 us  [swap(): return lax.ppermute(value, 'c', [(0, 1), (1, 0)])]
    all_gather x1, waiting for transfers between devices: 3.44 us -> 1.59 us  [shards(): feats = lax.all_gather(near, 'z', axis=0, tiled=True)]
    ppermute x22, starting transfers between devices: 34.3 us -> 36.2 us  [shift(): lax.ppermute(value, axis, [(i, (i + by) % size) for i in range(size)])]
    pallas_call x1, Pallas kernels: 10.5 us -> 8.96 us  [forward_tiles(): pl.pallas_call(forward_kernel, grid_spec=pltpu.PrefetchScalarGridSpec(num...]
  transfers between devices with their start and end apart: 28 -> 28, of which waited for: 16 -> 17; matrix products, arithmetic and copies ran while one was open for 3% -> 4% of each run, Pallas kernels for 12% -> 11%
where the time goes in v5:
time: 151 us; the launch traced here: 150 us
  waiting for transfers between devices  60.3 us (40%)
  starting transfers between devices  42.9 us (28%)
  Pallas kernels  17 us (11%)
  between operations  14.9 us (10%)
  other arithmetic  5.94 us (4%)
  blocking collectives  5.25 us (3%)
  local copies, waits for them, and re-layouts  2.16 us (1%)
  matrix products  1.89 us (1%)
    ppermute x22, waiting for transfers between devices, shift(): lax.ppermute(value, axis, [(i, (i + by) % size) for i in range(size)])  56.2 us
    ppermute x22, starting transfers between devices, shift(): lax.ppermute(value, axis, [(i, (i + by) % size) for i in range(size)])  36.2 us
    pallas_call x1, Pallas kernels, forward_tiles(): pl.pallas_call(forward_kernel, grid_spec=pltpu.PrefetchScalarGridSpec(num...  8.96 us
    pallas_call x1, Pallas kernels, backward_tiles(): pl.pallas_call(backward_kernel, grid_spec=pltpu.PrefetchScalarGridSpec(nu...  8.06 us
    ppermute x3, starting transfers between devices, swap(): return lax.ppermute(value, 'c', [(0, 1), (1, 0)])  6.69 us
    all_gather x1, blocking collectives, shards(): grad_weight = lax.all_gather(part, 'c', axis=0, tiled=True)  5.25 us
  transfers between devices with their start and end apart: 28, of which 17 were waited for; matrix products, arithmetic and copies ran while one was open for 4% of the time, Pallas kernels for 11%

profile of v5, /device:TPU:1, one launch (start us, length us, event | category | flops | bytes accessed | tf_op | source)
XLA Modules:
  0.0 150.4 jit_solution(3827980315274120919)
XLA Ops:
  9.2 3.6 %collective-permute-start.3 = (bf16[2,256,128]{2,1,0:T(8,128)(2,1)S(1)}, bf16[2,256,128]{2,1,0:T(8,128)(2,1)S(1)}, u32[]{:S(2)}, u32[]{:S(2)}) collective-permute-start(bf16[2,256,128]{2,1,0:T(8,128)(2,1)S(1)} %bitcast.58), channel_id=1, source_target_pairs={{0,6},{2,0},{4,2},{6,4},{1,7},{3,1},{5,3},{7,5},{8,14},{10,8},{12,... | collective-permute-start | bytes 393224 | tf_op jit(solution)/shard_map/ppermute | solution.py:162
  13.9 2.5 %collective-permute-start = (bf16[2,128,256]{2,1,0:T(8,128)(2,1)S(1)}, bf16[2,128,256]{2,1,0:T(8,128)(2,1)S(1)}, u32[]{:S(2)}, u32[]{:S(2)}) collective-permute-start(bf16[2,128,256]{2,1,0:T(8,128)(2,1)S(1)} %bitcast.62), channel_id=1, source_target_pairs={{0,192},{64,0},{128,64},{192,128},{1,193},{65,1},{129,65},{193,129... | collective-permute-start | bytes 393224 | tf_op jit(solution)/shard_map/ppermute | solution.py:162
  16.9 2.2 %collective-permute-start.2 = (bf16[2,128,256]{2,1,0:T(8,128)(2,1)S(1)}, bf16[2,128,256]{2,1,0:T(8,128)(2,1)S(1)}, u32[]{:S(2)}, u32[]{:S(2)}) collective-permute-start(bf16[2,128,256]{2,1,0:T(8,128)(2,1)S(1)} %bitcast.64), channel_id=1, source_target_pairs={{0,64},{64,128},{128,192},{192,0},{1,65},{65,129},{129,193},{193,1... | collective-permute-start | bytes 393224 | tf_op jit(solution)/shard_map/ppermute | solution.py:162
  19.0 3.4 %collective-permute-done.5 = bf16[2,256,128]{2,1,0:T(8,128)(2,1)S(1)} collective-permute-done((bf16[2,256,128]{2,1,0:T(8,128)(2,1)S(1)}, bf16[2,256,128]{2,1,0:T(8,128)(2,1)S(1)}, u32[]{:S(2)}, u32[]{:S(2)}) %collective-permute-start.5) | collective-permute-done | bytes 131104 | tf_op jit(solution)/shard_map/ppermute | solution.py:162
  25.6 2.7 %collective-permute-start.6 = (bf16[8,256,128]{2,1,0:T(8,128)(2,1)S(1)}, bf16[8,256,128]{2,1,0:T(8,128)(2,1)S(1)}, u32[]{:S(2)}, u32[]{:S(2)}) collective-permute-start(bf16[8,256,128]{2,1,0:T(8,128)(2,1)S(1)} %pad_maximum_fusion.2), channel_id=1, source_target_pairs={{0,1},{1,0},{2,3},{3,2},{4,5},{5,4},{6,7},{7,6},{8,9},{9,8},{10,11... | collective-permute-start | bytes 1572872 | tf_op jit(solution)/shard_map/ppermute | solution.py:178
  29.9 8.1 %backward_tiles.1 = (bf16[16,256,128]{2,1,0:T(8,128)(2,1)S(1)}, bf16[16,256,128]{2,1,0:T(8,128)(2,1)S(1)}, bf16[32,256,128]{2,1,0:T(8,128)(2,1)S(1)}) custom-call(s32[192]{0:T(256)S(1)} %bitcast.46, s32[192]{0:T(256)S(1)} %bitcast.50, s32[2]{0:T(128)S(1)} %pad_add_fusion.count.info, bf16[192,128,128]{2,1,0:T(8,128)(2,1)} %bitcast.51, ...), custom_call_target="tpu_custom_call" | custom-call | flops 1610612736 | bytes 12582912 | tf_op jit(solution)/shard_map/backward_tiles/pallas_call | solution.py:143
  38.0 2.7 %collective-permute-start.8 = (bf16[16,256,128]{2,1,0:T(8,128)(2,1)S(1)}, bf16[16,256,128]{2,1,0:T(8,128)(2,1)S(1)}, u32[]{:S(2)}, u32[]{:S(2)}) collective-permute-start(bf16[16,256,128]{2,1,0:T(8,128)(2,1)S(1)} %get-tuple-element.23), channel_id=1, source_target_pairs={{0,192},{64,0},{128,64},{192,128},{1,193},{65,1},{129,65},{193,129... | collective-permute-start | bytes 3145736 | tf_op jit(solution)/shard_map/ppermute | solution.py:162
  40.7 23.0 %collective-permute-done.7 = bf16[16,256,128]{2,1,0:T(8,128)(2,1)S(1)} collective-permute-done((bf16[16,256,128]{2,1,0:T(8,128)(2,1)S(1)}, bf16[16,256,128]{2,1,0:T(8,128)(2,1)S(1)}, u32[]{:S(2)}, u32[]{:S(2)}) %collective-permute-start.7) | collective-permute-done | bytes 1048608 | tf_op jit(solution)/shard_map/ppermute | solution.py:162
  64.0 2.4 %collective-permute-start.10 = (bf16[8,256,128]{2,1,0:T(8,128)(2,1)S(1)}, bf16[8,256,128]{2,1,0:T(8,128)(2,1)S(1)}, u32[]{:S(2)}, u32[]{:S(2)}) collective-permute-start(bf16[8,256,128]{2,1,0:T(8,128)(2,1)S(1)} %get-tuple-element.25), channel_id=1, source_target_pairs={{0,192},{64,0},{128,64},{192,128},{1,193},{65,1},{129,65},{193,129... | collective-permute-start | bytes 1572872 | tf_op jit(solution)/shard_map/ppermute | solution.py:162
  66.4 10.1 %collective-permute-done.10 = bf16[8,256,128]{2,1,0:T(8,128)(2,1)S(1)} collective-permute-done((bf16[8,256,128]{2,1,0:T(8,128)(2,1)S(1)}, bf16[8,256,128]{2,1,0:T(8,128)(2,1)S(1)}, u32[]{:S(2)}, u32[]{:S(2)}) %collective-permute-start.10) | collective-permute-done | bytes 524320 | tf_op jit(solution)/shard_map/ppermute | solution.py:162
  76.5 3.0 %collective-permute-done.9 = bf16[8,256,128]{2,1,0:T(8,128)(2,1)S(1)} collective-permute-done((bf16[8,256,128]{2,1,0:T(8,128)(2,1)S(1)}, bf16[8,256,128]{2,1,0:T(8,128)(2,1)S(1)}, u32[]{:S(2)}, u32[]{:S(2)}) %collective-permute-start.9) | collective-permute-done | bytes 524320 | tf_op jit(solution)/shard_map/ppermute | solution.py:162
  81.4 1.6 %all-gather.2.cloned.1.call-done.feats = bf16[64,128,256]{2,1,0:T(8,128)(2,1)} async-done(((bf16[8,128,256]{2,1,0:T(8,128)(2,1)}), bf16[64,128,256]{2,1,0:T(8,128)(2,1)}) %all-gather.2.cloned.1.call-update) | async-done | bytes 4194320 | tf_op jit(solution)/shard_map/all_gather | solution.py:206
  83.0 9.0 %forward_tiles.1 = (bf16[16,128,256]{2,1,0:T(8,128)(2,1)S(1)}, f32[2,144,256]{2,1,0:T(8,128)S(1)}) custom-call(s32[192]{0:T(256)S(1)} %bitcast.47, s32[192]{0:T(256)S(1)} %bitcast.49, s32[2]{0:T(128)S(1)} %pad_add_fusion.count.info, bf16[192,128,128]{2,1,0:T(8,128)(2,1)} %bitcast.52, bf16[64,128,256]{2,1,0:T(8,128)(2,1)} %all-gather.2.cloned.1.call-done.feats, ...), custom_call_target="tpu_custom_call" | custom-call | flops 1610612736 | bytes 12582912 | tf_op jit(solution)/shard_map/forward_tiles/pallas_call | solution.py:118
  94.0 2.6 %collective-permute-start.12 = (bf16[144,256]{1,0:T(8,128)(2,1)S(1)}, bf16[144,256]{1,0:T(8,128)(2,1)S(1)}, u32[]{:S(2)}, u32[]{:S(2)}) collective-permute-start(bf16[144,256]{1,0:T(8,128)(2,1)S(1)} %fusion.7), channel_id=1, source_target_pairs={{0,4},{2,6},{4,0},{6,2},{1,5},{3,7},{5,1},{7,3},{8,12},{10,14},{12... | collective-permute-start | bytes 221192 | tf_op jit(solution)/shard_map/ppermute | solution.py:162
  100.2 2.3 %collective-permute-done.14 = bf16[144,256]{1,0:T(8,128)(2,1)S(1)} collective-permute-done((bf16[144,256]{1,0:T(8,128)(2,1)S(1)}, bf16[144,256]{1,0:T(8,128)(2,1)S(1)}, u32[]{:S(2)}, u32[]{:S(2)}) %collective-permute-start.14) | collective-permute-done | bytes 73760 | tf_op jit(solution)/shard_map/ppermute | solution.py:162
  102.5 2.6 %collective-permute-start.15 = (bf16[144,256]{1,0:T(8,128)(2,1)S(1)}, bf16[144,256]{1,0:T(8,128)(2,1)S(1)}, u32[]{:S(2)}, u32[]{:S(2)}) collective-permute-start(bf16[144,256]{1,0:T(8,128)(2,1)S(1)} %add_convert_fusion.3), channel_id=1, source_target_pairs={{0,128},{64,192},{128,0},{192,64},{1,129},{65,193},{129,1},{193,65... | collective-permute-start | bytes 221192 | tf_op jit(solution)/shard_map/ppermute | solution.py:162
  106.7 3.0 %collective-permute-start.21 = (bf16[4,256,256]{2,1,0:T(8,128)(2,1)S(1)}, bf16[4,256,256]{2,1,0:T(8,128)(2,1)S(1)}, u32[]{:S(2)}, u32[]{:S(2)}) collective-permute-start(bf16[4,256,256]{2,1,0:T(8,128)(2,1)S(1)} %bitcast.57), channel_id=1, source_target_pairs={{0,1},{1,0},{2,3},{3,2},{4,5},{5,4},{6,7},{7,6},{8,9},{9,8},{10,11... | collective-permute-start | bytes 1572872 | tf_op jit(solution)/shard_map/ppermute | solution.py:178
  110.4 3.6 %collective-permute-start.18 = (bf16[144,256]{1,0:T(8,128)(2,1)S(1)}, bf16[144,256]{1,0:T(8,128)(2,1)S(1)}, u32[]{:S(2)}, u32[]{:S(2)}) collective-permute-start(bf16[144,256]{1,0:T(8,128)(2,1)S(1)} %add_convert_fusion.2), channel_id=1, source_target_pairs={{0,32},{8,40},{16,48},{24,56},{32,0},{40,8},{48,16},{56,24},{1,33}... | collective-permute-start | bytes 221192 | tf_op jit(solution)/shard_map/ppermute | solution.py:162
  114.7 3.0 %collective-permute-start.20 = (bf16[144,256]{1,0:T(8,128)(2,1)S(1)}, bf16[144,256]{1,0:T(8,128)(2,1)S(1)}, u32[]{:S(2)}, u32[]{:S(2)}) collective-permute-start(bf16[144,256]{1,0:T(8,128)(2,1)S(1)} %add_convert_fusion.2), channel_id=1, source_target_pairs={{0,48},{8,56},{16,0},{24,8},{32,16},{40,24},{48,32},{56,40},{1,49}... | collective-permute-start | bytes 221192 | tf_op jit(solution)/shard_map/ppermute | solution.py:162
  119.1 4.5 %collective-permute-done.19 = bf16[144,256]{1,0:T(8,128)(2,1)S(1)} collective-permute-done((bf16[144,256]{1,0:T(8,128)(2,1)S(1)}, bf16[144,256]{1,0:T(8,128)(2,1)S(1)}, u32[]{:S(2)}, u32[]{:S(2)}) %collective-permute-start.19) | collective-permute-done | bytes 73760 | tf_op jit(solution)/shard_map/ppermute | solution.py:162
  124.0 3.3 %collective-permute-start.23 = (bf16[256,256]{1,0:T(8,128)(2,1)S(1)}, bf16[256,256]{1,0:T(8,128)(2,1)S(1)}, u32[]{:S(2)}, u32[]{:S(2)}) collective-permute-start(bf16[256,256]{1,0:T(8,128)(2,1)S(1)} %get-tuple-element.42), channel_id=1, source_target_pairs={{0,6},{2,0},{4,2},{6,4},{1,7},{3,1},{5,3},{7,5},{8,14},{10,8},{12,... | collective-permute-start | bytes 393224 | tf_op jit(solution)/shard_map/ppermute | solution.py:162
  127.3 2.4 %collective-permute-start.24 = (bf16[256,256]{1,0:T(8,128)(2,1)S(1)}, bf16[256,256]{1,0:T(8,128)(2,1)S(1)}, u32[]{:S(2)}, u32[]{:S(2)}) collective-permute-start(bf16[256,256]{1,0:T(8,128)(2,1)S(1)} %get-tuple-element.41), channel_id=1, source_target_pairs={{0,4},{2,6},{4,0},{6,2},{1,5},{3,7},{5,1},{7,3},{8,12},{10,14},{12... | collective-permute-start | bytes 393224 | tf_op jit(solution)/shard_map/ppermute | solution.py:162
  130.3 3.7 %collective-permute-done.24 = bf16[256,256]{1,0:T(8,128)(2,1)S(1)} collective-permute-done((bf16[256,256]{1,0:T(8,128)(2,1)S(1)}, bf16[256,256]{1,0:T(8,128)(2,1)S(1)}, u32[]{:S(2)}, u32[]{:S(2)}) %collective-permute-start.24) | collective-permute-done | bytes 131104 | tf_op jit(solution)/shard_map/ppermute | solution.py:162
  137.6 5.3 %all_gather.7 = f32[256,256]{1,0:T(8,128)S(1)} all-gather(f32[128,256]{1,0:T(8,128)S(1)} %slice_add_fusion), channel_id=1, replica_groups=mesh['x'=4,'z'=8,'y'=4,'c'=2] {'c'}, dimensions={0}, use_global_device_ids=true | all-gather | bytes 393216 | tf_op jit(solution)/shard_map/all_gather | solution.py:265
  (73 shorter events, 25.1 us)
Async XLA Ops:
  7.2 75.8 %all-gather.2.cloned.1.call-start = ((), (), s32[]{:S(2)}) async-start(), calls=%async_computation.1 | async-start | bytes 4718592 | tf_op jit(solution)/shard_map/all_gather | solution.py:206
  9.2 7.7 %collective-permute-start.3 = (bf16[2,256,128]{2,1,0:T(8,128)(2,1)S(1)}, bf16[2,256,128]{2,1,0:T(8,128)(2,1)S(1)}, u32[]{:S(2)}, u32[]{:S(2)}) collective-permute-start(bf16[2,256,128]{2,1,0:T(8,128)(2,1)S(1)} %bitcast.58), channel_id=1, source_target_pairs={{0,6},{2,0},{4,2},{6,4},{1,7},{3,1},{5,3},{7,5},{8,14},{10,8},{12,... | collective-permute-start | bytes 393224 | tf_op jit(solution)/shard_map/ppermute | solution.py:162
  12.8 6.2 %collective-permute-start.4 = (bf16[2,256,128]{2,1,0:T(8,128)(2,1)S(1)}, bf16[2,256,128]{2,1,0:T(8,128)(2,1)S(1)}, u32[]{:S(2)}, u32[]{:S(2)}) collective-permute-start(bf16[2,256,128]{2,1,0:T(8,128)(2,1)S(1)} %bitcast.59), channel_id=1, source_target_pairs={{0,4},{2,6},{4,0},{6,2},{1,5},{3,7},{5,1},{7,3},{8,12},{10,14},{12... | collective-permute-start | bytes 393224 | tf_op jit(solution)/shard_map/ppermute | solution.py:162
  13.2 9.3 %collective-permute-start.5 = (bf16[2,256,128]{2,1,0:T(8,128)(2,1)S(1)}, bf16[2,256,128]{2,1,0:T(8,128)(2,1)S(1)}, u32[]{:S(2)}, u32[]{:S(2)}) collective-permute-start(bf16[2,256,128]{2,1,0:T(8,128)(2,1)S(1)} %bitcast.60), channel_id=1, source_target_pairs={{0,2},{2,4},{4,6},{6,0},{1,3},{3,5},{5,7},{7,1},{8,10},{10,12},{12... | collective-permute-start | bytes 393224 | tf_op jit(solution)/shard_map/ppermute | solution.py:162
  13.9 8.7 %collective-permute-start = (bf16[2,128,256]{2,1,0:T(8,128)(2,1)S(1)}, bf16[2,128,256]{2,1,0:T(8,128)(2,1)S(1)}, u32[]{:S(2)}, u32[]{:S(2)}) collective-permute-start(bf16[2,128,256]{2,1,0:T(8,128)(2,1)S(1)} %bitcast.62), channel_id=1, source_target_pairs={{0,192},{64,0},{128,64},{192,128},{1,193},{65,1},{129,65},{193,129... | collective-permute-start | bytes 393224 | tf_op jit(solution)/shard_map/ppermute | solution.py:162
  16.3 6.2 %collective-permute-start.1 = (bf16[2,128,256]{2,1,0:T(8,128)(2,1)S(1)}, bf16[2,128,256]{2,1,0:T(8,128)(2,1)S(1)}, u32[]{:S(2)}, u32[]{:S(2)}) collective-permute-start(bf16[2,128,256]{2,1,0:T(8,128)(2,1)S(1)} %bitcast.63), channel_id=1, source_target_pairs={{0,128},{64,192},{128,0},{192,64},{1,129},{65,193},{129,1},{193,65... | collective-permute-start | bytes 393224 | tf_op jit(solution)/shard_map/ppermute | solution.py:162
  16.9 7.1 %collective-permute-start.2 = (bf16[2,128,256]{2,1,0:T(8,128)(2,1)S(1)}, bf16[2,128,256]{2,1,0:T(8,128)(2,1)S(1)}, u32[]{:S(2)}, u32[]{:S(2)}) collective-permute-start(bf16[2,128,256]{2,1,0:T(8,128)(2,1)S(1)} %bitcast.64), channel_id=1, source_target_pairs={{0,64},{64,128},{128,192},{192,0},{1,65},{65,129},{129,193},{193,1... | collective-permute-start | bytes 393224 | tf_op jit(solution)/shard_map/ppermute | solution.py:162
  24.8 110.1 %reduce-scatter.2.cloned.1.call-start = ((), (), s32[]{:S(2)}) async-start(), calls=%async_computation.2 | async-start | bytes 2359296 | tf_op jit(solution)/shard_map/reduce_scatter | solution.py:230
  37.9 25.8 %collective-permute-start.7 = (bf16[16,256,128]{2,1,0:T(8,128)(2,1)S(1)}, bf16[16,256,128]{2,1,0:T(8,128)(2,1)S(1)}, u32[]{:S(2)}, u32[]{:S(2)}) collective-permute-start(bf16[16,256,128]{2,1,0:T(8,128)(2,1)S(1)} %get-tuple-element.22), channel_id=1, source_target_pairs={{0,64},{64,128},{128,192},{192,0},{1,65},{65,129},{129,193},{193,1... | collective-permute-start | bytes 3145736 | tf_op jit(solution)/shard_map/ppermute | solution.py:162
  38.0 25.7 %collective-permute-start.8 = (bf16[16,256,128]{2,1,0:T(8,128)(2,1)S(1)}, bf16[16,256,128]{2,1,0:T(8,128)(2,1)S(1)}, u32[]{:S(2)}, u32[]{:S(2)}) collective-permute-start(bf16[16,256,128]{2,1,0:T(8,128)(2,1)S(1)} %get-tuple-element.23), channel_id=1, source_target_pairs={{0,192},{64,0},{128,64},{192,128},{1,193},{65,1},{129,65},{193,129... | collective-permute-start | bytes 3145736 | tf_op jit(solution)/shard_map/ppermute | solution.py:162
  64.0 12.5 %collective-permute-start.10 = (bf16[8,256,128]{2,1,0:T(8,128)(2,1)S(1)}, bf16[8,256,128]{2,1,0:T(8,128)(2,1)S(1)}, u32[]{:S(2)}, u32[]{:S(2)}) collective-permute-start(bf16[8,256,128]{2,1,0:T(8,128)(2,1)S(1)} %get-tuple-element.25), channel_id=1, source_target_pairs={{0,192},{64,0},{128,64},{192,128},{1,193},{65,1},{129,65},{193,129... | collective-permute-start | bytes 1572872 | tf_op jit(solution)/shard_map/ppermute | solution.py:162
  66.4 13.0 %collective-permute-start.9 = (bf16[8,256,128]{2,1,0:T(8,128)(2,1)S(1)}, bf16[8,256,128]{2,1,0:T(8,128)(2,1)S(1)}, u32[]{:S(2)}, u32[]{:S(2)}) collective-permute-start(bf16[8,256,128]{2,1,0:T(8,128)(2,1)S(1)} %get-tuple-element.24), channel_id=1, source_target_pairs={{0,64},{64,128},{128,192},{192,0},{1,65},{65,129},{129,193},{193,1... | collective-permute-start | bytes 1572872 | tf_op jit(solution)/shard_map/ppermute | solution.py:162
  94.0 4.8 %collective-permute-start.12 = (bf16[144,256]{1,0:T(8,128)(2,1)S(1)}, bf16[144,256]{1,0:T(8,128)(2,1)S(1)}, u32[]{:S(2)}, u32[]{:S(2)}) collective-permute-start(bf16[144,256]{1,0:T(8,128)(2,1)S(1)} %fusion.7), channel_id=1, source_target_pairs={{0,4},{2,6},{4,0},{6,2},{1,5},{3,7},{5,1},{7,3},{8,12},{10,14},{12... | collective-permute-start | bytes 221192 | tf_op jit(solution)/shard_map/ppermute | solution.py:162
  102.5 7.2 %collective-permute-start.15 = (bf16[144,256]{1,0:T(8,128)(2,1)S(1)}, bf16[144,256]{1,0:T(8,128)(2,1)S(1)}, u32[]{:S(2)}, u32[]{:S(2)}) collective-permute-start(bf16[144,256]{1,0:T(8,128)(2,1)S(1)} %add_convert_fusion.3), channel_id=1, source_target_pairs={{0,128},{64,192},{128,0},{192,64},{1,129},{65,193},{129,1},{193,65... | collective-permute-start | bytes 221192 | tf_op jit(solution)/shard_map/ppermute | solution.py:162
  105.2 4.6 %collective-permute-start.16 = (bf16[144,256]{1,0:T(8,128)(2,1)S(1)}, bf16[144,256]{1,0:T(8,128)(2,1)S(1)}, u32[]{:S(2)}, u32[]{:S(2)}) collective-permute-start(bf16[144,256]{1,0:T(8,128)(2,1)S(1)} %add_convert_fusion.3), channel_id=1, source_target_pairs={{0,192},{64,0},{128,64},{192,128},{1,193},{65,1},{129,65},{193,129... | collective-permute-start | bytes 221192 | tf_op jit(solution)/shard_map/ppermute | solution.py:162
  105.2 5.2 %collective-permute-start.17 = (bf16[144,256]{1,0:T(8,128)(2,1)S(1)}, bf16[144,256]{1,0:T(8,128)(2,1)S(1)}, u32[]{:S(2)}, u32[]{:S(2)}) collective-permute-start(bf16[144,256]{1,0:T(8,128)(2,1)S(1)} %add_convert_fusion.3), channel_id=1, source_target_pairs={{0,64},{64,128},{128,192},{192,0},{1,65},{65,129},{129,193},{193,1... | collective-permute-start | bytes 221192 | tf_op jit(solution)/shard_map/ppermute | solution.py:162
  106.7 17.0 %collective-permute-start.21 = (bf16[4,256,256]{2,1,0:T(8,128)(2,1)S(1)}, bf16[4,256,256]{2,1,0:T(8,128)(2,1)S(1)}, u32[]{:S(2)}, u32[]{:S(2)}) collective-permute-start(bf16[4,256,256]{2,1,0:T(8,128)(2,1)S(1)} %bitcast.57), channel_id=1, source_target_pairs={{0,1},{1,0},{2,3},{3,2},{4,5},{5,4},{6,7},{7,6},{8,9},{9,8},{10,11... | collective-permute-start | bytes 1572872 | tf_op jit(solution)/shard_map/ppermute | solution.py:178
  110.4 8.7 %collective-permute-start.18 = (bf16[144,256]{1,0:T(8,128)(2,1)S(1)}, bf16[144,256]{1,0:T(8,128)(2,1)S(1)}, u32[]{:S(2)}, u32[]{:S(2)}) collective-permute-start(bf16[144,256]{1,0:T(8,128)(2,1)S(1)} %add_convert_fusion.2), channel_id=1, source_target_pairs={{0,32},{8,40},{16,48},{24,56},{32,0},{40,8},{48,16},{56,24},{1,33}... | collective-permute-start | bytes 221192 | tf_op jit(solution)/shard_map/ppermute | solution.py:162
  114.0 9.6 %collective-permute-start.19 = (bf16[144,256]{1,0:T(8,128)(2,1)S(1)}, bf16[144,256]{1,0:T(8,128)(2,1)S(1)}, u32[]{:S(2)}, u32[]{:S(2)}) collective-permute-start(bf16[144,256]{1,0:T(8,128)(2,1)S(1)} %add_convert_fusion.2), channel_id=1, source_target_pairs={{0,16},{8,24},{16,32},{24,40},{32,48},{40,56},{48,0},{56,8},{1,17}... | collective-permute-start | bytes 221192 | tf_op jit(solution)/shard_map/ppermute | solution.py:162
  114.7 9.0 %collective-permute-start.20 = (bf16[144,256]{1,0:T(8,128)(2,1)S(1)}, bf16[144,256]{1,0:T(8,128)(2,1)S(1)}, u32[]{:S(2)}, u32[]{:S(2)}) collective-permute-start(bf16[144,256]{1,0:T(8,128)(2,1)S(1)} %add_convert_fusion.2), channel_id=1, source_target_pairs={{0,48},{8,56},{16,0},{24,8},{32,16},{40,24},{48,32},{56,40},{1,49}... | collective-permute-start | bytes 221192 | tf_op jit(solution)/shard_map/ppermute | solution.py:162
  123.9 6.1 %collective-permute-start.22 = (bf16[256,256]{1,0:T(8,128)(2,1)S(1)}, bf16[256,256]{1,0:T(8,128)(2,1)S(1)}, u32[]{:S(2)}, u32[]{:S(2)}) collective-permute-start(bf16[256,256]{1,0:T(8,128)(2,1)S(1)} %get-tuple-element.40), channel_id=1, source_target_pairs={{0,2},{2,4},{4,6},{6,0},{1,3},{3,5},{5,7},{7,1},{8,10},{10,12},{12... | collective-permute-start | bytes 393224 | tf_op jit(solution)/shard_map/ppermute | solution.py:162
  124.0 6.3 %collective-permute-start.23 = (bf16[256,256]{1,0:T(8,128)(2,1)S(1)}, bf16[256,256]{1,0:T(8,128)(2,1)S(1)}, u32[]{:S(2)}, u32[]{:S(2)}) collective-permute-start(bf16[256,256]{1,0:T(8,128)(2,1)S(1)} %get-tuple-element.42), channel_id=1, source_target_pairs={{0,6},{2,0},{4,2},{6,4},{1,7},{3,1},{5,3},{7,5},{8,14},{10,8},{12,... | collective-permute-start | bytes 393224 | tf_op jit(solution)/shard_map/ppermute | solution.py:162
  127.3 6.7 %collective-permute-start.24 = (bf16[256,256]{1,0:T(8,128)(2,1)S(1)}, bf16[256,256]{1,0:T(8,128)(2,1)S(1)}, u32[]{:S(2)}, u32[]{:S(2)}) collective-permute-start(bf16[256,256]{1,0:T(8,128)(2,1)S(1)} %get-tuple-element.41), channel_id=1, source_target_pairs={{0,4},{2,6},{4,0},{6,2},{1,5},{3,7},{5,1},{7,3},{8,12},{10,14},{12... | collective-permute-start | bytes 393224 | tf_op jit(solution)/shard_map/ppermute | solution.py:162
  129.7 7.3 %collective-permute-start.25 = (f32[144,256]{1,0:T(8,128)S(1)}, f32[144,256]{1,0:T(8,128)S(1)}, u32[]{:S(2)}, u32[]{:S(2)}) collective-permute-start(f32[144,256]{1,0:T(8,128)S(1)} %add_add_fusion), channel_id=1, source_target_pairs={{0,8},{8,0},{16,24},{24,16},{32,40},{40,32},{48,56},{56,48},{1,9},... | collective-permute-start | bytes 442376 | tf_op jit(solution)/shard_map/ppermute | solution.py:249
  (8 other events, 193.6 us)
Sparse Core Ops, SparseCore 0:
  24.9 57.9 all-gather.1
  85.5 42.3 reduce-scatter.1

commit v6 on v5

--- a/solution.py
+++ b/solution.py
@@ -242,11 +242,14 @@
         own, up, across, down = (value.astype(F32) for value in gather4(part, axis))
         part = ((own + across) + (up + down)).astype(BF16)
     half = band_terms[0].astype(F32) + swap(band_terms[1]).astype(F32)
+    part, half = lax.optimization_barrier((part, half))
     own, up, down, across = (
         value.astype(F32) for value in [part] + [shift(part, "z", NZ, by) for by in (2, -2, 4)]
     )
-    part, half = lax.optimization_barrier(((own + across) + (up + down), half))
-    paired = lax.ppermute(part, "z", [(i, i ^ 1) for i in range(NZ)])
+    part = (own + across) + (up + down)
+    other = lax.ppermute(part, "z", [(i, i ^ 1) for i in range(NZ)])
+    grad_bias = part[TILE] + other[TILE]
+    part = part[:TILE] + other[:TILE]
 
     half16 = half.astype(BF16)
     total = half[0]
@@ -259,9 +262,7 @@
         "ahn,gh->ang", own_z, weight.astype(F32), precision=lax.Precision.HIGHEST
     ).reshape(2 * TILE, H)
     grad_features = (grad_features * inv_root[:, None]).astype(BF16)
-    paired, grad_features = lax.optimization_barrier((paired, grad_features))
-    grad_bias = part[TILE] + paired[TILE]
-    part = part[:TILE] + paired[:TILE]
+    part, grad_features = lax.optimization_barrier((part, grad_features))
     grad_weight = lax.all_gather(part, "c", axis=0, tiled=True)
     return (layer_out, grad_weight, grad_bias, grad_features)
 

time: 151 us -> 146 us (0.967)
  waiting for transfers between devices: 60.3 us -> 55.4 us
  starting transfers between devices: 42.9 us -> 45.7 us
  Pallas kernels: 17 us -> 15.3 us
    ppermute x22, waiting for transfers between devices: 56.2 us -> 46.6 us  [shift(): lax.ppermute(value, axis, [(i, (i + by) % size) for i in range(size)])]
    ppermute x1, starting transfers between devices: 0.01 us -> 3.69 us  [shards(): other = lax.ppermute(part, 'z', [(i, i ^ 1) for i in range(NZ)])]
    all_gather x1, waiting for transfers between devices: 1.59 us -> 4.31 us  [shards(): feats = lax.all_gather(near, 'z', axis=0, tiled=True)]
    ppermute x1, waiting for transfers between devices: 0.01 us -> 1.9 us  [shards(): other = lax.ppermute(part, 'z', [(i, i ^ 1) for i in range(NZ)])]
  transfers between devices with their start and end apart: 28 -> 28, of which waited for: 17 -> 17; matrix products, arithmetic and copies ran while one was open for 4% -> 3% of each run, Pallas kernels for 11% -> 10%
where the time goes in v6:
time: 146 us
  waiting for transfers between devices  55.4 us (38%)
  starting transfers between devices  45.7 us (31%)
  Pallas kernels  15.3 us (10%)
  between operations  14.9 us (10%)
  other arithmetic  5.94 us (4%)
  blocking collectives  4.47 us (3%)
  local copies, waits for them, and re-layouts  2.16 us (1%)
  matrix products  1.9 us (1%)
    ppermute x22, waiting for transfers between devices, shift(): lax.ppermute(value, axis, [(i, (i + by) % size) for i in range(size)])  46.6 us
    ppermute x22, starting transfers between devices, shift(): lax.ppermute(value, axis, [(i, (i + by) % size) for i in range(size)])  36.3 us
    pallas_call x1, Pallas kernels, forward_tiles(): pl.pallas_call(forward_kernel, grid_spec=pltpu.PrefetchScalarGridSpec(num...  8.09 us
    pallas_call x1, Pallas kernels, backward_tiles(): pl.pallas_call(backward_kernel, grid_spec=pltpu.PrefetchScalarGridSpec(nu...  7.19 us
    ppermute x3, starting transfers between devices, swap(): return lax.ppermute(value, 'c', [(0, 1), (1, 0)])  5.59 us
    all_gather x1, blocking collectives, shards(): grad_weight = lax.all_gather(part, 'c', axis=0, tiled=True)  4.47 us
    all_gather x1, waiting for transfers between devices, shards(): feats = lax.all_gather(near, 'z', axis=0, tiled=True)  4.31 us
    ppermute x1, starting transfers between devices, shards(): other = lax.ppermute(part, 'z', [(i, i ^ 1) for i in range(NZ)])  3.69 us
  transfers between devices with their start and end apart: 28, of which 17 were waited for; matrix products, arithmetic and copies ran while one was open for 3% of the time, Pallas kernels for 10%

profile of v6, /device:TPU:1, one launch (start us, length us, event | category | flops | bytes accessed | tf_op | source)
XLA Modules:
  0.0 145.7 jit_solution(10399425197388063014)
XLA Ops:
  9.2 3.6 %collective-permute-start.3 = (bf16[2,256,128]{2,1,0:T(8,128)(2,1)S(1)}, bf16[2,256,128]{2,1,0:T(8,128)(2,1)S(1)}, u32[]{:S(2)}, u32[]{:S(2)}) collective-permute-start(bf16[2,256,128]{2,1,0:T(8,128)(2,1)S(1)} %bitcast.58), channel_id=1, source_target_pairs={{0,6},{2,0},{4,2},{6,4},{1,7},{3,1},{5,3},{7,5},{8,14},{10,8},{12,... | collective-permute-start | bytes 393224 | tf_op jit(solution)/shard_map/ppermute | solution.py:162
  13.9 2.5 %collective-permute-start = (bf16[2,128,256]{2,1,0:T(8,128)(2,1)S(1)}, bf16[2,128,256]{2,1,0:T(8,128)(2,1)S(1)}, u32[]{:S(2)}, u32[]{:S(2)}) collective-permute-start(bf16[2,128,256]{2,1,0:T(8,128)(2,1)S(1)} %bitcast.62), channel_id=1, source_target_pairs={{0,192},{64,0},{128,64},{192,128},{1,193},{65,1},{129,65},{193,129... | collective-permute-start | bytes 393224 | tf_op jit(solution)/shard_map/ppermute | solution.py:162
  16.9 2.2 %collective-permute-start.2 = (bf16[2,128,256]{2,1,0:T(8,128)(2,1)S(1)}, bf16[2,128,256]{2,1,0:T(8,128)(2,1)S(1)}, u32[]{:S(2)}, u32[]{:S(2)}) collective-permute-start(bf16[2,128,256]{2,1,0:T(8,128)(2,1)S(1)} %bitcast.64), channel_id=1, source_target_pairs={{0,64},{64,128},{128,192},{192,0},{1,65},{65,129},{129,193},{193,1... | collective-permute-start | bytes 393224 | tf_op jit(solution)/shard_map/ppermute | solution.py:162
  19.0 3.4 %collective-permute-done.5 = bf16[2,256,128]{2,1,0:T(8,128)(2,1)S(1)} collective-permute-done((bf16[2,256,128]{2,1,0:T(8,128)(2,1)S(1)}, bf16[2,256,128]{2,1,0:T(8,128)(2,1)S(1)}, u32[]{:S(2)}, u32[]{:S(2)}) %collective-permute-start.5) | collective-permute-done | bytes 131104 | tf_op jit(solution)/shard_map/ppermute | solution.py:162
  25.6 2.7 %collective-permute-start.6 = (bf16[8,256,128]{2,1,0:T(8,128)(2,1)S(1)}, bf16[8,256,128]{2,1,0:T(8,128)(2,1)S(1)}, u32[]{:S(2)}, u32[]{:S(2)}) collective-permute-start(bf16[8,256,128]{2,1,0:T(8,128)(2,1)S(1)} %pad_maximum_fusion.2), channel_id=1, source_target_pairs={{0,1},{1,0},{2,3},{3,2},{4,5},{5,4},{6,7},{7,6},{8,9},{9,8},{10,11... | collective-permute-start | bytes 1572872 | tf_op jit(solution)/shard_map/ppermute | solution.py:178
  29.9 7.2 %backward_tiles.1 = (bf16[16,256,128]{2,1,0:T(8,128)(2,1)S(1)}, bf16[16,256,128]{2,1,0:T(8,128)(2,1)S(1)}, bf16[32,256,128]{2,1,0:T(8,128)(2,1)S(1)}) custom-call(s32[192]{0:T(256)S(1)} %bitcast.46, s32[192]{0:T(256)S(1)} %bitcast.50, s32[2]{0:T(128)S(1)} %pad_add_fusion.count.info, bf16[192,128,128]{2,1,0:T(8,128)(2,1)} %bitcast.51, ...), custom_call_target="tpu_custom_call" | custom-call | flops 1610612736 | bytes 12582912 | tf_op jit(solution)/shard_map/backward_tiles/pallas_call | solution.py:143
  37.2 2.7 %collective-permute-start.8 = (bf16[16,256,128]{2,1,0:T(8,128)(2,1)S(1)}, bf16[16,256,128]{2,1,0:T(8,128)(2,1)S(1)}, u32[]{:S(2)}, u32[]{:S(2)}) collective-permute-start(bf16[16,256,128]{2,1,0:T(8,128)(2,1)S(1)} %get-tuple-element.23), channel_id=1, source_target_pairs={{0,192},{64,0},{128,64},{192,128},{1,193},{65,1},{129,65},{193,129... | collective-permute-start | bytes 3145736 | tf_op jit(solution)/shard_map/ppermute | solution.py:162
  39.8 22.0 %collective-permute-done.7 = bf16[16,256,128]{2,1,0:T(8,128)(2,1)S(1)} collective-permute-done((bf16[16,256,128]{2,1,0:T(8,128)(2,1)S(1)}, bf16[16,256,128]{2,1,0:T(8,128)(2,1)S(1)}, u32[]{:S(2)}, u32[]{:S(2)}) %collective-permute-start.7) | collective-permute-done | bytes 1048608 | tf_op jit(solution)/shard_map/ppermute | solution.py:162
  62.6 2.0 %collective-permute-start.10 = (bf16[8,256,128]{2,1,0:T(8,128)(2,1)S(1)}, bf16[8,256,128]{2,1,0:T(8,128)(2,1)S(1)}, u32[]{:S(2)}, u32[]{:S(2)}) collective-permute-start(bf16[8,256,128]{2,1,0:T(8,128)(2,1)S(1)} %get-tuple-element.25), channel_id=1, source_target_pairs={{0,192},{64,0},{128,64},{192,128},{1,193},{65,1},{129,65},{193,129... | collective-permute-start | bytes 1572872 | tf_op jit(solution)/shard_map/ppermute | solution.py:162
  65.0 11.1 %collective-permute-done.10 = bf16[8,256,128]{2,1,0:T(8,128)(2,1)S(1)} collective-permute-done((bf16[8,256,128]{2,1,0:T(8,128)(2,1)S(1)}, bf16[8,256,128]{2,1,0:T(8,128)(2,1)S(1)}, u32[]{:S(2)}, u32[]{:S(2)}) %collective-permute-start.10) | collective-permute-done | bytes 524320 | tf_op jit(solution)/shard_map/ppermute | solution.py:162
  78.7 4.3 %all-gather.2.cloned.1.call-done.feats = bf16[64,128,256]{2,1,0:T(8,128)(2,1)} async-done(((bf16[8,128,256]{2,1,0:T(8,128)(2,1)}), bf16[64,128,256]{2,1,0:T(8,128)(2,1)}) %all-gather.2.cloned.1.call-update) | async-done | bytes 4194320 | tf_op jit(solution)/shard_map/all_gather | solution.py:206
  83.0 8.1 %forward_tiles.1 = (bf16[16,128,256]{2,1,0:T(8,128)(2,1)S(1)}, f32[2,144,256]{2,1,0:T(8,128)S(1)}) custom-call(s32[192]{0:T(256)S(1)} %bitcast.47, s32[192]{0:T(256)S(1)} %bitcast.49, s32[2]{0:T(128)S(1)} %pad_add_fusion.count.info, bf16[192,128,128]{2,1,0:T(8,128)(2,1)} %bitcast.52, bf16[64,128,256]{2,1,0:T(8,128)(2,1)} %all-gather.2.cloned.1.call-done.feats, ...), custom_call_target="tpu_custom_call" | custom-call | flops 1610612736 | bytes 12582912 | tf_op jit(solution)/shard_map/forward_tiles/pallas_call | solution.py:118
  91.1 1.6 %collective-permute-start.11 = (f32[144,256]{1,0:T(8,128)S(1)}, f32[144,256]{1,0:T(8,128)S(1)}, u32[]{:S(2)}, u32[]{:S(2)}) collective-permute-start(f32[144,256]{1,0:T(8,128)S(1)} %slice_bitcast_fusion), channel_id=1, source_target_pairs={{0,1},{1,0},{2,3},{3,2},{4,5},{5,4},{6,7},{7,6},{8,9},{9,8},{10,11... | collective-permute-start | bytes 442376 | tf_op jit(solution)/shard_map/ppermute | solution.py:178
  93.8 2.4 %collective-permute-start.12 = (bf16[144,256]{1,0:T(8,128)(2,1)S(1)}, bf16[144,256]{1,0:T(8,128)(2,1)S(1)}, u32[]{:S(2)}, u32[]{:S(2)}) collective-permute-start(bf16[144,256]{1,0:T(8,128)(2,1)S(1)} %fusion.7), channel_id=1, source_target_pairs={{0,4},{2,6},{4,0},{6,2},{1,5},{3,7},{5,1},{7,3},{8,12},{10,14},{12... | collective-permute-start | bytes 221192 | tf_op jit(solution)/shard_map/ppermute | solution.py:162
  101.4 3.2 %collective-permute-start.15 = (bf16[144,256]{1,0:T(8,128)(2,1)S(1)}, bf16[144,256]{1,0:T(8,128)(2,1)S(1)}, u32[]{:S(2)}, u32[]{:S(2)}) collective-permute-start(bf16[144,256]{1,0:T(8,128)(2,1)S(1)} %add_convert_fusion.3), channel_id=1, source_target_pairs={{0,128},{64,192},{128,0},{192,64},{1,129},{65,193},{129,1},{193,65... | collective-permute-start | bytes 221192 | tf_op jit(solution)/shard_map/ppermute | solution.py:162
  106.4 2.5 %collective-permute-done.16 = bf16[144,256]{1,0:T(8,128)(2,1)S(1)} collective-permute-done((bf16[144,256]{1,0:T(8,128)(2,1)S(1)}, bf16[144,256]{1,0:T(8,128)(2,1)S(1)}, u32[]{:S(2)}, u32[]{:S(2)}) %collective-permute-start.16) | collective-permute-done | bytes 73760 | tf_op jit(solution)/shard_map/ppermute | solution.py:162
  108.9 1.8 %collective-permute-done.17 = bf16[144,256]{1,0:T(8,128)(2,1)S(1)} collective-permute-done((bf16[144,256]{1,0:T(8,128)(2,1)S(1)}, bf16[144,256]{1,0:T(8,128)(2,1)S(1)}, u32[]{:S(2)}, u32[]{:S(2)}) %collective-permute-start.17) | collective-permute-done | bytes 73760 | tf_op jit(solution)/shard_map/ppermute | solution.py:162
  110.9 3.8 %collective-permute-start.22 = (bf16[144,256]{1,0:T(8,128)(2,1)S(1)}, bf16[144,256]{1,0:T(8,128)(2,1)S(1)}, u32[]{:S(2)}, u32[]{:S(2)}) collective-permute-start(bf16[144,256]{1,0:T(8,128)(2,1)S(1)} %add_convert_fusion.2), channel_id=1, source_target_pairs={{0,32},{8,40},{16,48},{24,56},{32,0},{40,8},{48,16},{56,24},{1,33}... | collective-permute-start | bytes 221192 | tf_op jit(solution)/shard_map/ppermute | solution.py:162
  114.7 2.2 %collective-permute-start.23 = (bf16[144,256]{1,0:T(8,128)(2,1)S(1)}, bf16[144,256]{1,0:T(8,128)(2,1)S(1)}, u32[]{:S(2)}, u32[]{:S(2)}) collective-permute-start(bf16[144,256]{1,0:T(8,128)(2,1)S(1)} %add_convert_fusion.2), channel_id=1, source_target_pairs={{0,16},{8,24},{16,32},{24,40},{32,48},{40,56},{48,0},{56,8},{1,17}... | collective-permute-start | bytes 221192 | tf_op jit(solution)/shard_map/ppermute | solution.py:162
  118.8 2.3 %collective-permute-start.20 = (bf16[256,256]{1,0:T(8,128)(2,1)S(1)}, bf16[256,256]{1,0:T(8,128)(2,1)S(1)}, u32[]{:S(2)}, u32[]{:S(2)}) collective-permute-start(bf16[256,256]{1,0:T(8,128)(2,1)S(1)} %get-tuple-element.42), channel_id=1, source_target_pairs={{0,6},{2,0},{4,2},{6,4},{1,7},{3,1},{5,3},{7,5},{8,14},{10,8},{12,... | collective-permute-start | bytes 393224 | tf_op jit(solution)/shard_map/ppermute | solution.py:162
  121.1 2.6 %collective-permute-start.21 = (bf16[256,256]{1,0:T(8,128)(2,1)S(1)}, bf16[256,256]{1,0:T(8,128)(2,1)S(1)}, u32[]{:S(2)}, u32[]{:S(2)}) collective-permute-start(bf16[256,256]{1,0:T(8,128)(2,1)S(1)} %get-tuple-element.41), channel_id=1, source_target_pairs={{0,4},{2,6},{4,0},{6,2},{1,5},{3,7},{5,1},{7,3},{8,12},{10,14},{12... | collective-permute-start | bytes 393224 | tf_op jit(solution)/shard_map/ppermute | solution.py:162
  124.5 3.7 %collective-permute-start.25 = (f32[144,256]{1,0:T(8,128)S(1)}, f32[144,256]{1,0:T(8,128)S(1)}, u32[]{:S(2)}, u32[]{:S(2)}) collective-permute-start(f32[144,256]{1,0:T(8,128)S(1)} %add_add_fusion), channel_id=1, source_target_pairs={{0,8},{8,0},{16,24},{24,16},{32,40},{40,32},{48,56},{56,48},{1,9},... | collective-permute-start | bytes 442376 | tf_op jit(solution)/shard_map/ppermute | solution.py:250
  129.1 1.9 %collective-permute-done.25 = f32[144,256]{1,0:T(8,128)S(1)} collective-permute-done((f32[144,256]{1,0:T(8,128)S(1)}, f32[144,256]{1,0:T(8,128)S(1)}, u32[]{:S(2)}, u32[]{:S(2)}) %collective-permute-start.25) | collective-permute-done | bytes 147488 | tf_op jit(solution)/shard_map/ppermute | solution.py:250
  133.7 4.5 %all_gather.7 = f32[256,256]{1,0:T(8,128)S(1)} all-gather(f32[128,256]{1,0:T(8,128)S(1)} %slice_add_fusion), channel_id=1, replica_groups=mesh['x'=4,'z'=8,'y'=4,'c'=2] {'c'}, dimensions={0}, use_global_device_ids=true | all-gather | bytes 393216 | tf_op jit(solution)/shard_map/all_gather | solution.py:266
  (73 shorter events, 26.5 us)
Async XLA Ops:
  7.2 75.8 %all-gather.2.cloned.1.call-start = ((), (), s32[]{:S(2)}) async-start(), calls=%async_computation.1 | async-start | bytes 4718592 | tf_op jit(solution)/shard_map/all_gather | solution.py:206
  9.2 7.7 %collective-permute-start.3 = (bf16[2,256,128]{2,1,0:T(8,128)(2,1)S(1)}, bf16[2,256,128]{2,1,0:T(8,128)(2,1)S(1)}, u32[]{:S(2)}, u32[]{:S(2)}) collective-permute-start(bf16[2,256,128]{2,1,0:T(8,128)(2,1)S(1)} %bitcast.58), channel_id=1, source_target_pairs={{0,6},{2,0},{4,2},{6,4},{1,7},{3,1},{5,3},{7,5},{8,14},{10,8},{12,... | collective-permute-start | bytes 393224 | tf_op jit(solution)/shard_map/ppermute | solution.py:162
  12.8 6.2 %collective-permute-start.4 = (bf16[2,256,128]{2,1,0:T(8,128)(2,1)S(1)}, bf16[2,256,128]{2,1,0:T(8,128)(2,1)S(1)}, u32[]{:S(2)}, u32[]{:S(2)}) collective-permute-start(bf16[2,256,128]{2,1,0:T(8,128)(2,1)S(1)} %bitcast.59), channel_id=1, source_target_pairs={{0,4},{2,6},{4,0},{6,2},{1,5},{3,7},{5,1},{7,3},{8,12},{10,14},{12... | collective-permute-start | bytes 393224 | tf_op jit(solution)/shard_map/ppermute | solution.py:162
  13.2 9.3 %collective-permute-start.5 = (bf16[2,256,128]{2,1,0:T(8,128)(2,1)S(1)}, bf16[2,256,128]{2,1,0:T(8,128)(2,1)S(1)}, u32[]{:S(2)}, u32[]{:S(2)}) collective-permute-start(bf16[2,256,128]{2,1,0:T(8,128)(2,1)S(1)} %bitcast.60), channel_id=1, source_target_pairs={{0,2},{2,4},{4,6},{6,0},{1,3},{3,5},{5,7},{7,1},{8,10},{10,12},{12... | collective-permute-start | bytes 393224 | tf_op jit(solution)/shard_map/ppermute | solution.py:162
  13.9 8.7 %collective-permute-start = (bf16[2,128,256]{2,1,0:T(8,128)(2,1)S(1)}, bf16[2,128,256]{2,1,0:T(8,128)(2,1)S(1)}, u32[]{:S(2)}, u32[]{:S(2)}) collective-permute-start(bf16[2,128,256]{2,1,0:T(8,128)(2,1)S(1)} %bitcast.62), channel_id=1, source_target_pairs={{0,192},{64,0},{128,64},{192,128},{1,193},{65,1},{129,65},{193,129... | collective-permute-start | bytes 393224 | tf_op jit(solution)/shard_map/ppermute | solution.py:162
  16.3 6.2 %collective-permute-start.1 = (bf16[2,128,256]{2,1,0:T(8,128)(2,1)S(1)}, bf16[2,128,256]{2,1,0:T(8,128)(2,1)S(1)}, u32[]{:S(2)}, u32[]{:S(2)}) collective-permute-start(bf16[2,128,256]{2,1,0:T(8,128)(2,1)S(1)} %bitcast.63), channel_id=1, source_target_pairs={{0,128},{64,192},{128,0},{192,64},{1,129},{65,193},{129,1},{193,65... | collective-permute-start | bytes 393224 | tf_op jit(solution)/shard_map/ppermute | solution.py:162
  16.9 7.1 %collective-permute-start.2 = (bf16[2,128,256]{2,1,0:T(8,128)(2,1)S(1)}, bf16[2,128,256]{2,1,0:T(8,128)(2,1)S(1)}, u32[]{:S(2)}, u32[]{:S(2)}) collective-permute-start(bf16[2,128,256]{2,1,0:T(8,128)(2,1)S(1)} %bitcast.64), channel_id=1, source_target_pairs={{0,64},{64,128},{128,192},{192,0},{1,65},{65,129},{129,193},{193,1... | collective-permute-start | bytes 393224 | tf_op jit(solution)/shard_map/ppermute | solution.py:162
  24.8 106.8 %reduce-scatter.2.cloned.1.call-start = ((), (), s32[]{:S(2)}) async-start(), calls=%async_computation.2 | async-start | bytes 2359296 | tf_op jit(solution)/shard_map/reduce_scatter | solution.py:230
  37.1 24.8 %collective-permute-start.7 = (bf16[16,256,128]{2,1,0:T(8,128)(2,1)S(1)}, bf16[16,256,128]{2,1,0:T(8,128)(2,1)S(1)}, u32[]{:S(2)}, u32[]{:S(2)}) collective-permute-start(bf16[16,256,128]{2,1,0:T(8,128)(2,1)S(1)} %get-tuple-element.22), channel_id=1, source_target_pairs={{0,64},{64,128},{128,192},{192,0},{1,65},{65,129},{129,193},{193,1... | collective-permute-start | bytes 3145736 | tf_op jit(solution)/shard_map/ppermute | solution.py:162
  37.2 25.2 %collective-permute-start.8 = (bf16[16,256,128]{2,1,0:T(8,128)(2,1)S(1)}, bf16[16,256,128]{2,1,0:T(8,128)(2,1)S(1)}, u32[]{:S(2)}, u32[]{:S(2)}) collective-permute-start(bf16[16,256,128]{2,1,0:T(8,128)(2,1)S(1)} %get-tuple-element.23), channel_id=1, source_target_pairs={{0,192},{64,0},{128,64},{192,128},{1,193},{65,1},{129,65},{193,129... | collective-permute-start | bytes 3145736 | tf_op jit(solution)/shard_map/ppermute | solution.py:162
  62.6 13.5 %collective-permute-start.10 = (bf16[8,256,128]{2,1,0:T(8,128)(2,1)S(1)}, bf16[8,256,128]{2,1,0:T(8,128)(2,1)S(1)}, u32[]{:S(2)}, u32[]{:S(2)}) collective-permute-start(bf16[8,256,128]{2,1,0:T(8,128)(2,1)S(1)} %get-tuple-element.25), channel_id=1, source_target_pairs={{0,192},{64,0},{128,64},{192,128},{1,193},{65,1},{129,65},{193,129... | collective-permute-start | bytes 1572872 | tf_op jit(solution)/shard_map/ppermute | solution.py:162
  64.6 12.1 %collective-permute-start.9 = (bf16[8,256,128]{2,1,0:T(8,128)(2,1)S(1)}, bf16[8,256,128]{2,1,0:T(8,128)(2,1)S(1)}, u32[]{:S(2)}, u32[]{:S(2)}) collective-permute-start(bf16[8,256,128]{2,1,0:T(8,128)(2,1)S(1)} %get-tuple-element.24), channel_id=1, source_target_pairs={{0,64},{64,128},{128,192},{192,0},{1,65},{65,129},{129,193},{193,1... | collective-permute-start | bytes 1572872 | tf_op jit(solution)/shard_map/ppermute | solution.py:162
  93.8 5.2 %collective-permute-start.12 = (bf16[144,256]{1,0:T(8,128)(2,1)S(1)}, bf16[144,256]{1,0:T(8,128)(2,1)S(1)}, u32[]{:S(2)}, u32[]{:S(2)}) collective-permute-start(bf16[144,256]{1,0:T(8,128)(2,1)S(1)} %fusion.7), channel_id=1, source_target_pairs={{0,4},{2,6},{4,0},{6,2},{1,5},{3,7},{5,1},{7,3},{8,12},{10,14},{12... | collective-permute-start | bytes 221192 | tf_op jit(solution)/shard_map/ppermute | solution.py:162
  96.6 4.8 %collective-permute-start.14 = (bf16[144,256]{1,0:T(8,128)(2,1)S(1)}, bf16[144,256]{1,0:T(8,128)(2,1)S(1)}, u32[]{:S(2)}, u32[]{:S(2)}) collective-permute-start(bf16[144,256]{1,0:T(8,128)(2,1)S(1)} %fusion.7), channel_id=1, source_target_pairs={{0,2},{2,4},{4,6},{6,0},{1,3},{3,5},{5,7},{7,1},{8,10},{10,12},{12... | collective-permute-start | bytes 221192 | tf_op jit(solution)/shard_map/ppermute | solution.py:162
  97.7 13.0 %collective-permute-start.18 = (bf16[4,256,256]{2,1,0:T(8,128)(2,1)S(1)}, bf16[4,256,256]{2,1,0:T(8,128)(2,1)S(1)}, u32[]{:S(2)}, u32[]{:S(2)}) collective-permute-start(bf16[4,256,256]{2,1,0:T(8,128)(2,1)S(1)} %bitcast.57), channel_id=1, source_target_pairs={{0,1},{1,0},{2,3},{3,2},{4,5},{5,4},{6,7},{7,6},{8,9},{9,8},{10,11... | collective-permute-start | bytes 1572872 | tf_op jit(solution)/shard_map/ppermute | solution.py:178
  101.4 5.0 %collective-permute-start.15 = (bf16[144,256]{1,0:T(8,128)(2,1)S(1)}, bf16[144,256]{1,0:T(8,128)(2,1)S(1)}, u32[]{:S(2)}, u32[]{:S(2)}) collective-permute-start(bf16[144,256]{1,0:T(8,128)(2,1)S(1)} %add_convert_fusion.3), channel_id=1, source_target_pairs={{0,128},{64,192},{128,0},{192,64},{1,129},{65,193},{129,1},{193,65... | collective-permute-start | bytes 221192 | tf_op jit(solution)/shard_map/ppermute | solution.py:162
  106.2 4.5 %collective-permute-start.17 = (bf16[144,256]{1,0:T(8,128)(2,1)S(1)}, bf16[144,256]{1,0:T(8,128)(2,1)S(1)}, u32[]{:S(2)}, u32[]{:S(2)}) collective-permute-start(bf16[144,256]{1,0:T(8,128)(2,1)S(1)} %add_convert_fusion.3), channel_id=1, source_target_pairs={{0,64},{64,128},{128,192},{192,0},{1,65},{65,129},{129,193},{193,1... | collective-permute-start | bytes 221192 | tf_op jit(solution)/shard_map/ppermute | solution.py:162
  110.9 10.3 %collective-permute-start.22 = (bf16[144,256]{1,0:T(8,128)(2,1)S(1)}, bf16[144,256]{1,0:T(8,128)(2,1)S(1)}, u32[]{:S(2)}, u32[]{:S(2)}) collective-permute-start(bf16[144,256]{1,0:T(8,128)(2,1)S(1)} %add_convert_fusion.2), channel_id=1, source_target_pairs={{0,32},{8,40},{16,48},{24,56},{32,0},{40,8},{48,16},{56,24},{1,33}... | collective-permute-start | bytes 221192 | tf_op jit(solution)/shard_map/ppermute | solution.py:162
  114.7 9.3 %collective-permute-start.23 = (bf16[144,256]{1,0:T(8,128)(2,1)S(1)}, bf16[144,256]{1,0:T(8,128)(2,1)S(1)}, u32[]{:S(2)}, u32[]{:S(2)}) collective-permute-start(bf16[144,256]{1,0:T(8,128)(2,1)S(1)} %add_convert_fusion.2), channel_id=1, source_target_pairs={{0,16},{8,24},{16,32},{24,40},{32,48},{40,56},{48,0},{56,8},{1,17}... | collective-permute-start | bytes 221192 | tf_op jit(solution)/shard_map/ppermute | solution.py:162
  116.9 7.6 %collective-permute-start.24 = (bf16[144,256]{1,0:T(8,128)(2,1)S(1)}, bf16[144,256]{1,0:T(8,128)(2,1)S(1)}, u32[]{:S(2)}, u32[]{:S(2)}) collective-permute-start(bf16[144,256]{1,0:T(8,128)(2,1)S(1)} %add_convert_fusion.2), channel_id=1, source_target_pairs={{0,48},{8,56},{16,0},{24,8},{32,16},{40,24},{48,32},{56,40},{1,49}... | collective-permute-start | bytes 221192 | tf_op jit(solution)/shard_map/ppermute | solution.py:162
  118.4 9.8 %collective-permute-start.19 = (bf16[256,256]{1,0:T(8,128)(2,1)S(1)}, bf16[256,256]{1,0:T(8,128)(2,1)S(1)}, u32[]{:S(2)}, u32[]{:S(2)}) collective-permute-start(bf16[256,256]{1,0:T(8,128)(2,1)S(1)} %get-tuple-element.40), channel_id=1, source_target_pairs={{0,2},{2,4},{4,6},{6,0},{1,3},{3,5},{5,7},{7,1},{8,10},{10,12},{12... | collective-permute-start | bytes 393224 | tf_op jit(solution)/shard_map/ppermute | solution.py:162
  118.8 9.4 %collective-permute-start.20 = (bf16[256,256]{1,0:T(8,128)(2,1)S(1)}, bf16[256,256]{1,0:T(8,128)(2,1)S(1)}, u32[]{:S(2)}, u32[]{:S(2)}) collective-permute-start(bf16[256,256]{1,0:T(8,128)(2,1)S(1)} %get-tuple-element.42), channel_id=1, source_target_pairs={{0,6},{2,0},{4,2},{6,4},{1,7},{3,1},{5,3},{7,5},{8,14},{10,8},{12,... | collective-permute-start | bytes 393224 | tf_op jit(solution)/shard_map/ppermute | solution.py:162
  121.1 7.0 %collective-permute-start.21 = (bf16[256,256]{1,0:T(8,128)(2,1)S(1)}, bf16[256,256]{1,0:T(8,128)(2,1)S(1)}, u32[]{:S(2)}, u32[]{:S(2)}) collective-permute-start(bf16[256,256]{1,0:T(8,128)(2,1)S(1)} %get-tuple-element.41), channel_id=1, source_target_pairs={{0,4},{2,6},{4,0},{6,2},{1,5},{3,7},{5,1},{7,3},{8,12},{10,14},{12... | collective-permute-start | bytes 393224 | tf_op jit(solution)/shard_map/ppermute | solution.py:162
  124.5 6.5 %collective-permute-start.25 = (f32[144,256]{1,0:T(8,128)S(1)}, f32[144,256]{1,0:T(8,128)S(1)}, u32[]{:S(2)}, u32[]{:S(2)}) collective-permute-start(f32[144,256]{1,0:T(8,128)S(1)} %add_add_fusion), channel_id=1, source_target_pairs={{0,8},{8,0},{16,24},{24,16},{32,40},{40,32},{48,56},{56,48},{1,9},... | collective-permute-start | bytes 442376 | tf_op jit(solution)/shard_map/ppermute | solution.py:250
  (8 other events, 195.4 us)
Sparse Core Ops, SparseCore 0:
  24.9 57.9 all-gather.1
  85.5 41.6 reduce-scatter.1
